TPU v7x, 512 devices: a whole 4x8x8 slice. The times are simulated.
512 devices in a mesh: rows: 128 (over z, y, core), grp: 4 (over x).
Axes of the slice: x: 4, y: 8, z: 8, core: 2. Of those that a mesh axis runs over, the one named last changes fastest.
Arguments:
- embeddings: float32 [65536, 768], P(('rows', 'grp')), may hold values from -100 to 100
- assignments: int32 [65536], P(('rows', 'grp')), may hold values from 0 to 16383, as said below
Outputs:
- whitened: float32 [65536, 768], P(('rows', 'grp'))
- centroid_means: float32 [16384, 768], P(('rows', 'grp'))
Inputs may be any that keep to these rules, and one draw needn't show every extreme that they name: `assignments`: owner o holds the 128 centroids o * 128 to (o + 1) * 128 - 1. The 128 rows of one device name centroids of at most 2 rows for any one owner, and exactly 2 for some owner. Some centroids are named by no row.
All inputs are finite; a program needn't handle non-finite values.
Results may differ from a plain program's by a relative error of at most 0.00007.
Values sent between devices are 32-bit elements; how exact they have to be, the bound alone decides.
No kernel may reach another device: no remote copies, remote signals or barrier semaphores. Data moves between devices by JAX's collectives and lax.ppermute only.
A program may use at most 64 MiB of HBM per device.

v0:
```python
import jax
import jax.numpy as jnp
from jax import lax
from jax.sharding import PartitionSpec as P

CENTROIDS = 16384


def cut_along(value, dim, peers):
    before, after = (value.shape[:dim], value.shape[dim + 1 :])
    return jnp.moveaxis(value.reshape(*before, peers, -1, *after), dim, 0)


def sum_at_owner(value, axis, dim):
    peers = lax.axis_size(axis)
    tiles = lax.all_to_all(cut_along(value, dim, peers), axis, 0, 0, tiled=True)
    return jnp.sum(tiles, axis=0)


def sent_together(arrays, axis, dim, along):
    columns = [a.reshape(*a.shape[:along], -1) for a in arrays]
    both = jnp.concatenate(columns, axis=along)
    out, at, finished = (sum_at_owner(both, axis, dim), 0, [])
    for a, column in zip(arrays, columns):
        share = out[..., at : at + column.shape[along]]
        finished.append(share.reshape(*share.shape[:along], *a.shape[along:]))
        at += column.shape[along]
    return tuple(finished)


def whiten_rows(factor, values):
    return lax.linalg.triangular_solve(
        factor, values, left_side=False, lower=True, transpose_a=True
    )


def body(embeddings, assignments):
    rows_here = embeddings.shape[0]
    width = embeddings.shape[1]
    owners = lax.axis_size("rows")
    groups = lax.axis_size("grp")
    total = rows_here * owners * groups
    partial_value = jnp.dot(
        embeddings.T,
        embeddings,
        precision=lax.Precision.HIGHEST,
        preferred_element_type=jnp.float32,
    )
    gram = lax.psum(partial_value, ("rows", "grp"))
    factor = jnp.linalg.cholesky(gram / total + 1e-05 * jnp.eye(width, dtype=jnp.float32))
    whitened = whiten_rows(factor, embeddings)
    per_owner = CENTROIDS // owners
    capacity = max(2, 2 * rows_here // owners)
    target = assignments // per_owner
    local = assignments % per_owner
    hits = (target[:, None] == jnp.arange(owners, dtype=jnp.int32)[None, :]).astype(jnp.int32)
    rank = jnp.sum(hits * (jnp.cumsum(hits, axis=0) - 1), axis=1)
    slot = target * capacity + rank
    outgoing = jnp.zeros((owners * capacity, width), jnp.float32).at[slot].set(whitened)
    labels = jnp.full((owners * capacity,), -1, jnp.int32).at[slot].set(local)
    incoming, tags = (
        lax.all_to_all(
            outgoing.reshape(owners, capacity, width),
            "rows",
            split_axis=0,
            concat_axis=0,
            tiled=True,
        ),
        lax.all_to_all(
            labels.reshape(owners, capacity), "rows", split_axis=0, concat_axis=0, tiled=True
        ),
    )
    member = (tags.reshape(-1)[None, :] == jnp.arange(per_owner, dtype=jnp.int32)[:, None]).astype(
        jnp.float32
    )
    list_sums = jnp.dot(
        member,
        incoming.reshape(-1, width),
        precision=lax.Precision.HIGHEST,
        preferred_element_type=jnp.float32,
    )
    list_counts = jnp.sum(member, axis=1)
    list_sums, list_counts = sent_together((list_sums, list_counts), "grp", 0, 1)
    centroid_means = list_sums / jnp.maximum(list_counts, 1.0)[:, None]
    return (whitened, centroid_means)


def solution(mesh):
    return jax.shard_map(
        body,
        mesh=mesh,
        in_specs=(P(("rows", "grp"), None), P(("rows", "grp"))),
        out_specs=(P(("rows", "grp"), None), P(("rows", "grp"), None)),
        check_vma=False,
    )
```

profile of v0, /device:TPU:1, one launch (start us, length us, event | category | flops | bytes accessed | tf_op | source)
XLA Modules:
  0.0 600.4 jit_solution(3531689166305248254)
XLA Ops:
  7.2 4.6 fusion.60
  14.1 18.4 %all-to-all-start = ((s32[128,1,2]{2,1,0:T(1,128)}), s32[128,1,2]{2,1,0:T(1,128)S(1)}, u32[]{:S(2)}, u32[]{:S(2)}) async-start(s32[128,1,2]{2,1,0:T(1,128)} %bitcast.18), calls=%async_computation | async-start | bytes 131072 | tf_op jit(solution)/shard_map/all_to_all | solution.py:69
  32.5 266.2 %all-reduce.3.cloned.1.call-done = f32[768,768]{0,1:T(8,128)} async-done(((f32[768,768]{0,1:T(8,128)}), f32[768,768]{0,1:T(8,128)}) %all-reduce.3.cloned.1.call-update) | async-done | bytes 2359312 | tf_op jit(solution)/shard_map/psum | solution.py:49
  298.7 3.3 select_add_fusion
  302.0 3.3 copy.56
  308.8 11.7 %cholesky.164 = f32[128,128]{1,0:T(8,128)S(1)} custom-call(f32[128,128]{1,0:T(8,128)S(1)} %cholesky.421), custom_call_target="Cholesky" | custom-call | tf_op jit(solution)/shard_map/jit(cholesky)/cholesky | solution.py:50
  320.6 9.8 %custom-call.46 = f32[1,128,128]{1,2,0:T(8,128)S(1)} custom-call(f32[1,128,128]{2,1,0:T(8,128)S(1)} %get-tuple-element.63), custom_call_target="InvertDiagBlocksLowerTriangular" | custom-call | tf_op jit(solution)/shard_map/jit(cholesky)/cholesky | solution.py:50
  333.4 11.7 %cholesky.187 = f32[128,128]{1,0:T(8,128)S(1)} custom-call(f32[128,128]{1,0:T(8,128)S(1)} %cholesky.425), custom_call_target="Cholesky" | custom-call | tf_op jit(solution)/shard_map/jit(cholesky)/cholesky | solution.py:50
  345.3 10.0 %custom-call.47 = f32[1,128,128]{1,2,0:T(8,128)S(1)} custom-call(f32[1,128,128]{2,1,0:T(8,128)S(1)} %get-tuple-element.61), custom_call_target="InvertDiagBlocksLowerTriangular" | custom-call | tf_op jit(solution)/shard_map/jit(cholesky)/cholesky | solution.py:50
  357.9 11.7 %cholesky.352 = f32[128,128]{1,0:T(8,128)S(1)} custom-call(f32[128,128]{1,0:T(8,128)S(1)} %cholesky.430), custom_call_target="Cholesky" | custom-call | tf_op jit(solution)/shard_map/jit(cholesky)/cholesky | solution.py:50
  369.7 9.8 %custom-call.48 = f32[1,128,128]{1,2,0:T(8,128)S(1)} custom-call(f32[1,128,128]{2,1,0:T(8,128)S(1)} %get-tuple-element.59), custom_call_target="InvertDiagBlocksLowerTriangular" | custom-call | tf_op jit(solution)/shard_map/jit(cholesky)/cholesky | solution.py:50
  382.1 12.1 %cholesky.371 = f32[128,128]{1,0:T(8,128)S(1)} custom-call(f32[128,128]{1,0:T(8,128)S(1)} %cholesky.435), custom_call_target="Cholesky" | custom-call | tf_op jit(solution)/shard_map/jit(cholesky)/cholesky | solution.py:50
  394.3 9.8 %custom-call.49 = f32[1,128,128]{1,2,0:T(8,128)S(1)} custom-call(f32[1,128,128]{2,1,0:T(8,128)S(1)} %get-tuple-element.57), custom_call_target="InvertDiagBlocksLowerTriangular" | custom-call | tf_op jit(solution)/shard_map/jit(cholesky)/cholesky | solution.py:50
  406.4 11.7 %cholesky.390 = f32[128,128]{1,0:T(8,128)S(1)} custom-call(f32[128,128]{1,0:T(8,128)S(1)} %cholesky.440), custom_call_target="Cholesky" | custom-call | tf_op jit(solution)/shard_map/jit(cholesky)/cholesky | solution.py:50
  418.2 9.8 %custom-call.50 = f32[1,128,128]{1,2,0:T(8,128)S(1)} custom-call(f32[1,128,128]{2,1,0:T(8,128)S(1)} %get-tuple-element.55), custom_call_target="InvertDiagBlocksLowerTriangular" | custom-call | tf_op jit(solution)/shard_map/jit(cholesky)/cholesky | solution.py:50
  430.1 11.7 %cholesky.408 = f32[128,128]{1,0:T(8,128)S(1)} custom-call(f32[128,128]{1,0:T(8,128)S(1)} %convolution_subtract_fusion.7), custom_call_target="Cholesky" | custom-call | tf_op jit(solution)/shard_map/jit(cholesky)/cholesky | solution.py:50
  450.6 21.1 %while.1 = (s32[]{:T(128)}, f32[768,768]{0,1:T(8,128)}, s32[6,2]{0,1:T(2,128)S(1)}, f32[6,128,128]{2,1,0:T(8,128)}, s32[]{:T(128)}) while((s32[]{:T(128)}, f32[768,768]{0,1:T(8,128)}, s32[6,2]{0,1:T(2,128)S(1)}, f32[6,128,128]{2,1,0:T(8,128)}, s32[]{:T(128)}) %tuple.47), condition=%wide.while_cond, body=%wide.while_body.sunk | while | flops 2 | bytes 393329 | solution.py:32
  451.2 2.2 dynamic-slice.7
  454.7 2.2 dynamic-slice.7
  458.3 2.2 dynamic-slice.7
  471.7 59.8 %custom-call.51 = f32[6,128,128]{1,2,0:T(8,128)S(1)} custom-call(f32[6,128,128]{2,1,0:T(8,128)} %get-tuple-element.9), custom_call_target="InvertDiagBlocksLowerTriangular" | custom-call | tf_op jit(solution)/shard_map/triangular_solve | solution.py:32
  543.1 10.6 %all-to-all-start.1 = ((f32[128,2,768]{2,1,0:T(2,128)}), f32[128,2,768]{2,1,0:T(2,128)S(1)}, u32[]{:S(2)}, u32[]{:S(2)}) async-start(f32[128,2,768]{2,1,0:T(2,128)} %reshape.92), calls=%async_computation.1 | async-start | bytes 1572864 | tf_op jit(solution)/shard_map/all_to_all | solution.py:62
  555.5 24.1 %all-to-all-done.1 = f32[128,2,768]{2,1,0:T(2,128)S(1)} async-done(((f32[128,2,768]{2,1,0:T(2,128)}), f32[128,2,768]{2,1,0:T(2,128)S(1)}, u32[]{:S(2)}, u32[]{:S(2)}) %all-to-all-start.1) | async-done | bytes 786464 | tf_op jit(solution)/shard_map/all_to_all | solution.py:62
  580.7 11.7 %all_to_all.19 = f32[4,32,769]{2,1,0:T(8,128)S(1)} all-to-all(f32[4,32,769]{2,1,0:T(8,128)S(1)} %pad_maximum_fusion), channel_id=1, replica_groups=mesh['rows'=128,'grp'=4] {'grp'}, dimensions={0} | all-to-all | bytes 787456 | tf_op jit(solution)/shard_map/all_to_all | solution.py:16
  (118 shorter events, 53.2 us)
Async XLA Ops:
  7.2 4.7 copy-start.4
  7.2 291.6 %all-reduce.3.cloned.1.call-start = ((), (), s32[]{:S(2)}) async-start(), calls=%async_computation.3 | async-start | bytes 4718592 | tf_op jit(solution)/shard_map/psum | solution.py:49
  14.1 529.0 %all-to-all-start = ((s32[128,1,2]{2,1,0:T(1,128)}), s32[128,1,2]{2,1,0:T(1,128)S(1)}, u32[]{:S(2)}, u32[]{:S(2)}) async-start(s32[128,1,2]{2,1,0:T(1,128)} %bitcast.18), calls=%async_computation | async-start | bytes 131072 | tf_op jit(solution)/shard_map/all_to_all | solution.py:69
  302.0 3.3 copy-start
  307.4 1.4 copy-start.1
  449.0 82.4 %copy-start.2 = (f32[128,768]{1,0:T(8,128)S(1)}, f32[128,768]{1,0:T(8,128)}, u32[]{:S(2)}) copy-start(f32[128,768]{1,0:T(8,128)} %param.2) | copy-start | bytes 1179652
  540.5 39.7 %copy-start.3 = (f32[128,768]{1,0:T(8,128)}, f32[128,768]{1,0:T(8,128)S(1)}, u32[]{:S(2)}) copy-start(f32[128,768]{1,0:T(8,128)S(1)} %copy.72) | copy-start | bytes 1179652
  543.1 36.6 %all-to-all-start.1 = ((f32[128,2,768]{2,1,0:T(2,128)}), f32[128,2,768]{2,1,0:T(2,128)S(1)}, u32[]{:S(2)}, u32[]{:S(2)}) async-start(f32[128,2,768]{2,1,0:T(2,128)} %reshape.92), calls=%async_computation.1 | async-start | bytes 1572864 | tf_op jit(solution)/shard_map/all_to_all | solution.py:62
Sparse Core Ops, SparseCore 0:
  12.9 285.7 all-reduce.2
where the time goes:
time: 606 us; the launch traced here: 600 us
  waiting for transfers between devices  290 us (48%)
  other arithmetic  192 us (32%)
  local copies, waits for them, and re-layouts  32.6 us (5%)
  starting transfers between devices  29.1 us (5%)
  matrix products  25.6 us (4%)
  between operations  18.5 us (3%)
  blocking collectives  11.7 us (2%)
    psum x1, waiting for transfers between devices, body(): gram = lax.psum(partial_value, ('rows', 'grp'))  266 us
    another operation x22, other arithmetic, body(): jnp.linalg.cholesky(gram / total + 1e-05 * jnp.eye(width, dtype=jnp.float...  123 us
    another operation x3, other arithmetic, whiten_rows(): lax.linalg.triangular_solve(factor, values, left_side=False, lower=True,...  61.3 us
    all_to_all x1, waiting for transfers between devices, body(): lax.all_to_all(outgoing.reshape(owners, capacity, width), 'rows', split_a...  24.1 us
    another operation x30, local copies, waits for them, and re-layouts  21 us
    all_to_all x1, starting transfers between devices, body(): lax.all_to_all(labels.reshape(owners, capacity), 'rows', split_axis=0, co...  18.4 us
  transfers between devices with their start and end apart: 3, of which 2 were waited for; matrix products, arithmetic and copies ran while one was open for 40% of the time, Pallas kernels for 0%

commit v1 on v0

v1 whole, which is shorter than its diff:
```python
import jax
import jax.numpy as jnp
from jax import lax
from jax.sharding import Mesh, PartitionSpec as P

CENTROIDS = 16384
CAP = 2
B = 128


def spread(value, axis):
    peers = lax.axis_size(axis)
    copies = jnp.broadcast_to(value[None], (peers, *value.shape))
    return lax.all_to_all(copies, axis, 0, 0, tiled=True)


def reduced(pieces, axis):
    return jnp.sum(lax.all_to_all(pieces, axis, 0, 0, tiled=True), axis=0)


def gram_sum(part):
    mine = reduced(part.reshape(8, 336, B), ("core", "x"))
    mine = reduced(mine.reshape(8, 42, B), "y")
    mine = jnp.sum(spread(mine, "z"), axis=0)
    mine = spread(mine, "y").reshape(336, B)
    return spread(mine, ("core", "x")).reshape(2688, B)


def body(embeddings, assignments):
    rows_here, width = embeddings.shape
    rows_axes = ("z", "y", "core")
    owners = lax.axis_size(rows_axes)
    total = rows_here * owners * lax.axis_size("x")
    per_owner = CENTROIDS // owners
    n = width // B
    part = jnp.dot(
        embeddings.T, embeddings, precision=lax.Precision.HIGHEST, preferred_element_type=jnp.float32
    )
    lower = [(i, j) for j in range(n) for i in range(j, n)]
    part = jnp.concatenate([part[i * B : i * B + B, j * B : j * B + B] for i, j in lower], axis=0)

    target = assignments // per_owner
    local = assignments % per_owner
    same = target[:, None] == target[None, :]
    before = jnp.arange(rows_here)[:, None] > jnp.arange(rows_here)[None, :]
    rank = jnp.sum((same & before).astype(jnp.int32), axis=1)
    slot = target * CAP + rank
    chosen = slot[None, :] == jnp.arange(owners * CAP, dtype=jnp.int32)[:, None]
    outgoing = jnp.dot(
        chosen.astype(jnp.float32), embeddings, precision=lax.Precision.HIGHEST, preferred_element_type=jnp.float32
    )
    labels = jnp.sum(jnp.where(chosen, (local + 1)[None, :], 0), axis=1) - 1
    outgoing = outgoing.reshape(owners, CAP * width)
    labels = jnp.pad(labels.reshape(owners, CAP).astype(jnp.float32), ((0, 0), (0, B - CAP)))
    packed = jnp.concatenate([outgoing, labels], axis=1).reshape(owners, CAP * n + 1, B)
    packed = lax.all_to_all(packed, rows_axes, 0, 0, tiled=True).reshape(owners, CAP * width + B)
    incoming = packed[:, : CAP * width].reshape(owners * CAP, width)
    tags = packed[:, CAP * width : CAP * width + CAP].reshape(-1).astype(jnp.int32)
    member = (tags[None, :] == jnp.arange(per_owner, dtype=jnp.int32)[:, None]).astype(jnp.float32)
    sums = jnp.dot(member, incoming, precision=lax.Precision.HIGHEST, preferred_element_type=jnp.float32)
    counts = jnp.sum(member, axis=1)
    groups = lax.axis_size("x")
    keep = per_owner // groups
    sums = sums.reshape(groups, keep * n, B)
    counts = jnp.pad(counts.reshape(groups, 1, keep), ((0, 0), (0, 7), (0, B - keep)))
    mine = reduced(jnp.concatenate([sums, counts], axis=1), "x")
    sums = mine[: keep * n].reshape(keep, width)
    counts = mine[keep * n, :keep]

    whole = gram_sum(part)
    at = {ij: whole[k * B : k * B + B] for k, ij in enumerate(lower)}
    grid = [[at[i, j] if i >= j else at[j, i].T for j in range(n)] for i in range(n)]
    gram = jnp.block(grid) / total + 1e-05 * jnp.eye(width, dtype=jnp.float32)
    factor = lax.linalg.cholesky(gram, symmetrize_input=False)
    means = sums / jnp.maximum(counts, 1.0)[:, None]
    solved = lax.linalg.triangular_solve(
        factor, jnp.concatenate([embeddings, means], axis=0), left_side=False, lower=True, transpose_a=True
    )
    return solved[:rows_here], solved[rows_here:]


def solution(mesh):
    fine = Mesh(mesh.devices.reshape(8, 8, 2, 4), ("z", "y", "core", "x"))
    spec = ("z", "y", "core", "x")
    return jax.shard_map(
        body,
        mesh=fine,
        in_specs=(P(spec, None), P(spec)),
        out_specs=(P(spec, None), P(spec, None)),
        check_vma=False,
    )
```

time: 606 us -> 421 us (0.69)
  waiting for transfers between devices: 290 us -> 98.5 us
  local copies, waits for them, and re-layouts: 32.6 us -> 55.6 us
  starting transfers between devices: 29.1 us -> 43 us
  between operations: 18.5 us -> 5.36 us
  blocking collectives: 11.7 us -> 0 us
    psum x1 -> x0, waiting for transfers between devices: 266 us -> none  [body(): gram = lax.psum(partial_value, ('rows', 'grp'))]
    all_to_all x2 -> x7, waiting for transfers between devices: 24.1 us -> 98.5 us  [the longest x3 35.9 us: spread(): return lax.all_to_all(copies, axis, 0, 0, tiled=True)]
    unnamed x11 -> x51, local copies, waits for them, and re-layouts: 1.59 us -> 21 us
    all_to_all x2 -> x7, starting transfers between devices: 29.1 us -> 43 us  [the longest x3 17.2 us: reduced(): return jnp.sum(lax.all_to_all(pieces, axis, 0, 0, tiled=True), axis=0)]
    all_to_all x1 -> x0, blocking collectives: 11.7 us -> none  [sum_at_owner(): tiles = lax.all_to_all(cut_along(value, dim, peers), axis, 0, 0, tiled=True)]
    another operation x50 -> x25, local copies, waits for them, and re-layouts: 21.9 us -> 21.7 us
  transfers between devices with their start and end apart: 3 -> 7, of which waited for: 2 -> 7; matrix products, arithmetic and copies ran while one was open for 40% -> 1% of each run, Pallas kernels for 0% -> 0%
where the time goes in v1:
time: 421 us; the launch traced here: 413 us
  other arithmetic  189 us (45%)
  waiting for transfers between devices  98.5 us (23%)
  local copies, waits for them, and re-layouts  55.6 us (13%)
  starting transfers between devices  43 us (10%)
  matrix products  21.7 us (5%)
  between operations  5.36 us (1%)
    another operation x23, other arithmetic, body(): factor = lax.linalg.cholesky(gram, symmetrize_input=False)  124 us
    another operation x3, other arithmetic, body(): lax.linalg.triangular_solve(factor, jnp.concatenate([embeddings, means],...  61.4 us
    all_to_all x3, waiting for transfers between devices, spread(): return lax.all_to_all(copies, axis, 0, 0, tiled=True)  35.9 us
    all_to_all x3, waiting for transfers between devices, reduced(): return jnp.sum(lax.all_to_all(pieces, axis, 0, 0, tiled=True), axis=0)  31.7 us
    all_to_all x1, waiting for transfers between devices, body(): lax.all_to_all(packed, rows_axes, 0, 0, tiled=True)  30.9 us
    another operation x18, local copies, waits for them, and re-layouts  21.5 us
    unnamed x51, local copies, waits for them, and re-layouts  21 us
    all_to_all x3, starting transfers between devices, reduced(): return jnp.sum(lax.all_to_all(pieces, axis, 0, 0, tiled=True), axis=0)  17.2 us
  transfers between devices with their start and end apart: 7, of which 7 were waited for; matrix products, arithmetic and copies ran while one was open for 1% of the time, Pallas kernels for 0%

profile of v1, /device:TPU:1, one launch (start us, length us, event | category | flops | bytes accessed | tf_op | source)
XLA Modules:
  0.0 413.2 jit_solution(13413140351686486532)
XLA Ops:
  8.0 10.4 %all-to-all-start.2 = ((f32[8,336,128]{2,1,0:T(8,128)}), f32[8,336,128]{2,1,0:T(8,128)S(1)}, u32[]{:S(2)}, u32[]{:S(2)}) async-start(f32[8,336,128]{2,1,0:T(8,128)} %bitcast.3), calls=%async_computation.2 | async-start | bytes 2752512 | tf_op jit(solution)/shard_map/all_to_all | solution.py:18
  19.2 17.7 %all-to-all-done.2 = f32[8,336,128]{2,1,0:T(8,128)S(1)} async-done(((f32[8,336,128]{2,1,0:T(8,128)}), f32[8,336,128]{2,1,0:T(8,128)S(1)}, u32[]{:S(2)}, u32[]{:S(2)}) %all-to-all-start.2) | async-done | bytes 1376288 | tf_op jit(solution)/shard_map/all_to_all | solution.py:18
  43.2 7.8 %all-to-all-done.3 = f32[8,42,128]{2,1,0:T(8,128)S(1)} async-done(((f32[8,42,128]{2,1,0:T(8,128)}), f32[8,42,128]{2,1,0:T(8,128)S(1)}, u32[]{:S(2)}, u32[]{:S(2)}) %all-to-all-start.3) | async-done | bytes 172064 | tf_op jit(solution)/shard_map/all_to_all | solution.py:18
  51.0 11.9 %all-to-all-start = ((f32[128,13,128]{2,1,0:T(8,128)}), f32[128,13,128]{2,1,0:T(8,128)S(1)}, u32[]{:S(2)}, u32[]{:S(2)}) async-start(f32[128,13,128]{2,1,0:T(8,128)} %copy.120), calls=%async_computation | async-start | bytes 2097152 | tf_op jit(solution)/shard_map/all_to_all | solution.py:56
  63.0 30.9 %all-to-all-done = f32[128,13,128]{2,1,0:T(8,128)S(1)} async-done(((f32[128,13,128]{2,1,0:T(8,128)}), f32[128,13,128]{2,1,0:T(8,128)S(1)}, u32[]{:S(2)}, u32[]{:S(2)}) %all-to-all-start) | async-done | bytes 852000 | tf_op jit(solution)/shard_map/all_to_all | solution.py:56
  99.1 9.8 %all-to-all-done.4 = f32[8,42,128]{2,1,0:T(8,128)S(1)} async-done(((f32[8,42,128]{2,1,0:T(8,128)}), f32[8,42,128]{2,1,0:T(8,128)S(1)}, u32[]{:S(2)}, u32[]{:S(2)}) %all-to-all-start.4) | async-done | bytes 172064 | tf_op jit(solution)/shard_map/all_to_all | solution.py:14
  109.5 3.6 all-to-all-start.5
  114.6 7.9 %all-to-all-done.5 = f32[8,42,128]{2,1,0:T(8,128)S(1)} async-done(((f32[8,42,128]{2,1,0:T(8,128)}), f32[8,42,128]{2,1,0:T(8,128)S(1)}, u32[]{:S(2)}, u32[]{:S(2)}) %all-to-all-start.5) | async-done | bytes 172064 | tf_op jit(solution)/shard_map/all_to_all | solution.py:14
  126.1 6.3 %all-to-all-done.1 = f32[4,200,128]{2,1,0:T(8,128)S(1)} async-done(((f32[4,200,128]{2,1,0:T(8,128)}), f32[4,200,128]{2,1,0:T(8,128)S(1)}, u32[]{:S(2)}, u32[]{:S(2)}) %all-to-all-start.1) | async-done | bytes 409632 | tf_op jit(solution)/shard_map/all_to_all | solution.py:18
  133.5 6.8 %all-to-all-start.6 = ((f32[8,336,128]{2,1,0:T(8,128)}), f32[8,336,128]{2,1,0:T(8,128)S(1)}, u32[]{:S(2)}, u32[]{:S(2)}) async-start(f32[8,336,128]{2,1,0:T(8,128)} %broadcast_in_dim.25), calls=%async_computation.6 | async-start | bytes 2752512 | tf_op jit(solution)/shard_map/all_to_all | solution.py:14
  140.5 18.2 %all-to-all-done.6 = f32[8,336,128]{2,1,0:T(8,128)S(1)} async-done(((f32[8,336,128]{2,1,0:T(8,128)}), f32[8,336,128]{2,1,0:T(8,128)S(1)}, u32[]{:S(2)}, u32[]{:S(2)}) %all-to-all-start.6) | async-done | bytes 1376288 | tf_op jit(solution)/shard_map/all_to_all | solution.py:14
  182.5 11.7 %cholesky.164 = f32[128,128]{1,0:T(8,128)S(1)} custom-call(f32[128,128]{1,0:T(8,128)S(1)} %cholesky.421), custom_call_target="Cholesky" | custom-call | tf_op jit(solution)/shard_map/cholesky | solution.py:74
  194.4 9.8 %custom-call.35 = f32[1,128,128]{1,2,0:T(8,128)S(1)} custom-call(f32[1,128,128]{2,1,0:T(8,128)S(1)} %get-tuple-element.64), custom_call_target="InvertDiagBlocksLowerTriangular" | custom-call | tf_op jit(solution)/shard_map/cholesky | solution.py:74
  207.0 11.9 %cholesky.187 = f32[128,128]{1,0:T(8,128)S(1)} custom-call(f32[128,128]{1,0:T(8,128)S(1)} %cholesky.425), custom_call_target="Cholesky" | custom-call | tf_op jit(solution)/shard_map/cholesky | solution.py:74
  220.3 9.8 %custom-call.36 = f32[1,128,128]{1,2,0:T(8,128)S(1)} custom-call(f32[1,128,128]{2,1,0:T(8,128)S(1)} %get-tuple-element.61), custom_call_target="InvertDiagBlocksLowerTriangular" | custom-call | tf_op jit(solution)/shard_map/cholesky | solution.py:74
  232.0 11.7 %cholesky.352 = f32[128,128]{1,0:T(8,128)S(1)} custom-call(f32[128,128]{1,0:T(8,128)S(1)} %cholesky.430), custom_call_target="Cholesky" | custom-call | tf_op jit(solution)/shard_map/cholesky | solution.py:74
  244.4 9.8 %custom-call.37 = f32[1,128,128]{1,2,0:T(8,128)S(1)} custom-call(f32[1,128,128]{2,1,0:T(8,128)S(1)} %get-tuple-element.58), custom_call_target="InvertDiagBlocksLowerTriangular" | custom-call | tf_op jit(solution)/shard_map/cholesky | solution.py:74
  256.1 12.1 %cholesky.371 = f32[128,128]{1,0:T(8,128)S(1)} custom-call(f32[128,128]{1,0:T(8,128)S(1)} %cholesky.435), custom_call_target="Cholesky" | custom-call | tf_op jit(solution)/shard_map/cholesky | solution.py:74
  269.0 9.8 %custom-call.38 = f32[1,128,128]{1,2,0:T(8,128)S(1)} custom-call(f32[1,128,128]{2,1,0:T(8,128)S(1)} %get-tuple-element.55), custom_call_target="InvertDiagBlocksLowerTriangular" | custom-call | tf_op jit(solution)/shard_map/cholesky | solution.py:74
  280.6 11.7 %cholesky.390 = f32[128,128]{1,0:T(8,128)S(1)} custom-call(f32[128,128]{1,0:T(8,128)S(1)} %cholesky.440), custom_call_target="Cholesky" | custom-call | tf_op jit(solution)/shard_map/cholesky | solution.py:74
  293.0 9.8 %custom-call.39 = f32[1,128,128]{1,2,0:T(8,128)S(1)} custom-call(f32[1,128,128]{2,1,0:T(8,128)S(1)} %get-tuple-element.52), custom_call_target="InvertDiagBlocksLowerTriangular" | custom-call | tf_op jit(solution)/shard_map/cholesky | solution.py:74
  304.3 11.9 %cholesky.408 = f32[128,128]{1,0:T(8,128)S(1)} custom-call(f32[128,128]{1,0:T(8,128)S(1)} %convolution_subtract_fusion.9), custom_call_target="Cholesky" | custom-call | tf_op jit(solution)/shard_map/cholesky | solution.py:74
  322.4 21.5 %while.1 = (s32[]{:T(128)}, f32[768,768]{1,0:T(8,128)}, s32[6,2]{0,1:T(2,128)S(1)}, f32[6,128,128]{2,1,0:T(8,128)}, s32[]{:T(128)}) while((s32[]{:T(128)}, f32[768,768]{1,0:T(8,128)}, s32[6,2]{0,1:T(2,128)S(1)}, f32[6,128,128]{2,1,0:T(8,128)}, s32[]{:T(128)}) %tuple.60), condition=%wide.while_cond, body=%wide.while_body.sunk | while | flops 2 | bytes 132705 | solution.py:76
  343.9 59.8 %custom-call.40 = f32[6,128,128]{1,2,0:T(8,128)S(1)} custom-call(f32[6,128,128]{2,1,0:T(8,128)} %get-tuple-element.9), custom_call_target="InvertDiagBlocksLowerTriangular" | custom-call | tf_op jit(solution)/shard_map/triangular_solve | solution.py:76
  (167 shorter events, 96.8 us)
Async XLA Ops:
  4.6 13.8 %copy-start.2 = (s32[128]{0:T(128)S(1)}, s32[128]{0:T(128)}, u32[]{:S(2)}) copy-start(s32[128]{0:T(128)} %param.3) | copy-start | bytes 1540
  4.6 14.1 %copy-start = (f32[128,768]{1,0:T(8,128)S(1)}, f32[128,768]{1,0:T(8,128)}, u32[]{:S(2)}) copy-start(f32[128,768]{1,0:T(8,128)} %param.2) | copy-start | bytes 1179652
  8.0 28.9 %all-to-all-start.2 = ((f32[8,336,128]{2,1,0:T(8,128)}), f32[8,336,128]{2,1,0:T(8,128)S(1)}, u32[]{:S(2)}, u32[]{:S(2)}) async-start(f32[8,336,128]{2,1,0:T(8,128)} %bitcast.3), calls=%async_computation.2 | async-start | bytes 2752512 | tf_op jit(solution)/shard_map/all_to_all | solution.py:18
  37.6 13.4 %all-to-all-start.3 = ((f32[8,42,128]{2,1,0:T(8,128)}), f32[8,42,128]{2,1,0:T(8,128)S(1)}, u32[]{:S(2)}, u32[]{:S(2)}) async-start(f32[8,42,128]{2,1,0:T(8,128)} %reshape.113), calls=%async_computation.3 | async-start | bytes 393216 | tf_op jit(solution)/shard_map/all_to_all | solution.py:18
  51.0 42.8 %all-to-all-start = ((f32[128,13,128]{2,1,0:T(8,128)}), f32[128,13,128]{2,1,0:T(8,128)S(1)}, u32[]{:S(2)}, u32[]{:S(2)}) async-start(f32[128,13,128]{2,1,0:T(8,128)} %copy.120), calls=%async_computation | async-start | bytes 2097152 | tf_op jit(solution)/shard_map/all_to_all | solution.py:56
  94.6 14.3 %all-to-all-start.4 = ((f32[8,42,128]{2,1,0:T(8,128)}), f32[8,42,128]{2,1,0:T(8,128)S(1)}, u32[]{:S(2)}, u32[]{:S(2)}) async-start(f32[8,42,128]{2,1,0:T(8,128)} %broadcast_in_dim.22), calls=%async_computation.4 | async-start | bytes 393216 | tf_op jit(solution)/shard_map/all_to_all | solution.py:14
  109.5 13.0 %all-to-all-start.5 = ((f32[8,42,128]{2,1,0:T(8,128)}), f32[8,42,128]{2,1,0:T(8,128)S(1)}, u32[]{:S(2)}, u32[]{:S(2)}) async-start(f32[8,42,128]{2,1,0:T(8,128)} %broadcast_in_dim.23), calls=%async_computation.5 | async-start | bytes 393216 | tf_op jit(solution)/shard_map/all_to_all | solution.py:14
  122.6 9.8 %all-to-all-start.1 = ((f32[4,200,128]{2,1,0:T(8,128)}), f32[4,200,128]{2,1,0:T(8,128)S(1)}, u32[]{:S(2)}, u32[]{:S(2)}) async-start(f32[4,200,128]{2,1,0:T(8,128)} %select_maximum_fusion.1), calls=%async_computation.1 | async-start | bytes 819200 | tf_op jit(solution)/shard_map/all_to_all | solution.py:18
  133.5 25.2 %all-to-all-start.6 = ((f32[8,336,128]{2,1,0:T(8,128)}), f32[8,336,128]{2,1,0:T(8,128)S(1)}, u32[]{:S(2)}, u32[]{:S(2)}) async-start(f32[8,336,128]{2,1,0:T(8,128)} %broadcast_in_dim.25), calls=%async_computation.6 | async-start | bytes 2752512 | tf_op jit(solution)/shard_map/all_to_all | solution.py:14
  181.1 1.4 copy-start.1

commit v2 on v1

--- a/solution.py
+++ b/solution.py
@@ -1,11 +1,111 @@
+import functools
+
 import jax
 import jax.numpy as jnp
 from jax import lax
+from jax.experimental import pallas as pl
+from jax.experimental.pallas import tpu as pltpu
 from jax.sharding import Mesh, PartitionSpec as P
 
 CENTROIDS = 16384
 CAP = 2
 B = 128
+
+HI = lax.Precision.HIGHEST
+NT = (((1,), (1,)), ((), ()))
+
+
+def mul_t(a, b):
+    return lax.dot_general(a, b, NT, precision=HI, preferred_element_type=jnp.float32)
+
+
+def inverse_factor(block):
+    groups = B // 8
+    tiles = [block[8 * i : 8 * i + 8] for i in range(groups)]
+    lane = lax.broadcasted_iota(jnp.int32, (8, B), 1)
+    sub = lax.broadcasted_iota(jnp.int32, (8, B), 0)
+    for g in range(groups):
+        done = (lane >= 8 * g) & (lane < 8 * g + 8)
+        cols = [[jnp.broadcast_to(t[:, 8 * g + k : 8 * g + k + 1], (8, B)) for k in range(8)] for t in tiles[g:]]
+        here = jnp.where(lane == sub + 8 * g, 1.0, jnp.where(done, 0.0, tiles[g]))
+        rows = [here[k : k + 1] for k in range(8)]
+        small = [[cols[0][p][k : k + 1] for p in range(8)] for k in range(8)]
+        scaled = []
+        for p in range(8):
+            r = 1.0 / small[p][p]
+            for k in range(p + 1, 8):
+                m = small[k][p] * r
+                for q in range(k, 8):
+                    small[q][k] = small[q][k] - m * small[q][p]
+                rows[k] = rows[k] - m * rows[p]
+                for c in cols[1:]:
+                    c[k] = c[k] - m * c[p]
+            scaled.append(rows[p] * r)
+        for i in range(g + 1, groups):
+            new = jnp.where(done, 0.0, tiles[i])
+            for p in range(8):
+                new = new - cols[i - g][p] * scaled[p]
+            tiles[i] = new
+        tiles[g] = jnp.concatenate([rows[k] * lax.rsqrt(small[k][k]) for k in range(8)], axis=0)
+    row = lax.broadcasted_iota(jnp.int32, (B, B), 0)
+    col = lax.broadcasted_iota(jnp.int32, (B, B), 1)
+    return jnp.where(col <= row, jnp.concatenate(tiles, axis=0), 0.0)
+
+
+def first(j, n):
+    return (j * n - j * (j - 1) // 2) * B
+
+
+def whiten_kernel(total, n, gram_ref, x_ref, out_ref, a_ref, x_blocks, inv_ref):
+    row = lax.broadcasted_iota(jnp.int32, (B, B), 0)
+    col = lax.broadcasted_iota(jnp.int32, (B, B), 1)
+    a_ref[...] = gram_ref[...] * (1.0 / total)
+    for j in range(n):
+        at = first(j, n)
+        a_ref[at : at + B] += jnp.where(row == col, 1e-05, 0.0)
+        x_blocks[j] = x_ref[:, j * B : j * B + B]
+
+    def step(k, carry):
+        inv_ref[...] = inverse_factor(a_ref[pl.ds(pl.multiple_of(first(k, n), B), B)])
+        for now in range(n):
+
+            @pl.when(k == now)
+            def _():
+                inv = inv_ref[...]
+                at = first(now, n) + B
+                below = (n - now - 1) * B
+                solved = mul_t(x_blocks[now], inv)
+                out_ref[:, now * B : now * B + B] = solved
+                if below:
+                    panel = mul_t(a_ref[at : at + below], inv)
+                    for j in range(now + 1, n):
+                        top = (j - now - 1) * B
+                        to = first(j, n)
+                        part = panel[top : top + B]
+                        a_ref[to : to + (n - j) * B] -= mul_t(panel[top:], part)
+                        x_blocks[j] -= mul_t(solved, part)
+
+        return carry
+
+    lax.fori_loop(0, n, step, 0)
+
+
+def whiten(gram, x, total):
+    n = x.shape[1] // B
+    return pl.pallas_call(
+        functools.partial(whiten_kernel, total, n),
+        out_shape=jax.ShapeDtypeStruct(x.shape, jnp.float32),
+        in_specs=[pl.BlockSpec(memory_space=pltpu.VMEM)] * 2,
+        out_specs=pl.BlockSpec(memory_space=pltpu.VMEM),
+        scratch_shapes=[
+            pltpu.VMEM(gram.shape, jnp.float32),
+            pltpu.VMEM((n, x.shape[0], B), jnp.float32),
+            pltpu.VMEM((B, B), jnp.float32),
+        ],
+        compiler_params=pltpu.CompilerParams(vmem_limit_bytes=32 << 20),
+        cost_estimate=pl.CostEstimate(flops=20_000_000_000, bytes_accessed=4_000_000, transcendentals=0),
+        name="whiten",
+    )(gram, x)
 
 
 def spread(value, axis):
@@ -68,14 +168,8 @@
     counts = mine[keep * n, :keep]
 
     whole = gram_sum(part)
-    at = {ij: whole[k * B : k * B + B] for k, ij in enumerate(lower)}
-    grid = [[at[i, j] if i >= j else at[j, i].T for j in range(n)] for i in range(n)]
-    gram = jnp.block(grid) / total + 1e-05 * jnp.eye(width, dtype=jnp.float32)
-    factor = lax.linalg.cholesky(gram, symmetrize_input=False)
     means = sums / jnp.maximum(counts, 1.0)[:, None]
-    solved = lax.linalg.triangular_solve(
-        factor, jnp.concatenate([embeddings, means], axis=0), left_side=False, lower=True, transpose_a=True
-    )
+    solved = whiten(whole, jnp.concatenate([embeddings, means], axis=0), total)
     return solved[:rows_here], solved[rows_here:]
 
 

time: 421 us -> 191 us (0.45); the launches traced: 413 us -> 190 us
  other arithmetic: 189 us -> 1.5 us
  local copies, waits for them, and re-layouts: 55.6 us -> 12.2 us
  Pallas kernels: 0 us -> 29.9 us
  matrix products: 21.7 us -> 4.07 us
  between operations: 5.36 us -> 0.88 us
    another operation x26 -> x0, other arithmetic: 186 us -> none  [the longest x23 124 us: body(): factor = lax.linalg.cholesky(gram, symmetrize_input=False)]
    pallas_call x0 -> x1, Pallas kernels: none -> 29.9 us  [whiten(): pl.pallas_call(functools.partial(whiten_kernel, total, n), out_shape=jax....]
    another operation x25 -> x0, local copies, waits for them, and re-layouts: 21.7 us -> none
    another operation x21 -> x0, matrix products: 17.7 us -> none  [the longest x10 9.81 us: body(): factor = lax.linalg.cholesky(gram, symmetrize_input=False)]
    unnamed x51 -> x10, local copies, waits for them, and re-layouts: 21 us -> 3.63 us
  transfers between devices with their start and end apart: 7 -> 7, of which waited for: 7 -> 7; matrix products, arithmetic and copies ran while one was open for 1% -> 3% of each run, Pallas kernels for 0% -> 0%
where the time goes in v2:
time: 191 us; the launch traced here: 190 us
  waiting for transfers between devices  98.6 us (52%)
  starting transfers between devices  43 us (23%)
  Pallas kernels  29.9 us (16%)
  local copies, waits for them, and re-layouts  12.2 us (6%)
  matrix products  4.07 us (2%)
    all_to_all x3, waiting for transfers between devices, spread(): return lax.all_to_all(copies, axis, 0, 0, tiled=True)  36 us
    all_to_all x3, waiting for transfers between devices, reduced(): return jnp.sum(lax.all_to_all(pieces, axis, 0, 0, tiled=True), axis=0)  31.7 us
    all_to_all x1, waiting for transfers between devices, body(): lax.all_to_all(packed, rows_axes, 0, 0, tiled=True)  30.9 us
    pallas_call x1, Pallas kernels, whiten(): pl.pallas_call(functools.partial(whiten_kernel, total, n), out_shape=jax....  29.9 us
    all_to_all x3, starting transfers between devices, reduced(): return jnp.sum(lax.all_to_all(pieces, axis, 0, 0, tiled=True), axis=0)  17.4 us
    all_to_all x3, starting transfers between devices, spread(): return lax.all_to_all(copies, axis, 0, 0, tiled=True)  13.7 us
    all_to_all x1, starting transfers between devices, body(): lax.all_to_all(packed, rows_axes, 0, 0, tiled=True)  11.9 us
  transfers between devices with their start and end apart: 7, of which 7 were waited for; matrix products, arithmetic and copies ran while one was open for 3% of the time, Pallas kernels for 0%

profile of v2, /device:TPU:1, one launch (start us, length us, event | category | flops | bytes accessed | tf_op | source)
XLA Modules:
  0.0 190.1 jit_solution(5619036490255387240)
XLA Ops:
  0.6 3.2 %fusion.7 = f32[768,768]{1,0:T(8,128)S(1)} fusion(f32[128,768]{1,0:T(8,128)} %param.2), kind=kOutput, calls=%fused_computation.34 | convolution fusion | flops 905969664 | bytes 2752512 | tf_op jit(solution)/shard_map/dot_general | solution.py:136
  3.8 0.8 slice_dynamic-update-slice_fusion
  4.6 0.7 slice_dynamic-update-slice_fusion.1
  5.3 0.7 slice_dynamic-update-slice_fusion.2
  8.0 10.5 %all-to-all-start = ((f32[8,336,128]{2,1,0:T(8,128)}), f32[8,336,128]{2,1,0:T(8,128)S(1)}, u32[]{:S(2)}, u32[]{:S(2)}) async-start(f32[8,336,128]{2,1,0:T(8,128)} %bitcast), calls=%async_computation | async-start | bytes 2752512 | tf_op jit(solution)/shard_map/all_to_all | solution.py:118
  19.3 17.7 %all-to-all-done = f32[8,336,128]{2,1,0:T(8,128)S(1)} async-done(((f32[8,336,128]{2,1,0:T(8,128)}), f32[8,336,128]{2,1,0:T(8,128)S(1)}, u32[]{:S(2)}, u32[]{:S(2)}) %all-to-all-start) | async-done | bytes 1376288 | tf_op jit(solution)/shard_map/all_to_all | solution.py:118
  37.1 0.7 reshape.61
  37.8 3.4 %all-to-all-start.1 = ((f32[8,42,128]{2,1,0:T(8,128)}), f32[8,42,128]{2,1,0:T(8,128)S(1)}, u32[]{:S(2)}, u32[]{:S(2)}) async-start(f32[8,42,128]{2,1,0:T(8,128)} %reshape.61), calls=%async_computation.1 | async-start | bytes 393216 | tf_op jit(solution)/shard_map/all_to_all | solution.py:118
  42.0 1.4 copy.31
  43.4 7.8 %all-to-all-done.1 = f32[8,42,128]{2,1,0:T(8,128)S(1)} async-done(((f32[8,42,128]{2,1,0:T(8,128)}), f32[8,42,128]{2,1,0:T(8,128)S(1)}, u32[]{:S(2)}, u32[]{:S(2)}) %all-to-all-start.1) | async-done | bytes 172064 | tf_op jit(solution)/shard_map/all_to_all | solution.py:118
  51.2 11.9 %all-to-all-start.5 = ((f32[128,13,128]{2,1,0:T(8,128)}), f32[128,13,128]{2,1,0:T(8,128)S(1)}, u32[]{:S(2)}, u32[]{:S(2)}) async-start(f32[128,13,128]{2,1,0:T(8,128)} %copy.31), calls=%async_computation.5 | async-start | bytes 2097152 | tf_op jit(solution)/shard_map/all_to_all | solution.py:156
  63.1 30.9 %all-to-all-done.5 = f32[128,13,128]{2,1,0:T(8,128)S(1)} async-done(((f32[128,13,128]{2,1,0:T(8,128)}), f32[128,13,128]{2,1,0:T(8,128)S(1)}, u32[]{:S(2)}, u32[]{:S(2)}) %all-to-all-start.5) | async-done | bytes 852000 | tf_op jit(solution)/shard_map/all_to_all | solution.py:156
  94.7 3.4 %all-to-all-start.2 = ((f32[8,42,128]{2,1,0:T(8,128)}), f32[8,42,128]{2,1,0:T(8,128)S(1)}, u32[]{:S(2)}, u32[]{:S(2)}) async-start(f32[8,42,128]{2,1,0:T(8,128)} %broadcast_in_dim.20), calls=%async_computation.2 | async-start | bytes 393216 | tf_op jit(solution)/shard_map/all_to_all | solution.py:114
  99.4 9.5 %all-to-all-done.2 = f32[8,42,128]{2,1,0:T(8,128)S(1)} async-done(((f32[8,42,128]{2,1,0:T(8,128)}), f32[8,42,128]{2,1,0:T(8,128)S(1)}, u32[]{:S(2)}, u32[]{:S(2)}) %all-to-all-start.2) | async-done | bytes 172064 | tf_op jit(solution)/shard_map/all_to_all | solution.py:114
  109.7 3.6 %all-to-all-start.3 = ((f32[8,42,128]{2,1,0:T(8,128)}), f32[8,42,128]{2,1,0:T(8,128)S(1)}, u32[]{:S(2)}, u32[]{:S(2)}) async-start(f32[8,42,128]{2,1,0:T(8,128)} %broadcast_in_dim.21), calls=%async_computation.3 | async-start | bytes 393216 | tf_op jit(solution)/shard_map/all_to_all | solution.py:114
  113.8 0.8 select_maximum_fusion.1
  114.6 8.2 %all-to-all-done.3 = f32[8,42,128]{2,1,0:T(8,128)S(1)} async-done(((f32[8,42,128]{2,1,0:T(8,128)}), f32[8,42,128]{2,1,0:T(8,128)S(1)}, u32[]{:S(2)}, u32[]{:S(2)}) %all-to-all-start.3) | async-done | bytes 172064 | tf_op jit(solution)/shard_map/all_to_all | solution.py:114
  122.7 3.5 %all-to-all-start.6 = ((f32[4,200,128]{2,1,0:T(8,128)}), f32[4,200,128]{2,1,0:T(8,128)S(1)}, u32[]{:S(2)}, u32[]{:S(2)}) async-start(f32[4,200,128]{2,1,0:T(8,128)} %select_maximum_fusion.1), calls=%async_computation.6 | async-start | bytes 819200 | tf_op jit(solution)/shard_map/all_to_all | solution.py:118
  126.2 6.3 %all-to-all-done.6 = f32[4,200,128]{2,1,0:T(8,128)S(1)} async-done(((f32[4,200,128]{2,1,0:T(8,128)}), f32[4,200,128]{2,1,0:T(8,128)S(1)}, u32[]{:S(2)}, u32[]{:S(2)}) %all-to-all-start.6) | async-done | bytes 409632 | tf_op jit(solution)/shard_map/all_to_all | solution.py:118
  132.5 1.2 broadcast_in_dim.23
  133.6 6.7 %all-to-all-start.4 = ((f32[8,336,128]{2,1,0:T(8,128)}), f32[8,336,128]{2,1,0:T(8,128)S(1)}, u32[]{:S(2)}, u32[]{:S(2)}) async-start(f32[8,336,128]{2,1,0:T(8,128)} %broadcast_in_dim.23), calls=%async_computation.4 | async-start | bytes 2752512 | tf_op jit(solution)/shard_map/all_to_all | solution.py:114
  140.5 18.3 %all-to-all-done.4 = f32[8,336,128]{2,1,0:T(8,128)S(1)} async-done(((f32[8,336,128]{2,1,0:T(8,128)}), f32[8,336,128]{2,1,0:T(8,128)S(1)}, u32[]{:S(2)}, u32[]{:S(2)}) %all-to-all-start.4) | async-done | bytes 1376288 | tf_op jit(solution)/shard_map/all_to_all | solution.py:114
  158.8 29.9 %whiten.1 = f32[160,768]{1,0:T(8,128)S(1)} custom-call(f32[2688,128]{1,0:T(8,128)S(1)} %bitcast.11, f32[160,768]{1,0:T(8,128)S(1)} %pad_maximum_fusion.x_ref), custom_call_target="tpu_custom_call" | custom-call | flops 20000000000 | bytes 4000000 | tf_op jit(solution)/shard_map/whiten/pallas_call | solution.py:95
  188.7 0.8 slice.78
  (42 shorter events, 7.6 us)
Async XLA Ops:
  8.0 10.5 %copy-start.1 = (s32[128]{0:T(128)S(1)}, s32[128]{0:T(128)}, u32[]{:S(2)}) copy-start(s32[128]{0:T(128)} %param.3) | copy-start | bytes 1540
  8.0 10.8 %copy-start = (f32[128,768]{1,0:T(8,128)S(1)}, f32[128,768]{1,0:T(8,128)}, u32[]{:S(2)}) copy-start(f32[128,768]{1,0:T(8,128)} %param.2) | copy-start | bytes 1179652
  8.0 29.0 %all-to-all-start = ((f32[8,336,128]{2,1,0:T(8,128)}), f32[8,336,128]{2,1,0:T(8,128)S(1)}, u32[]{:S(2)}, u32[]{:S(2)}) async-start(f32[8,336,128]{2,1,0:T(8,128)} %bitcast), calls=%async_computation | async-start | bytes 2752512 | tf_op jit(solution)/shard_map/all_to_all | solution.py:118
  37.8 13.4 %all-to-all-start.1 = ((f32[8,42,128]{2,1,0:T(8,128)}), f32[8,42,128]{2,1,0:T(8,128)S(1)}, u32[]{:S(2)}, u32[]{:S(2)}) async-start(f32[8,42,128]{2,1,0:T(8,128)} %reshape.61), calls=%async_computation.1 | async-start | bytes 393216 | tf_op jit(solution)/shard_map/all_to_all | solution.py:118
  51.2 42.8 %all-to-all-start.5 = ((f32[128,13,128]{2,1,0:T(8,128)}), f32[128,13,128]{2,1,0:T(8,128)S(1)}, u32[]{:S(2)}, u32[]{:S(2)}) async-start(f32[128,13,128]{2,1,0:T(8,128)} %copy.31), calls=%async_computation.5 | async-start | bytes 2097152 | tf_op jit(solution)/shard_map/all_to_all | solution.py:156
  94.7 14.3 %all-to-all-start.2 = ((f32[8,42,128]{2,1,0:T(8,128)}), f32[8,42,128]{2,1,0:T(8,128)S(1)}, u32[]{:S(2)}, u32[]{:S(2)}) async-start(f32[8,42,128]{2,1,0:T(8,128)} %broadcast_in_dim.20), calls=%async_computation.2 | async-start | bytes 393216 | tf_op jit(solution)/shard_map/all_to_all | solution.py:114
  109.7 13.0 %all-to-all-start.3 = ((f32[8,42,128]{2,1,0:T(8,128)}), f32[8,42,128]{2,1,0:T(8,128)S(1)}, u32[]{:S(2)}, u32[]{:S(2)}) async-start(f32[8,42,128]{2,1,0:T(8,128)} %broadcast_in_dim.21), calls=%async_computation.3 | async-start | bytes 393216 | tf_op jit(solution)/shard_map/all_to_all | solution.py:114
  122.7 9.8 %all-to-all-start.6 = ((f32[4,200,128]{2,1,0:T(8,128)}), f32[4,200,128]{2,1,0:T(8,128)S(1)}, u32[]{:S(2)}, u32[]{:S(2)}) async-start(f32[4,200,128]{2,1,0:T(8,128)} %select_maximum_fusion.1), calls=%async_computation.6 | async-start | bytes 819200 | tf_op jit(solution)/shard_map/all_to_all | solution.py:118
  133.6 25.2 %all-to-all-start.4 = ((f32[8,336,128]{2,1,0:T(8,128)}), f32[8,336,128]{2,1,0:T(8,128)S(1)}, u32[]{:S(2)}, u32[]{:S(2)}) async-start(f32[8,336,128]{2,1,0:T(8,128)} %broadcast_in_dim.23), calls=%async_computation.4 | async-start | bytes 2752512 | tf_op jit(solution)/shard_map/all_to_all | solution.py:114

commit v3 on v2

--- a/solution.py
+++ b/solution.py
@@ -11,6 +11,8 @@
 CAP = 2
 B = 128
 
+VMEM = pl.BlockSpec(memory_space=pltpu.VMEM)
+SCALAR = pl.BlockSpec(memory_space=pltpu.SMEM)
 HI = lax.Precision.HIGHEST
 NT = (((1,), (1,)), ((), ()))
 
@@ -56,10 +58,13 @@
     return (j * n - j * (j - 1) // 2) * B
 
 
-def whiten_kernel(total, n, gram_ref, x_ref, out_ref, a_ref, x_blocks, inv_ref):
+def whiten_kernel(total, n, bit_ref, mine_ref, other_ref, x_ref, out_ref, a_ref, x_blocks, inv_ref):
     row = lax.broadcasted_iota(jnp.int32, (B, B), 0)
     col = lax.broadcasted_iota(jnp.int32, (B, B), 1)
-    a_ref[...] = gram_ref[...] * (1.0 / total)
+    half = mine_ref.shape[0]
+    bit = bit_ref[0]
+    a_ref[pl.ds(pl.multiple_of(bit * half, 8), half)] = mine_ref[...] * (1.0 / total)
+    a_ref[pl.ds(pl.multiple_of((1 - bit) * half, 8), half)] = other_ref[...] * (1.0 / total)
     for j in range(n):
         at = first(j, n)
         a_ref[at : at + B] += jnp.where(row == col, 1e-05, 0.0)
@@ -90,40 +95,132 @@
     lax.fori_loop(0, n, step, 0)
 
 
-def whiten(gram, x, total):
+def whiten(bit, mine, other, x, total):
     n = x.shape[1] // B
     return pl.pallas_call(
         functools.partial(whiten_kernel, total, n),
         out_shape=jax.ShapeDtypeStruct(x.shape, jnp.float32),
-        in_specs=[pl.BlockSpec(memory_space=pltpu.VMEM)] * 2,
-        out_specs=pl.BlockSpec(memory_space=pltpu.VMEM),
+        in_specs=[SCALAR, VMEM, VMEM, VMEM],
+        out_specs=VMEM,
         scratch_shapes=[
-            pltpu.VMEM(gram.shape, jnp.float32),
+            pltpu.VMEM((2 * mine.shape[0], B), jnp.float32),
             pltpu.VMEM((n, x.shape[0], B), jnp.float32),
             pltpu.VMEM((B, B), jnp.float32),
         ],
-        compiler_params=pltpu.CompilerParams(vmem_limit_bytes=32 << 20),
+        compiler_params=pltpu.CompilerParams(vmem_limit_bytes=12 << 20),
         cost_estimate=pl.CostEstimate(flops=20_000_000_000, bytes_accessed=4_000_000, transcendentals=0),
         name="whiten",
-    )(gram, x)
-
-
-def spread(value, axis):
-    peers = lax.axis_size(axis)
-    copies = jnp.broadcast_to(value[None], (peers, *value.shape))
-    return lax.all_to_all(copies, axis, 0, 0, tiled=True)
+    )(bit, mine, other, x)
+
+
+def gram_kernel(n, bit_ref, x_ref, keep_ref, send_ref, all_ref):
+    turned = x_ref[...].T
+    for j in range(n):
+        all_ref[first(j, n) : first(j + 1, n)] = jnp.dot(
+            turned[j * B :], x_ref[:, j * B : j * B + B], precision=HI, preferred_element_type=jnp.float32
+        )
+    half = keep_ref.shape[0]
+    bit = bit_ref[0]
+    keep_ref[...] = all_ref[pl.ds(pl.multiple_of(bit * half, 8), half)]
+    send_ref[...] = all_ref[pl.ds(pl.multiple_of((1 - bit) * half, 8), half)]
+
+
+def gram_halves(bit, x):
+    n = x.shape[1] // B
+    rows = first(n, n)
+    return pl.pallas_call(
+        functools.partial(gram_kernel, n),
+        out_shape=[jax.ShapeDtypeStruct((rows // 2, B), jnp.float32)] * 2,
+        in_specs=[SCALAR, VMEM],
+        out_specs=[VMEM, VMEM],
+        scratch_shapes=[pltpu.VMEM((rows, B), jnp.float32)],
+        compiler_params=pltpu.CompilerParams(vmem_limit_bytes=12 << 20),
+        cost_estimate=pl.CostEstimate(flops=700_000_000, bytes_accessed=2_000_000, transcendentals=0),
+        name="gram",
+    )(bit, x)
+
+
+def cut_kernel(terms, order, at_ref, *refs):
+    ins, outs, total_ref = refs[:terms], refs[terms:-1], refs[-1]
+    rows = ins[0].shape[0]
+    total_ref[:rows] = functools.reduce(lambda a, b: a + b, [r[...] for r in ins])
+    if rows < total_ref.shape[0]:
+        total_ref[rows:] = jnp.zeros((total_ref.shape[0] - rows, B), jnp.float32)
+    size = outs[0].shape[0]
+    for s, out in enumerate(outs):
+        out[...] = total_ref[pl.ds(pl.multiple_of(order(at_ref[0], s) * size, 8), size)]
+
+
+def cut(at, arrays, pieces, rows, name):
+    return pl.pallas_call(
+        functools.partial(cut_kernel, len(arrays), lambda a, s: (a + s) & (pieces - 1)),
+        out_shape=[jax.ShapeDtypeStruct((rows // pieces, B), jnp.float32)] * pieces,
+        in_specs=[SCALAR] + [VMEM] * len(arrays),
+        out_specs=[VMEM] * pieces,
+        scratch_shapes=[pltpu.VMEM((rows, B), jnp.float32)],
+        compiler_params=pltpu.CompilerParams(vmem_limit_bytes=6 << 20),
+        cost_estimate=pl.CostEstimate(flops=1_000_000, bytes_accessed=3_000_000, transcendentals=0),
+        name=name,
+    )(at, *arrays)
+
+
+def place_kernel(at_ref, *refs):
+    out = refs[-1]
+    count = len(refs) - 1
+    size = refs[0].shape[0]
+    for s in range(count):
+        out[pl.ds(pl.multiple_of(((at_ref[0] - s) & (count - 1)) * size, 8), size)] = refs[s][...]
+
+
+def place(at, arrays, name):
+    rows = arrays[0].shape[0] * len(arrays)
+    return pl.pallas_call(
+        place_kernel,
+        out_shape=jax.ShapeDtypeStruct((rows, B), jnp.float32),
+        in_specs=[SCALAR] + [VMEM] * len(arrays),
+        out_specs=VMEM,
+        compiler_params=pltpu.CompilerParams(vmem_limit_bytes=6 << 20),
+        cost_estimate=pl.CostEstimate(flops=0, bytes_accessed=1_500_000, transcendentals=0),
+        name=name,
+    )(at, *arrays)
+
+
+def shifted(value, axis, by):
+    size = lax.axis_size(axis)
+    return lax.ppermute(value, axis, [(i, (i + by) % size) for i in range(size)])
+
+
+def swapped(value, axis, by):
+    return lax.ppermute(value, axis, [(i, i ^ by) for i in range(lax.axis_size(axis))])
+
+
+def index(axis):
+    return lax.axis_index(axis).reshape(1)
+
+
+def gram_sum(keep, send):
+    keep_rows = keep.shape[0]
+    x, y = index("x"), index("y")
+    pieces = cut(x, [keep, swapped(send, "core", 1)], 4, keep_rows, "cut_x")
+    terms = [pieces[0]] + [shifted(pieces[s], "x", s) for s in (1, 2, 3)]
+    rows = 384
+    for by in (1, 2, 4):
+        keep, send = cut((y // by) % 2, terms, 2, rows, "cut_y")
+        terms = [keep, swapped(send, "y", by)]
+        rows //= 2
+    mine = terms[0] + terms[1]
+    for by in (1, 2, 4):
+        mine = mine + swapped(mine, "z", by)
+    for by in (4, 2, 1):
+        other = swapped(mine, "y", by)
+        mine = place((y // by) % 2, [mine, other], "place_y")
+    mine = mine[: keep_rows // 4]
+    mine = place(x, [mine] + [shifted(mine, "x", s) for s in (1, 2, 3)], "place_x")
+    return mine, swapped(mine, "core", 1)
 
 
 def reduced(pieces, axis):
     return jnp.sum(lax.all_to_all(pieces, axis, 0, 0, tiled=True), axis=0)
-
-
-def gram_sum(part):
-    mine = reduced(part.reshape(8, 336, B), ("core", "x"))
-    mine = reduced(mine.reshape(8, 42, B), "y")
-    mine = jnp.sum(spread(mine, "z"), axis=0)
-    mine = spread(mine, "y").reshape(336, B)
-    return spread(mine, ("core", "x")).reshape(2688, B)
 
 
 def body(embeddings, assignments):
@@ -133,11 +230,8 @@
     total = rows_here * owners * lax.axis_size("x")
     per_owner = CENTROIDS // owners
     n = width // B
-    part = jnp.dot(
-        embeddings.T, embeddings, precision=lax.Precision.HIGHEST, preferred_element_type=jnp.float32
-    )
-    lower = [(i, j) for j in range(n) for i in range(j, n)]
-    part = jnp.concatenate([part[i * B : i * B + B, j * B : j * B + B] for i, j in lower], axis=0)
+    bit = index("core")
+    half, send = gram_halves(bit, embeddings)
 
     target = assignments // per_owner
     local = assignments % per_owner
@@ -167,9 +261,9 @@
     sums = mine[: keep * n].reshape(keep, width)
     counts = mine[keep * n, :keep]
 
-    whole = gram_sum(part)
+    mine, other = gram_sum(half, send)
     means = sums / jnp.maximum(counts, 1.0)[:, None]
-    solved = whiten(whole, jnp.concatenate([embeddings, means], axis=0), total)
+    solved = whiten(bit, mine, other, jnp.concatenate([embeddings, means], axis=0), total)
     return solved[:rows_here], solved[rows_here:]
 
 

time: 191 us -> 170 us (0.89)
  waiting for transfers between devices: 98.6 us -> 27.3 us
  starting transfers between devices: 43 us -> 101 us
  local copies, waits for them, and re-layouts: 12.2 us -> 4.7 us
  matrix products: 4.07 us -> 1.93 us
    ppermute x0 -> x17, starting transfers between devices: none -> 76.9 us  [the longest x11 56.6 us: swapped(): lax.ppermute(value, axis, [(i, i ^ by) for i in range(lax.axis_size(axis))])]
    all_to_all x3 -> x0, waiting for transfers between devices: 36 us -> none  [spread(): return lax.all_to_all(copies, axis, 0, 0, tiled=True)]
    all_to_all x3 -> x1, waiting for transfers between devices: 31.7 us -> 0.01 us  [reduced(): return jnp.sum(lax.all_to_all(pieces, axis, 0, 0, tiled=True), axis=0)]
    all_to_all x1, waiting for transfers between devices: 30.9 us -> 0.01 us  [body(): lax.all_to_all(packed, rows_axes, 0, 0, tiled=True)]
    ppermute x0 -> x17, waiting for transfers between devices: none -> 27.3 us  [the longest x11 15.9 us: swapped(): lax.ppermute(value, axis, [(i, i ^ by) for i in range(lax.axis_size(axis))])]
    all_to_all x3 -> x0, starting transfers between devices: 13.7 us -> none  [spread(): return lax.all_to_all(copies, axis, 0, 0, tiled=True)]
    all_to_all x3 -> x1, starting transfers between devices: 17.4 us -> 5.24 us  [reduced(): return jnp.sum(lax.all_to_all(pieces, axis, 0, 0, tiled=True), axis=0)]
    all_to_all x1, starting transfers between devices: 11.9 us -> 18.6 us  [body(): lax.all_to_all(packed, rows_axes, 0, 0, tiled=True)]
  transfers between devices with their start and end apart: 7 -> 19, of which waited for: 7 -> 14; matrix products, arithmetic and copies ran while one was open for 3% -> 2% of each run, Pallas kernels for 0% -> 1%
where the time goes in v3:
time: 170 us; the launch traced here: 169 us
  starting transfers between devices  101 us (59%)
  Pallas kernels  31.6 us (19%)
  waiting for transfers between devices  27.3 us (16%)
  local copies, waits for them, and re-layouts  4.7 us (3%)
  other arithmetic  2.09 us (1%)
  matrix products  1.93 us (1%)
    ppermute x11, starting transfers between devices, swapped(): lax.ppermute(value, axis, [(i, i ^ by) for i in range(lax.axis_size(axis))])  56.6 us
    pallas_call x1, Pallas kernels, whiten(): pl.pallas_call(functools.partial(whiten_kernel, total, n), out_shape=jax....  30 us
    ppermute x6, starting transfers between devices, shifted(): lax.ppermute(value, axis, [(i, (i + by) % size) for i in range(size)])  20.3 us
    all_to_all x1, starting transfers between devices, body(): lax.all_to_all(packed, rows_axes, 0, 0, tiled=True)  18.6 us
    ppermute x11, waiting for transfers between devices, swapped(): lax.ppermute(value, axis, [(i, i ^ by) for i in range(lax.axis_size(axis))])  15.9 us
    ppermute x6, waiting for transfers between devices, shifted(): lax.ppermute(value, axis, [(i, (i + by) % size) for i in range(size)])  11.4 us
    all_to_all x1, starting transfers between devices, reduced(): return jnp.sum(lax.all_to_all(pieces, axis, 0, 0, tiled=True), axis=0)  5.24 us
  transfers between devices with their start and end apart: 19, of which 14 were waited for; matrix products, arithmetic and copies ran while one was open for 2% of the time, Pallas kernels for 1%

profile of v3, /device:TPU:1, one launch (start us, length us, event | category | flops | bytes accessed | tf_op | source)
XLA Modules:
  0.0 169.5 jit_solution(1676606231766412146)
XLA Ops:
  5.3 18.6 %all-to-all-start = ((f32[128,13,128]{2,1,0:T(8,128)}), f32[128,13,128]{2,1,0:T(8,128)S(1)}, u32[]{:S(2)}, u32[]{:S(2)}) async-start(f32[128,13,128]{2,1,0:T(8,128)} %copy.23), calls=%async_computation | async-start | bytes 2097152 | tf_op jit(solution)/shard_map/all_to_all | solution.py:250
  25.3 2.8 %collective-permute-start = (f32[1344,128]{1,0:T(8,128)S(1)}, f32[1344,128]{1,0:T(8,128)S(1)}, u32[]{:S(2)}, u32[]{:S(2)}) collective-permute-start(f32[1344,128]{1,0:T(8,128)S(1)} %get-tuple-element.15), channel_id=1, source_target_pairs={{0,4},{4,0},{1,5},{5,1},{2,6},{6,2},{3,7},{7,3},{8,12},{12,8},{9,1... | collective-permute-start | bytes 2064392 | tf_op jit(solution)/shard_map/ppermute | solution.py:194
  29.9 3.1 %collective-permute-start.1 = (f32[336,128]{1,0:T(8,128)S(1)}, f32[336,128]{1,0:T(8,128)S(1)}, u32[]{:S(2)}, u32[]{:S(2)}) collective-permute-start(f32[336,128]{1,0:T(8,128)S(1)} %get-tuple-element.17), channel_id=1, source_target_pairs={{0,1},{1,2},{2,3},{3,0},{4,5},{5,6},{6,7},{7,4},{8,9},{9,10},{10,1... | collective-permute-start | bytes 516104 | tf_op jit(solution)/shard_map/ppermute | solution.py:190
  33.1 4.4 %collective-permute-start.2 = (f32[336,128]{1,0:T(8,128)S(1)}, f32[336,128]{1,0:T(8,128)S(1)}, u32[]{:S(2)}, u32[]{:S(2)}) collective-permute-start(f32[336,128]{1,0:T(8,128)S(1)} %get-tuple-element.18), channel_id=1, source_target_pairs={{0,2},{1,3},{2,0},{3,1},{4,6},{5,7},{6,4},{7,5},{8,10},{9,11},{10,... | collective-permute-start | bytes 516104 | tf_op jit(solution)/shard_map/ppermute | solution.py:190
  37.4 3.1 %collective-permute-start.3 = (f32[336,128]{1,0:T(8,128)S(1)}, f32[336,128]{1,0:T(8,128)S(1)}, u32[]{:S(2)}, u32[]{:S(2)}) collective-permute-start(f32[336,128]{1,0:T(8,128)S(1)} %get-tuple-element.19), channel_id=1, source_target_pairs={{0,3},{1,0},{2,1},{3,2},{4,7},{5,4},{6,5},{7,6},{8,11},{9,8},{10,9... | collective-permute-start | bytes 516104 | tf_op jit(solution)/shard_map/ppermute | solution.py:190
  40.5 2.8 %collective-permute-done.2.refs_2_ = f32[336,128]{1,0:T(8,128)S(1)} collective-permute-done((f32[336,128]{1,0:T(8,128)S(1)}, f32[336,128]{1,0:T(8,128)S(1)}, u32[]{:S(2)}, u32[]{:S(2)}) %collective-permute-start.2) | collective-permute-done | bytes 172064 | tf_op jit(solution)/shard_map/ppermute | solution.py:190
  44.3 2.8 %collective-permute-start.4 = (f32[192,128]{1,0:T(8,128)S(1)}, f32[192,128]{1,0:T(8,128)S(1)}, u32[]{:S(2)}, u32[]{:S(2)}) collective-permute-start(f32[192,128]{1,0:T(8,128)S(1)} %get-tuple-element.21), channel_id=1, source_target_pairs={{0,8},{8,0},{16,24},{24,16},{32,40},{40,32},{48,56},{56,48},{1,9},... | collective-permute-start | bytes 294920 | tf_op jit(solution)/shard_map/ppermute | solution.py:194
  47.2 2.8 %collective-permute-done.4.refs_1_ = f32[192,128]{1,0:T(8,128)S(1)} collective-permute-done((f32[192,128]{1,0:T(8,128)S(1)}, f32[192,128]{1,0:T(8,128)S(1)}, u32[]{:S(2)}, u32[]{:S(2)}) %collective-permute-start.4) | collective-permute-done | bytes 98336 | tf_op jit(solution)/shard_map/ppermute | solution.py:194
  50.0 4.7 %collective-permute-start.5 = (f32[96,128]{1,0:T(8,128)S(1)}, f32[96,128]{1,0:T(8,128)S(1)}, u32[]{:S(2)}, u32[]{:S(2)}) collective-permute-start(f32[96,128]{1,0:T(8,128)S(1)} %get-tuple-element.23), channel_id=1, source_target_pairs={{0,16},{8,24},{16,0},{24,8},{32,48},{40,56},{48,32},{56,40},{1,17}... | collective-permute-start | bytes 147464 | tf_op jit(solution)/shard_map/ppermute | solution.py:194
  56.2 6.8 %collective-permute-start.6 = (f32[48,128]{1,0:T(8,128)S(1)}, f32[48,128]{1,0:T(8,128)S(1)}, u32[]{:S(2)}, u32[]{:S(2)}) collective-permute-start(f32[48,128]{1,0:T(8,128)S(1)} %get-tuple-element.25), channel_id=1, source_target_pairs={{0,32},{8,40},{16,48},{24,56},{32,0},{40,8},{48,16},{56,24},{1,33}... | collective-permute-start | bytes 73736 | tf_op jit(solution)/shard_map/ppermute | solution.py:194
  64.6 3.1 %collective-permute-start.7 = (f32[48,128]{1,0:T(8,128)S(1)}, f32[48,128]{1,0:T(8,128)S(1)}, u32[]{:S(2)}, u32[]{:S(2)}) collective-permute-start(f32[48,128]{1,0:T(8,128)S(1)} %add.59), channel_id=1, source_target_pairs={{0,64},{64,0},{128,192},{192,128},{256,320},{320,256},{384,448},{4... | collective-permute-start | bytes 73736 | tf_op jit(solution)/shard_map/ppermute | solution.py:194
  69.2 4.1 %collective-permute-start.8 = (f32[48,128]{1,0:T(8,128)S(1)}, f32[48,128]{1,0:T(8,128)S(1)}, u32[]{:S(2)}, u32[]{:S(2)}) collective-permute-start(f32[48,128]{1,0:T(8,128)S(1)} %add.60), channel_id=1, source_target_pairs={{0,128},{64,192},{128,0},{192,64},{256,384},{320,448},{384,256},{4... | collective-permute-start | bytes 73736 | tf_op jit(solution)/shard_map/ppermute | solution.py:194
  74.7 7.1 %collective-permute-start.9 = (f32[48,128]{1,0:T(8,128)S(1)}, f32[48,128]{1,0:T(8,128)S(1)}, u32[]{:S(2)}, u32[]{:S(2)}) collective-permute-start(f32[48,128]{1,0:T(8,128)S(1)} %add.61), channel_id=1, source_target_pairs={{0,256},{64,320},{128,384},{192,448},{256,0},{320,64},{384,128},{4... | collective-permute-start | bytes 73736 | tf_op jit(solution)/shard_map/ppermute | solution.py:194
  83.1 7.2 %collective-permute-start.10 = (f32[48,128]{1,0:T(8,128)S(1)}, f32[48,128]{1,0:T(8,128)S(1)}, u32[]{:S(2)}, u32[]{:S(2)}) collective-permute-start(f32[48,128]{1,0:T(8,128)S(1)} %add.62.refs_0_), channel_id=1, source_target_pairs={{0,32},{8,40},{16,48},{24,56},{32,0},{40,8},{48,16},{56,24},{1,33}... | collective-permute-start | bytes 73736 | tf_op jit(solution)/shard_map/ppermute | solution.py:194
  91.6 4.3 %collective-permute-start.11 = (f32[96,128]{1,0:T(8,128)S(1)}, f32[96,128]{1,0:T(8,128)S(1)}, u32[]{:S(2)}, u32[]{:S(2)}) collective-permute-start(f32[96,128]{1,0:T(8,128)S(1)} %place_y.3.refs_0_), channel_id=1, source_target_pairs={{0,16},{8,24},{16,0},{24,8},{32,48},{40,56},{48,32},{56,40},{1,17}... | collective-permute-start | bytes 147464 | tf_op jit(solution)/shard_map/ppermute | solution.py:194
  97.5 3.0 %collective-permute-start.12 = (f32[192,128]{1,0:T(8,128)S(1)}, f32[192,128]{1,0:T(8,128)S(1)}, u32[]{:S(2)}, u32[]{:S(2)}) collective-permute-start(f32[192,128]{1,0:T(8,128)S(1)} %place_y.4.refs_0_), channel_id=1, source_target_pairs={{0,8},{8,0},{16,24},{24,16},{32,40},{40,32},{48,56},{56,48},{1,9},... | collective-permute-start | bytes 294920 | tf_op jit(solution)/shard_map/ppermute | solution.py:194
  103.1 5.2 %all-to-all-start.1 = ((f32[4,200,128]{2,1,0:T(8,128)}), f32[4,200,128]{2,1,0:T(8,128)S(1)}, u32[]{:S(2)}, u32[]{:S(2)}) async-start(f32[4,200,128]{2,1,0:T(8,128)} %select_maximum_fusion.1), calls=%async_computation.1 | async-start | bytes 819200 | tf_op jit(solution)/shard_map/all_to_all | solution.py:223
  108.4 4.6 %collective-permute-start.15 = (f32[336,128]{1,0:T(8,128)S(1)}, f32[336,128]{1,0:T(8,128)S(1)}, u32[]{:S(2)}, u32[]{:S(2)}) collective-permute-start(f32[336,128]{1,0:T(8,128)S(1)} %slice.28.refs_0_), channel_id=1, source_target_pairs={{0,3},{1,0},{2,1},{3,2},{4,7},{5,4},{6,5},{7,6},{8,11},{9,8},{10,9... | collective-permute-start | bytes 516104 | tf_op jit(solution)/shard_map/ppermute | solution.py:190
  113.0 3.2 %collective-permute-start.14 = (f32[336,128]{1,0:T(8,128)S(1)}, f32[336,128]{1,0:T(8,128)S(1)}, u32[]{:S(2)}, u32[]{:S(2)}) collective-permute-start(f32[336,128]{1,0:T(8,128)S(1)} %slice.28.refs_0_), channel_id=1, source_target_pairs={{0,2},{1,3},{2,0},{3,1},{4,6},{5,7},{6,4},{7,5},{8,10},{9,11},{10,... | collective-permute-start | bytes 516104 | tf_op jit(solution)/shard_map/ppermute | solution.py:190
  116.2 1.9 %collective-permute-start.13 = (f32[336,128]{1,0:T(8,128)S(1)}, f32[336,128]{1,0:T(8,128)S(1)}, u32[]{:S(2)}, u32[]{:S(2)}) collective-permute-start(f32[336,128]{1,0:T(8,128)S(1)} %slice.28.refs_0_), channel_id=1, source_target_pairs={{0,1},{1,2},{2,3},{3,0},{4,5},{5,6},{6,7},{7,4},{8,9},{9,10},{10,1... | collective-permute-start | bytes 516104 | tf_op jit(solution)/shard_map/ppermute | solution.py:190
  118.1 2.5 %collective-permute-done.14.refs_2_ = f32[336,128]{1,0:T(8,128)S(1)} collective-permute-done((f32[336,128]{1,0:T(8,128)S(1)}, f32[336,128]{1,0:T(8,128)S(1)}, u32[]{:S(2)}, u32[]{:S(2)}) %collective-permute-start.14) | collective-permute-done | bytes 172064 | tf_op jit(solution)/shard_map/ppermute | solution.py:190
  120.6 5.1 %collective-permute-done.13.refs_1_ = f32[336,128]{1,0:T(8,128)S(1)} collective-permute-done((f32[336,128]{1,0:T(8,128)S(1)}, f32[336,128]{1,0:T(8,128)S(1)}, u32[]{:S(2)}, u32[]{:S(2)}) %collective-permute-start.13) | collective-permute-done | bytes 172064 | tf_op jit(solution)/shard_map/ppermute | solution.py:190
  125.8 10.7 %collective-permute-start.16 = (f32[1344,128]{1,0:T(8,128)S(1)}, f32[1344,128]{1,0:T(8,128)S(1)}, u32[]{:S(2)}, u32[]{:S(2)}) collective-permute-start(f32[1344,128]{1,0:T(8,128)S(1)} %place_x.1.mine_ref), channel_id=1, source_target_pairs={{0,4},{4,0},{1,5},{5,1},{2,6},{6,2},{3,7},{7,3},{8,12},{12,8},{9,1... | collective-permute-start | bytes 2064392 | tf_op jit(solution)/shard_map/ppermute | solution.py:194
  138.1 30.0 %whiten.1 = f32[160,768]{1,0:T(8,128)S(1)} custom-call(s32[1]{0:T(128)} %bitcast.bit_ref, f32[1344,128]{1,0:T(8,128)S(1)} %place_x.1.mine_ref, f32[1344,128]{1,0:T(8,128)S(1)} %collective-permute-done.16.other_ref, f32[160,768]{1,0:T(8,128)S(1)} %pad_maximum_fusion.x_ref), custom_call_target="tpu_custom_call" | custom-call | flops 20000000000 | bytes 4000000 | tf_op jit(solution)/shard_map/whiten/pallas_call | solution.py:100
  (63 shorter events, 24.5 us)
Async XLA Ops:
  5.3 18.6 %copy-start = (f32[128,768]{1,0:T(8,128)S(1)}, f32[128,768]{1,0:T(8,128)}, u32[]{:S(2)}) copy-start(f32[128,768]{1,0:T(8,128)} %x_ref.1) | copy-start | bytes 1179652
  5.3 95.2 %all-to-all-start = ((f32[128,13,128]{2,1,0:T(8,128)}), f32[128,13,128]{2,1,0:T(8,128)S(1)}, u32[]{:S(2)}, u32[]{:S(2)}) async-start(f32[128,13,128]{2,1,0:T(8,128)} %copy.23), calls=%async_computation | async-start | bytes 2097152 | tf_op jit(solution)/shard_map/all_to_all | solution.py:250
  25.3 4.6 %collective-permute-start = (f32[1344,128]{1,0:T(8,128)S(1)}, f32[1344,128]{1,0:T(8,128)S(1)}, u32[]{:S(2)}, u32[]{:S(2)}) collective-permute-start(f32[1344,128]{1,0:T(8,128)S(1)} %get-tuple-element.15), channel_id=1, source_target_pairs={{0,4},{4,0},{1,5},{5,1},{2,6},{6,2},{3,7},{7,3},{8,12},{12,8},{9,1... | collective-permute-start | bytes 2064392 | tf_op jit(solution)/shard_map/ppermute | solution.py:194
  29.9 10.6 %collective-permute-start.1 = (f32[336,128]{1,0:T(8,128)S(1)}, f32[336,128]{1,0:T(8,128)S(1)}, u32[]{:S(2)}, u32[]{:S(2)}) collective-permute-start(f32[336,128]{1,0:T(8,128)S(1)} %get-tuple-element.17), channel_id=1, source_target_pairs={{0,1},{1,2},{2,3},{3,0},{4,5},{5,6},{6,7},{7,4},{8,9},{9,10},{10,1... | collective-permute-start | bytes 516104 | tf_op jit(solution)/shard_map/ppermute | solution.py:190
  33.1 10.2 %collective-permute-start.2 = (f32[336,128]{1,0:T(8,128)S(1)}, f32[336,128]{1,0:T(8,128)S(1)}, u32[]{:S(2)}, u32[]{:S(2)}) collective-permute-start(f32[336,128]{1,0:T(8,128)S(1)} %get-tuple-element.18), channel_id=1, source_target_pairs={{0,2},{1,3},{2,0},{3,1},{4,6},{5,7},{6,4},{7,5},{8,10},{9,11},{10,... | collective-permute-start | bytes 516104 | tf_op jit(solution)/shard_map/ppermute | solution.py:190
  37.4 6.8 %collective-permute-start.3 = (f32[336,128]{1,0:T(8,128)S(1)}, f32[336,128]{1,0:T(8,128)S(1)}, u32[]{:S(2)}, u32[]{:S(2)}) collective-permute-start(f32[336,128]{1,0:T(8,128)S(1)} %get-tuple-element.19), channel_id=1, source_target_pairs={{0,3},{1,0},{2,1},{3,2},{4,7},{5,4},{6,5},{7,6},{8,11},{9,8},{10,9... | collective-permute-start | bytes 516104 | tf_op jit(solution)/shard_map/ppermute | solution.py:190
  44.3 5.7 %collective-permute-start.4 = (f32[192,128]{1,0:T(8,128)S(1)}, f32[192,128]{1,0:T(8,128)S(1)}, u32[]{:S(2)}, u32[]{:S(2)}) collective-permute-start(f32[192,128]{1,0:T(8,128)S(1)} %get-tuple-element.21), channel_id=1, source_target_pairs={{0,8},{8,0},{16,24},{24,16},{32,40},{40,32},{48,56},{56,48},{1,9},... | collective-permute-start | bytes 294920 | tf_op jit(solution)/shard_map/ppermute | solution.py:194
  50.0 6.1 %collective-permute-start.5 = (f32[96,128]{1,0:T(8,128)S(1)}, f32[96,128]{1,0:T(8,128)S(1)}, u32[]{:S(2)}, u32[]{:S(2)}) collective-permute-start(f32[96,128]{1,0:T(8,128)S(1)} %get-tuple-element.23), channel_id=1, source_target_pairs={{0,16},{8,24},{16,0},{24,8},{32,48},{40,56},{48,32},{56,40},{1,17}... | collective-permute-start | bytes 147464 | tf_op jit(solution)/shard_map/ppermute | solution.py:194
  56.2 8.5 %collective-permute-start.6 = (f32[48,128]{1,0:T(8,128)S(1)}, f32[48,128]{1,0:T(8,128)S(1)}, u32[]{:S(2)}, u32[]{:S(2)}) collective-permute-start(f32[48,128]{1,0:T(8,128)S(1)} %get-tuple-element.25), channel_id=1, source_target_pairs={{0,32},{8,40},{16,48},{24,56},{32,0},{40,8},{48,16},{56,24},{1,33}... | collective-permute-start | bytes 73736 | tf_op jit(solution)/shard_map/ppermute | solution.py:194
  64.6 4.6 %collective-permute-start.7 = (f32[48,128]{1,0:T(8,128)S(1)}, f32[48,128]{1,0:T(8,128)S(1)}, u32[]{:S(2)}, u32[]{:S(2)}) collective-permute-start(f32[48,128]{1,0:T(8,128)S(1)} %add.59), channel_id=1, source_target_pairs={{0,64},{64,0},{128,192},{192,128},{256,320},{320,256},{384,448},{4... | collective-permute-start | bytes 73736 | tf_op jit(solution)/shard_map/ppermute | solution.py:194
  69.2 5.5 %collective-permute-start.8 = (f32[48,128]{1,0:T(8,128)S(1)}, f32[48,128]{1,0:T(8,128)S(1)}, u32[]{:S(2)}, u32[]{:S(2)}) collective-permute-start(f32[48,128]{1,0:T(8,128)S(1)} %add.60), channel_id=1, source_target_pairs={{0,128},{64,192},{128,0},{192,64},{256,384},{320,448},{384,256},{4... | collective-permute-start | bytes 73736 | tf_op jit(solution)/shard_map/ppermute | solution.py:194
  74.7 8.5 %collective-permute-start.9 = (f32[48,128]{1,0:T(8,128)S(1)}, f32[48,128]{1,0:T(8,128)S(1)}, u32[]{:S(2)}, u32[]{:S(2)}) collective-permute-start(f32[48,128]{1,0:T(8,128)S(1)} %add.61), channel_id=1, source_target_pairs={{0,256},{64,320},{128,384},{192,448},{256,0},{320,64},{384,128},{4... | collective-permute-start | bytes 73736 | tf_op jit(solution)/shard_map/ppermute | solution.py:194
  83.1 8.5 %collective-permute-start.10 = (f32[48,128]{1,0:T(8,128)S(1)}, f32[48,128]{1,0:T(8,128)S(1)}, u32[]{:S(2)}, u32[]{:S(2)}) collective-permute-start(f32[48,128]{1,0:T(8,128)S(1)} %add.62.refs_0_), channel_id=1, source_target_pairs={{0,32},{8,40},{16,48},{24,56},{32,0},{40,8},{48,16},{56,24},{1,33}... | collective-permute-start | bytes 73736 | tf_op jit(solution)/shard_map/ppermute | solution.py:194
  91.6 5.8 %collective-permute-start.11 = (f32[96,128]{1,0:T(8,128)S(1)}, f32[96,128]{1,0:T(8,128)S(1)}, u32[]{:S(2)}, u32[]{:S(2)}) collective-permute-start(f32[96,128]{1,0:T(8,128)S(1)} %place_y.3.refs_0_), channel_id=1, source_target_pairs={{0,16},{8,24},{16,0},{24,8},{32,48},{40,56},{48,32},{56,40},{1,17}... | collective-permute-start | bytes 147464 | tf_op jit(solution)/shard_map/ppermute | solution.py:194
  97.5 10.9 %collective-permute-start.12 = (f32[192,128]{1,0:T(8,128)S(1)}, f32[192,128]{1,0:T(8,128)S(1)}, u32[]{:S(2)}, u32[]{:S(2)}) collective-permute-start(f32[192,128]{1,0:T(8,128)S(1)} %place_y.4.refs_0_), channel_id=1, source_target_pairs={{0,8},{8,0},{16,24},{24,16},{32,40},{40,32},{48,56},{56,48},{1,9},... | collective-permute-start | bytes 294920 | tf_op jit(solution)/shard_map/ppermute | solution.py:194
  103.1 33.4 %all-to-all-start.1 = ((f32[4,200,128]{2,1,0:T(8,128)}), f32[4,200,128]{2,1,0:T(8,128)S(1)}, u32[]{:S(2)}, u32[]{:S(2)}) async-start(f32[4,200,128]{2,1,0:T(8,128)} %select_maximum_fusion.1), calls=%async_computation.1 | async-start | bytes 819200 | tf_op jit(solution)/shard_map/all_to_all | solution.py:223
  108.4 9.8 %collective-permute-start.15 = (f32[336,128]{1,0:T(8,128)S(1)}, f32[336,128]{1,0:T(8,128)S(1)}, u32[]{:S(2)}, u32[]{:S(2)}) collective-permute-start(f32[336,128]{1,0:T(8,128)S(1)} %slice.28.refs_0_), channel_id=1, source_target_pairs={{0,3},{1,0},{2,1},{3,2},{4,7},{5,4},{6,5},{7,6},{8,11},{9,8},{10,9... | collective-permute-start | bytes 516104 | tf_op jit(solution)/shard_map/ppermute | solution.py:190
  113.0 7.7 %collective-permute-start.14 = (f32[336,128]{1,0:T(8,128)S(1)}, f32[336,128]{1,0:T(8,128)S(1)}, u32[]{:S(2)}, u32[]{:S(2)}) collective-permute-start(f32[336,128]{1,0:T(8,128)S(1)} %slice.28.refs_0_), channel_id=1, source_target_pairs={{0,2},{1,3},{2,0},{3,1},{4,6},{5,7},{6,4},{7,5},{8,10},{9,11},{10,... | collective-permute-start | bytes 516104 | tf_op jit(solution)/shard_map/ppermute | solution.py:190
  116.2 9.6 %collective-permute-start.13 = (f32[336,128]{1,0:T(8,128)S(1)}, f32[336,128]{1,0:T(8,128)S(1)}, u32[]{:S(2)}, u32[]{:S(2)}) collective-permute-start(f32[336,128]{1,0:T(8,128)S(1)} %slice.28.refs_0_), channel_id=1, source_target_pairs={{0,1},{1,2},{2,3},{3,0},{4,5},{5,6},{6,7},{7,4},{8,9},{9,10},{10,1... | collective-permute-start | bytes 516104 | tf_op jit(solution)/shard_map/ppermute | solution.py:190
  125.8 12.3 %collective-permute-start.16 = (f32[1344,128]{1,0:T(8,128)S(1)}, f32[1344,128]{1,0:T(8,128)S(1)}, u32[]{:S(2)}, u32[]{:S(2)}) collective-permute-start(f32[1344,128]{1,0:T(8,128)S(1)} %place_x.1.mine_ref), channel_id=1, source_target_pairs={{0,4},{4,0},{1,5},{5,1},{2,6},{6,2},{3,7},{7,3},{8,12},{12,8},{9,1... | collective-permute-start | bytes 2064392 | tf_op jit(solution)/shard_map/ppermute | solution.py:194

commit v4 on v3

--- a/solution.py
+++ b/solution.py
@@ -58,7 +58,7 @@
     return (j * n - j * (j - 1) // 2) * B
 
 
-def whiten_kernel(total, n, bit_ref, mine_ref, other_ref, x_ref, out_ref, a_ref, x_blocks, inv_ref):
+def whiten_kernel(total, n, bit_ref, mine_ref, other_ref, x_ref, out_ref, a_ref, x_blocks):
     row = lax.broadcasted_iota(jnp.int32, (B, B), 0)
     col = lax.broadcasted_iota(jnp.int32, (B, B), 1)
     half = mine_ref.shape[0]
@@ -70,29 +70,24 @@
         a_ref[at : at + B] += jnp.where(row == col, 1e-05, 0.0)
         x_blocks[j] = x_ref[:, j * B : j * B + B]
 
-    def step(k, carry):
-        inv_ref[...] = inverse_factor(a_ref[pl.ds(pl.multiple_of(first(k, n), B), B)])
-        for now in range(n):
-
-            @pl.when(k == now)
-            def _():
-                inv = inv_ref[...]
-                at = first(now, n) + B
-                below = (n - now - 1) * B
-                solved = mul_t(x_blocks[now], inv)
-                out_ref[:, now * B : now * B + B] = solved
-                if below:
-                    panel = mul_t(a_ref[at : at + below], inv)
-                    for j in range(now + 1, n):
-                        top = (j - now - 1) * B
-                        to = first(j, n)
-                        part = panel[top : top + B]
-                        a_ref[to : to + (n - j) * B] -= mul_t(panel[top:], part)
-                        x_blocks[j] -= mul_t(solved, part)
-
-        return carry
-
-    lax.fori_loop(0, n, step, 0)
+    inv = inverse_factor(a_ref[:B])
+    for now in range(n):
+        at = first(now, n) + B
+        rest = range(now + 1, n)
+        panel = {i: mul_t(a_ref[at + (i - now - 1) * B : at + (i - now) * B], inv) for i in rest}
+        if now + 1 < n:
+            to = first(now + 1, n)
+            following = inverse_factor(a_ref[to : to + B] - mul_t(panel[now + 1], panel[now + 1]))
+        solved = mul_t(x_blocks[now], inv)
+        out_ref[:, now * B : now * B + B] = solved
+        for j in rest:
+            for i in range(j, n):
+                if i > now + 1:
+                    to = first(j, n) + (i - j) * B
+                    a_ref[to : to + B] -= mul_t(panel[i], panel[j])
+            x_blocks[j] -= mul_t(solved, panel[j])
+        if now + 1 < n:
+            inv = following
 
 
 def whiten(bit, mine, other, x, total):
@@ -105,7 +100,6 @@
         scratch_shapes=[
             pltpu.VMEM((2 * mine.shape[0], B), jnp.float32),
             pltpu.VMEM((n, x.shape[0], B), jnp.float32),
-            pltpu.VMEM((B, B), jnp.float32),
         ],
         compiler_params=pltpu.CompilerParams(vmem_limit_bytes=12 << 20),
         cost_estimate=pl.CostEstimate(flops=20_000_000_000, bytes_accessed=4_000_000, transcendentals=0),
@@ -142,10 +136,7 @@
 
 def cut_kernel(terms, order, at_ref, *refs):
     ins, outs, total_ref = refs[:terms], refs[terms:-1], refs[-1]
-    rows = ins[0].shape[0]
-    total_ref[:rows] = functools.reduce(lambda a, b: a + b, [r[...] for r in ins])
-    if rows < total_ref.shape[0]:
-        total_ref[rows:] = jnp.zeros((total_ref.shape[0] - rows, B), jnp.float32)
+    total_ref[...] = functools.reduce(lambda a, b: a + b, [r[...] for r in ins])
     size = outs[0].shape[0]
     for s, out in enumerate(outs):
         out[...] = total_ref[pl.ds(pl.multiple_of(order(at_ref[0], s) * size, 8), size)]
@@ -198,29 +189,30 @@
     return lax.axis_index(axis).reshape(1)
 
 
-def gram_sum(keep, send):
-    keep_rows = keep.shape[0]
-    x, y = index("x"), index("y")
-    pieces = cut(x, [keep, swapped(send, "core", 1)], 4, keep_rows, "cut_x")
-    terms = [pieces[0]] + [shifted(pieces[s], "x", s) for s in (1, 2, 3)]
-    rows = 384
-    for by in (1, 2, 4):
-        keep, send = cut((y // by) % 2, terms, 2, rows, "cut_y")
-        terms = [keep, swapped(send, "y", by)]
-        rows //= 2
-    mine = terms[0] + terms[1]
-    for by in (1, 2, 4):
-        mine = mine + swapped(mine, "z", by)
-    for by in (4, 2, 1):
-        other = swapped(mine, "y", by)
-        mine = place((y // by) % 2, [mine, other], "place_y")
-    mine = mine[: keep_rows // 4]
-    mine = place(x, [mine] + [shifted(mine, "x", s) for s in (1, 2, 3)], "place_x")
-    return mine, swapped(mine, "core", 1)
-
-
 def reduced(pieces, axis):
     return jnp.sum(lax.all_to_all(pieces, axis, 0, 0, tiled=True), axis=0)
+
+
+def spread(value, axis):
+    copies = jnp.broadcast_to(value[None], (lax.axis_size(axis), *value.shape))
+    return lax.all_to_all(copies, axis, 0, 0, tiled=True)
+
+
+def x_pieces(keep, send):
+    return cut(index("x"), [keep, swapped(send, "core", 1)], 4, keep.shape[0], "cut_x")
+
+
+def x_sum(pieces):
+    return functools.reduce(lambda a, b: a + b, [pieces[0]] + [shifted(pieces[s], "x", s) for s in (1, 2, 3)])
+
+
+def gram_sum(mine):
+    rows = mine.shape[0]
+    mine = reduced(mine.reshape(8, rows // 8, B), "y")
+    mine = jnp.sum(spread(mine, "z"), axis=0)
+    mine = spread(mine, "y").reshape(rows, B)
+    mine = place(index("x"), [mine] + [shifted(mine, "x", s) for s in (1, 2, 3)], "place_x")
+    return mine, swapped(mine, "core", 1)
 
 
 def body(embeddings, assignments):
@@ -231,7 +223,7 @@
     per_owner = CENTROIDS // owners
     n = width // B
     bit = index("core")
-    half, send = gram_halves(bit, embeddings)
+    pieces = x_pieces(*gram_halves(bit, embeddings))
 
     target = assignments // per_owner
     local = assignments % per_owner
@@ -246,8 +238,10 @@
     labels = jnp.sum(jnp.where(chosen, (local + 1)[None, :], 0), axis=1) - 1
     outgoing = outgoing.reshape(owners, CAP * width)
     labels = jnp.pad(labels.reshape(owners, CAP).astype(jnp.float32), ((0, 0), (0, B - CAP)))
-    packed = jnp.concatenate([outgoing, labels], axis=1).reshape(owners, CAP * n + 1, B)
-    packed = lax.all_to_all(packed, rows_axes, 0, 0, tiled=True).reshape(owners, CAP * width + B)
+    packed = jnp.concatenate([outgoing, labels], axis=1).reshape(owners, 1, CAP * width + B)
+    packed = lax.all_to_all(packed, rows_axes, 0, 0, tiled=True)
+    summed, packed = lax.optimization_barrier((x_sum(pieces), packed))
+    packed = packed.reshape(owners, CAP * width + B)
     incoming = packed[:, : CAP * width].reshape(owners * CAP, width)
     tags = packed[:, CAP * width : CAP * width + CAP].reshape(-1).astype(jnp.int32)
     member = (tags[None, :] == jnp.arange(per_owner, dtype=jnp.int32)[:, None]).astype(jnp.float32)
@@ -261,7 +255,7 @@
     sums = mine[: keep * n].reshape(keep, width)
     counts = mine[keep * n, :keep]
 
-    mine, other = gram_sum(half, send)
+    mine, other = gram_sum(summed)
     means = sums / jnp.maximum(counts, 1.0)[:, None]
     solved = whiten(bit, mine, other, jnp.concatenate([embeddings, means], axis=0), total)
     return solved[:rows_here], solved[rows_here:]

time: 170 us -> 145 us (0.85)
  starting transfers between devices: 101 us -> 63 us
  blocking collectives: 0 us -> 11.7 us
  waiting for transfers between devices: 27.3 us -> 32.1 us
  Pallas kernels: 31.6 us -> 27.2 us
    ppermute x11 -> x2, starting transfers between devices: 56.6 us -> 11.4 us  [swapped(): lax.ppermute(value, axis, [(i, i ^ by) for i in range(lax.axis_size(axis))])]
    all_to_all x1 -> x3, waiting for transfers between devices: 0.01 us -> 21.8 us  [the longest x2 15.2 us: spread(): return lax.all_to_all(copies, axis, 0, 0, tiled=True)]
    ppermute x11 -> x2, waiting for transfers between devices: 15.9 us -> 3.09 us  [swapped(): lax.ppermute(value, axis, [(i, i ^ by) for i in range(lax.axis_size(axis))])]
    all_to_all x0 -> x1, blocking collectives: none -> 11.7 us  [reduced(): return jnp.sum(lax.all_to_all(pieces, axis, 0, 0, tiled=True), axis=0)]
    all_to_all x1 -> x3, starting transfers between devices: 18.6 us -> 25.3 us  [the longest x1 18.6 us: body(): packed = lax.all_to_all(packed, rows_axes, 0, 0, tiled=True)]
    pallas_call x1, Pallas kernels: 30 us -> 25.7 us  [whiten(): pl.pallas_call(functools.partial(whiten_kernel, total, n), out_shape=jax....]
    ppermute x6, waiting for transfers between devices: 11.4 us -> 7.27 us  [shifted(): lax.ppermute(value, axis, [(i, (i + by) % size) for i in range(size)])]
  transfers between devices with their start and end apart: 19 -> 12, of which waited for: 14 -> 9; matrix products, arithmetic and copies ran while one was open for 2% -> 1% of each run, Pallas kernels for 1% -> 1%
where the time goes in v4:
time: 145 us; the launch traced here: 144 us
  starting transfers between devices  63 us (43%)
  waiting for transfers between devices  32.1 us (22%)
  Pallas kernels  27.2 us (19%)
  blocking collectives  11.7 us (8%)
  local copies, waits for them, and re-layouts  5.21 us (4%)
  other arithmetic  2.16 us (1%)
  matrix products  1.9 us (1%)
    pallas_call x1, Pallas kernels, whiten(): pl.pallas_call(functools.partial(whiten_kernel, total, n), out_shape=jax....  25.7 us
    ppermute x6, starting transfers between devices, shifted(): lax.ppermute(value, axis, [(i, (i + by) % size) for i in range(size)])  21.3 us
    all_to_all x1, starting transfers between devices, body(): packed = lax.all_to_all(packed, rows_axes, 0, 0, tiled=True)  18.6 us
    all_to_all x2, waiting for transfers between devices, spread(): return lax.all_to_all(copies, axis, 0, 0, tiled=True)  15.2 us
    all_to_all x1, blocking collectives, reduced(): return jnp.sum(lax.all_to_all(pieces, axis, 0, 0, tiled=True), axis=0)  11.7 us
    ppermute x2, starting transfers between devices, swapped(): lax.ppermute(value, axis, [(i, i ^ by) for i in range(lax.axis_size(axis))])  11.4 us
    ppermute x6, waiting for transfers between devices, shifted(): lax.ppermute(value, axis, [(i, (i + by) % size) for i in range(size)])  7.27 us
    all_to_all x2, starting transfers between devices, spread(): return lax.all_to_all(copies, axis, 0, 0, tiled=True)  6.78 us
  transfers between devices with their start and end apart: 12, of which 9 were waited for; matrix products, arithmetic and copies ran while one was open for 1% of the time, Pallas kernels for 1%

profile of v4, /device:TPU:1, one launch (start us, length us, event | category | flops | bytes accessed | tf_op | source)
XLA Modules:
  0.0 144.3 jit_solution(6816888631124633771)
XLA Ops:
  1.8 1.5 %fusion.1 = f32[256,768]{1,0:T(8,128)S(1)} fusion(f32[128,768]{1,0:T(8,128)} %x_ref.1, s32[128]{0:T(128)S(1)} %multiply_add_fusion), kind=kOutput, calls=%fused_computation.12 | convolution fusion | flops 302022656 | bytes 1180160 | tf_op jit(solution)/shard_map/dot_general | solution.py:235
  3.5 1.5 %reshape.66 = f32[128,1,1664]{2,1,0:T(1,128)} reshape(f32[128,1664]{1,0:T(8,128)S(1)} %select_maximum_fusion) | data formatting | bytes 1703936 | tf_op jit(solution)/shard_map/reshape | solution.py:241
  5.0 18.6 %all-to-all-start = ((f32[128,1,1664]{2,1,0:T(1,128)}), f32[128,1,1664]{2,1,0:T(1,128)S(1)}, u32[]{:S(2)}, u32[]{:S(2)}) async-start(f32[128,1,1664]{2,1,0:T(1,128)} %reshape.66), calls=%async_computation | async-start | bytes 1703936 | tf_op jit(solution)/shard_map/all_to_all | solution.py:242
  23.6 1.4 gram.1
  25.0 2.8 %collective-permute-start = (f32[1344,128]{1,0:T(8,128)S(1)}, f32[1344,128]{1,0:T(8,128)S(1)}, u32[]{:S(2)}, u32[]{:S(2)}) collective-permute-start(f32[1344,128]{1,0:T(8,128)S(1)} %get-tuple-element.11), channel_id=1, source_target_pairs={{0,4},{4,0},{1,5},{5,1},{2,6},{6,2},{3,7},{7,3},{8,12},{12,8},{9,1... | collective-permute-start | bytes 2064392 | tf_op jit(solution)/shard_map/ppermute | solution.py:185
  27.8 1.7 %collective-permute-done.refs_1_ = f32[1344,128]{1,0:T(8,128)S(1)} collective-permute-done((f32[1344,128]{1,0:T(8,128)S(1)}, f32[1344,128]{1,0:T(8,128)S(1)}, u32[]{:S(2)}, u32[]{:S(2)}) %collective-permute-start) | collective-permute-done | bytes 688160 | tf_op jit(solution)/shard_map/ppermute | solution.py:185
  29.7 3.1 %collective-permute-start.1 = (f32[336,128]{1,0:T(8,128)S(1)}, f32[336,128]{1,0:T(8,128)S(1)}, u32[]{:S(2)}, u32[]{:S(2)}) collective-permute-start(f32[336,128]{1,0:T(8,128)S(1)} %get-tuple-element.13), channel_id=1, source_target_pairs={{0,1},{1,2},{2,3},{3,0},{4,5},{5,6},{6,7},{7,4},{8,9},{9,10},{10,1... | collective-permute-start | bytes 516104 | tf_op jit(solution)/shard_map/ppermute | solution.py:181
  32.8 4.4 %collective-permute-start.2 = (f32[336,128]{1,0:T(8,128)S(1)}, f32[336,128]{1,0:T(8,128)S(1)}, u32[]{:S(2)}, u32[]{:S(2)}) collective-permute-start(f32[336,128]{1,0:T(8,128)S(1)} %get-tuple-element.14), channel_id=1, source_target_pairs={{0,2},{1,3},{2,0},{3,1},{4,6},{5,7},{6,4},{7,5},{8,10},{9,11},{10,... | collective-permute-start | bytes 516104 | tf_op jit(solution)/shard_map/ppermute | solution.py:181
  37.2 3.1 %collective-permute-start.3 = (f32[336,128]{1,0:T(8,128)S(1)}, f32[336,128]{1,0:T(8,128)S(1)}, u32[]{:S(2)}, u32[]{:S(2)}) collective-permute-start(f32[336,128]{1,0:T(8,128)S(1)} %get-tuple-element.15), channel_id=1, source_target_pairs={{0,3},{1,0},{2,1},{3,2},{4,7},{5,4},{6,5},{7,6},{8,11},{9,8},{10,9... | collective-permute-start | bytes 516104 | tf_op jit(solution)/shard_map/ppermute | solution.py:181
  40.3 2.8 %collective-permute-done.2 = f32[336,128]{1,0:T(8,128)S(1)} collective-permute-done((f32[336,128]{1,0:T(8,128)S(1)}, f32[336,128]{1,0:T(8,128)S(1)}, u32[]{:S(2)}, u32[]{:S(2)}) %collective-permute-start.2) | collective-permute-done | bytes 172064 | tf_op jit(solution)/shard_map/ppermute | solution.py:181
  44.1 6.5 %all-to-all-done = f32[128,1,1664]{2,1,0:T(1,128)S(1)} async-done(((f32[128,1,1664]{2,1,0:T(1,128)}), f32[128,1,1664]{2,1,0:T(1,128)S(1)}, u32[]{:S(2)}, u32[]{:S(2)}) %all-to-all-start) | async-done | bytes 852000 | tf_op jit(solution)/shard_map/all_to_all | solution.py:242
  50.6 11.7 %all_to_all.25 = f32[8,42,128]{2,1,0:T(8,128)S(1)} all-to-all(f32[8,42,128]{2,1,0:T(8,128)S(1)} %reshape.67), channel_id=1, replica_groups=mesh['z'=8,'y'=8,'core'=2,'x'=4] {'y'}, dimensions={0} | all-to-all | bytes 344064 | tf_op jit(solution)/shard_map/all_to_all | solution.py:193
  63.0 3.4 %all-to-all-start.2 = ((f32[8,42,128]{2,1,0:T(8,128)}), f32[8,42,128]{2,1,0:T(8,128)S(1)}, u32[]{:S(2)}, u32[]{:S(2)}) async-start(f32[8,42,128]{2,1,0:T(8,128)} %broadcast_in_dim.18), calls=%async_computation.2 | async-start | bytes 393216 | tf_op jit(solution)/shard_map/all_to_all | solution.py:198
  66.9 8.1 %all-to-all-done.2 = f32[8,42,128]{2,1,0:T(8,128)S(1)} async-done(((f32[8,42,128]{2,1,0:T(8,128)}), f32[8,42,128]{2,1,0:T(8,128)S(1)}, u32[]{:S(2)}, u32[]{:S(2)}) %all-to-all-start.2) | async-done | bytes 172064 | tf_op jit(solution)/shard_map/all_to_all | solution.py:198
  75.7 3.4 %all-to-all-start.3 = ((f32[8,42,128]{2,1,0:T(8,128)}), f32[8,42,128]{2,1,0:T(8,128)S(1)}, u32[]{:S(2)}, u32[]{:S(2)}) async-start(f32[8,42,128]{2,1,0:T(8,128)} %broadcast_in_dim.19), calls=%async_computation.3 | async-start | bytes 393216 | tf_op jit(solution)/shard_map/all_to_all | solution.py:198
  80.6 7.1 %all-to-all-done.3 = f32[8,42,128]{2,1,0:T(8,128)S(1)} async-done(((f32[8,42,128]{2,1,0:T(8,128)}), f32[8,42,128]{2,1,0:T(8,128)S(1)}, u32[]{:S(2)}, u32[]{:S(2)}) %all-to-all-start.3) | async-done | bytes 172064 | tf_op jit(solution)/shard_map/all_to_all | solution.py:198
  87.6 5.0 %all-to-all-start.4 = ((f32[4,200,128]{2,1,0:T(8,128)}), f32[4,200,128]{2,1,0:T(8,128)S(1)}, u32[]{:S(2)}, u32[]{:S(2)}) async-start(f32[4,200,128]{2,1,0:T(8,128)} %select_maximum_fusion.1), calls=%async_computation.4 | async-start | bytes 819200 | tf_op jit(solution)/shard_map/all_to_all | solution.py:193
  92.7 4.1 %collective-permute-start.4 = (f32[336,128]{1,0:T(8,128)S(1)}, f32[336,128]{1,0:T(8,128)S(1)}, u32[]{:S(2)}, u32[]{:S(2)}) collective-permute-start(f32[336,128]{1,0:T(8,128)S(1)} %reshape.68.refs_0_), channel_id=1, source_target_pairs={{0,1},{1,2},{2,3},{3,0},{4,5},{5,6},{6,7},{7,4},{8,9},{9,10},{10,1... | collective-permute-start | bytes 516104 | tf_op jit(solution)/shard_map/ppermute | solution.py:181
  96.8 3.6 %collective-permute-start.5 = (f32[336,128]{1,0:T(8,128)S(1)}, f32[336,128]{1,0:T(8,128)S(1)}, u32[]{:S(2)}, u32[]{:S(2)}) collective-permute-start(f32[336,128]{1,0:T(8,128)S(1)} %reshape.68.refs_0_), channel_id=1, source_target_pairs={{0,2},{1,3},{2,0},{3,1},{4,6},{5,7},{6,4},{7,5},{8,10},{9,11},{10,... | collective-permute-start | bytes 516104 | tf_op jit(solution)/shard_map/ppermute | solution.py:181
  100.4 3.1 %collective-permute-start.6 = (f32[336,128]{1,0:T(8,128)S(1)}, f32[336,128]{1,0:T(8,128)S(1)}, u32[]{:S(2)}, u32[]{:S(2)}) collective-permute-start(f32[336,128]{1,0:T(8,128)S(1)} %reshape.68.refs_0_), channel_id=1, source_target_pairs={{0,3},{1,0},{2,1},{3,2},{4,7},{5,4},{6,5},{7,6},{8,11},{9,8},{10,9... | collective-permute-start | bytes 516104 | tf_op jit(solution)/shard_map/ppermute | solution.py:181
  103.5 3.0 %collective-permute-done.5.refs_2_ = f32[336,128]{1,0:T(8,128)S(1)} collective-permute-done((f32[336,128]{1,0:T(8,128)S(1)}, f32[336,128]{1,0:T(8,128)S(1)}, u32[]{:S(2)}, u32[]{:S(2)}) %collective-permute-start.5) | collective-permute-done | bytes 172064 | tf_op jit(solution)/shard_map/ppermute | solution.py:181
  107.1 8.6 %collective-permute-start.7 = (f32[1344,128]{1,0:T(8,128)S(1)}, f32[1344,128]{1,0:T(8,128)S(1)}, u32[]{:S(2)}, u32[]{:S(2)}) collective-permute-start(f32[1344,128]{1,0:T(8,128)S(1)} %place_x.1.mine_ref), channel_id=1, source_target_pairs={{0,4},{4,0},{1,5},{5,1},{2,6},{6,2},{3,7},{7,3},{8,12},{12,8},{9,1... | collective-permute-start | bytes 2064392 | tf_op jit(solution)/shard_map/ppermute | solution.py:185
  115.9 1.3 collective-permute-done.7.other_ref
  117.2 25.7 %whiten.1 = f32[160,768]{1,0:T(8,128)S(1)} custom-call(s32[1]{0:T(128)} %bitcast.bit_ref, f32[1344,128]{1,0:T(8,128)S(1)} %place_x.1.mine_ref, f32[1344,128]{1,0:T(8,128)S(1)} %collective-permute-done.7.other_ref, f32[160,768]{1,0:T(8,128)S(1)} %pad_maximum_fusion.x_ref), custom_call_target="tpu_custom_call" | custom-call | flops 20000000000 | bytes 4000000 | tf_op jit(solution)/shard_map/whiten/pallas_call | solution.py:95
  (42 shorter events, 7.9 us)
Async XLA Ops:
  5.0 18.6 %copy-start = (f32[128,768]{1,0:T(8,128)S(1)}, f32[128,768]{1,0:T(8,128)}, u32[]{:S(2)}) copy-start(f32[128,768]{1,0:T(8,128)} %x_ref.1) | copy-start | bytes 1179652
  5.0 45.6 %all-to-all-start = ((f32[128,1,1664]{2,1,0:T(1,128)}), f32[128,1,1664]{2,1,0:T(1,128)S(1)}, u32[]{:S(2)}, u32[]{:S(2)}) async-start(f32[128,1,1664]{2,1,0:T(1,128)} %reshape.66), calls=%async_computation | async-start | bytes 1703936 | tf_op jit(solution)/shard_map/all_to_all | solution.py:242
  25.0 4.6 %collective-permute-start = (f32[1344,128]{1,0:T(8,128)S(1)}, f32[1344,128]{1,0:T(8,128)S(1)}, u32[]{:S(2)}, u32[]{:S(2)}) collective-permute-start(f32[1344,128]{1,0:T(8,128)S(1)} %get-tuple-element.11), channel_id=1, source_target_pairs={{0,4},{4,0},{1,5},{5,1},{2,6},{6,2},{3,7},{7,3},{8,12},{12,8},{9,1... | collective-permute-start | bytes 2064392 | tf_op jit(solution)/shard_map/ppermute | solution.py:185
  29.7 10.6 %collective-permute-start.1 = (f32[336,128]{1,0:T(8,128)S(1)}, f32[336,128]{1,0:T(8,128)S(1)}, u32[]{:S(2)}, u32[]{:S(2)}) collective-permute-start(f32[336,128]{1,0:T(8,128)S(1)} %get-tuple-element.13), channel_id=1, source_target_pairs={{0,1},{1,2},{2,3},{3,0},{4,5},{5,6},{6,7},{7,4},{8,9},{9,10},{10,1... | collective-permute-start | bytes 516104 | tf_op jit(solution)/shard_map/ppermute | solution.py:181
  32.8 10.2 %collective-permute-start.2 = (f32[336,128]{1,0:T(8,128)S(1)}, f32[336,128]{1,0:T(8,128)S(1)}, u32[]{:S(2)}, u32[]{:S(2)}) collective-permute-start(f32[336,128]{1,0:T(8,128)S(1)} %get-tuple-element.14), channel_id=1, source_target_pairs={{0,2},{1,3},{2,0},{3,1},{4,6},{5,7},{6,4},{7,5},{8,10},{9,11},{10,... | collective-permute-start | bytes 516104 | tf_op jit(solution)/shard_map/ppermute | solution.py:181
  37.2 6.8 %collective-permute-start.3 = (f32[336,128]{1,0:T(8,128)S(1)}, f32[336,128]{1,0:T(8,128)S(1)}, u32[]{:S(2)}, u32[]{:S(2)}) collective-permute-start(f32[336,128]{1,0:T(8,128)S(1)} %get-tuple-element.15), channel_id=1, source_target_pairs={{0,3},{1,0},{2,1},{3,2},{4,7},{5,4},{6,5},{7,6},{8,11},{9,8},{10,9... | collective-permute-start | bytes 516104 | tf_op jit(solution)/shard_map/ppermute | solution.py:181
  63.0 12.0 %all-to-all-start.2 = ((f32[8,42,128]{2,1,0:T(8,128)}), f32[8,42,128]{2,1,0:T(8,128)S(1)}, u32[]{:S(2)}, u32[]{:S(2)}) async-start(f32[8,42,128]{2,1,0:T(8,128)} %broadcast_in_dim.18), calls=%async_computation.2 | async-start | bytes 393216 | tf_op jit(solution)/shard_map/all_to_all | solution.py:198
  75.7 11.9 %all-to-all-start.3 = ((f32[8,42,128]{2,1,0:T(8,128)}), f32[8,42,128]{2,1,0:T(8,128)S(1)}, u32[]{:S(2)}, u32[]{:S(2)}) async-start(f32[8,42,128]{2,1,0:T(8,128)} %broadcast_in_dim.19), calls=%async_computation.3 | async-start | bytes 393216 | tf_op jit(solution)/shard_map/all_to_all | solution.py:198
  87.6 28.0 %all-to-all-start.4 = ((f32[4,200,128]{2,1,0:T(8,128)}), f32[4,200,128]{2,1,0:T(8,128)S(1)}, u32[]{:S(2)}, u32[]{:S(2)}) async-start(f32[4,200,128]{2,1,0:T(8,128)} %select_maximum_fusion.1), calls=%async_computation.4 | async-start | bytes 819200 | tf_op jit(solution)/shard_map/all_to_all | solution.py:193
  92.7 10.8 %collective-permute-start.4 = (f32[336,128]{1,0:T(8,128)S(1)}, f32[336,128]{1,0:T(8,128)S(1)}, u32[]{:S(2)}, u32[]{:S(2)}) collective-permute-start(f32[336,128]{1,0:T(8,128)S(1)} %reshape.68.refs_0_), channel_id=1, source_target_pairs={{0,1},{1,2},{2,3},{3,0},{4,5},{5,6},{6,7},{7,4},{8,9},{9,10},{10,1... | collective-permute-start | bytes 516104 | tf_op jit(solution)/shard_map/ppermute | solution.py:181
  96.8 9.7 %collective-permute-start.5 = (f32[336,128]{1,0:T(8,128)S(1)}, f32[336,128]{1,0:T(8,128)S(1)}, u32[]{:S(2)}, u32[]{:S(2)}) collective-permute-start(f32[336,128]{1,0:T(8,128)S(1)} %reshape.68.refs_0_), channel_id=1, source_target_pairs={{0,2},{1,3},{2,0},{3,1},{4,6},{5,7},{6,4},{7,5},{8,10},{9,11},{10,... | collective-permute-start | bytes 516104 | tf_op jit(solution)/shard_map/ppermute | solution.py:181
  100.4 6.6 %collective-permute-start.6 = (f32[336,128]{1,0:T(8,128)S(1)}, f32[336,128]{1,0:T(8,128)S(1)}, u32[]{:S(2)}, u32[]{:S(2)}) collective-permute-start(f32[336,128]{1,0:T(8,128)S(1)} %reshape.68.refs_0_), channel_id=1, source_target_pairs={{0,3},{1,0},{2,1},{3,2},{4,7},{5,4},{6,5},{7,6},{8,11},{9,8},{10,9... | collective-permute-start | bytes 516104 | tf_op jit(solution)/shard_map/ppermute | solution.py:181
  107.1 10.1 %collective-permute-start.7 = (f32[1344,128]{1,0:T(8,128)S(1)}, f32[1344,128]{1,0:T(8,128)S(1)}, u32[]{:S(2)}, u32[]{:S(2)}) collective-permute-start(f32[1344,128]{1,0:T(8,128)S(1)} %place_x.1.mine_ref), channel_id=1, source_target_pairs={{0,4},{4,0},{1,5},{5,1},{2,6},{6,2},{3,7},{7,3},{8,12},{12,8},{9,1... | collective-permute-start | bytes 2064392 | tf_op jit(solution)/shard_map/ppermute | solution.py:185

commit v5 on v4

--- a/solution.py
+++ b/solution.py
@@ -28,27 +28,48 @@
     sub = lax.broadcasted_iota(jnp.int32, (8, B), 0)
     for g in range(groups):
         done = (lane >= 8 * g) & (lane < 8 * g + 8)
-        cols = [[jnp.broadcast_to(t[:, 8 * g + k : 8 * g + k + 1], (8, B)) for k in range(8)] for t in tiles[g:]]
+
+        def columns(tile):
+            return [jnp.broadcast_to(tile[:, 8 * g + k : 8 * g + k + 1], (8, B)) for k in range(8)]
+
+        own = columns(tiles[g])
+        s = [[own[p][k : k + 1] for p in range(k + 1)] for k in range(8)]
+        mult, recip = {}, []
+        for p in range(0, 8, 2):
+            a, e, c = s[p][p], s[p + 1][p], s[p + 1][p + 1]
+            det = a * c - e * e
+            r0, rd = 1.0 / a, 1.0 / det
+            r1, both = a * rd, r0 * rd
+            mult[p + 1, p] = m = e * r0
+            second = {q: s[q][p + 1] - m * s[q][p] for q in range(p + 2, 8)}
+            cross = {q: a * s[q][p + 1] - e * s[q][p] for q in range(p + 2, min(p + 4, 8))}
+            for k in range(p + 2, 8):
+                mult[k, p], mult[k, p + 1] = m0, m1 = s[k][p] * r0, second[k] * r1
+                for q in range(k, 8):
+                    if q in cross:
+                        s[q][k] = (s[q][k] - (s[k][p] * s[q][p]) * r0) - (cross[k] * cross[q]) * both
+                    else:
+                        s[q][k] = (s[q][k] - m0 * s[q][p]) - m1 * second[q]
+            s[p + 1][p + 1] = det * r0
+            recip += [r0, r1]
         here = jnp.where(lane == sub + 8 * g, 1.0, jnp.where(done, 0.0, tiles[g]))
-        rows = [here[k : k + 1] for k in range(8)]
-        small = [[cols[0][p][k : k + 1] for p in range(8)] for k in range(8)]
-        scaled = []
+        rows = [jnp.broadcast_to(here[k : k + 1], (8, B)) for k in range(8)]
         for p in range(8):
-            r = 1.0 / small[p][p]
             for k in range(p + 1, 8):
-                m = small[k][p] * r
-                for q in range(k, 8):
-                    small[q][k] = small[q][k] - m * small[q][p]
-                rows[k] = rows[k] - m * rows[p]
-                for c in cols[1:]:
-                    c[k] = c[k] - m * c[p]
-            scaled.append(rows[p] * r)
+                rows[k] = rows[k] - mult[k, p] * rows[p]
+        scaled = [rows[p] * recip[p] for p in range(8)]
         for i in range(g + 1, groups):
             new = jnp.where(done, 0.0, tiles[i])
+            below = columns(tiles[i])
             for p in range(8):
-                new = new - cols[i - g][p] * scaled[p]
+                for k in range(p + 1, 8):
+                    below[k] = below[k] - mult[k, p] * below[p]
+                new = new - below[p] * scaled[p]
             tiles[i] = new
-        tiles[g] = jnp.concatenate([rows[k] * lax.rsqrt(small[k][k]) for k in range(8)], axis=0)
+        final = rows[0] * lax.rsqrt(s[0][0])
+        for k in range(1, 8):
+            final = jnp.where(sub == k, rows[k] * lax.rsqrt(s[k][k]), final)
+        tiles[g] = final
     row = lax.broadcasted_iota(jnp.int32, (B, B), 0)
     col = lax.broadcasted_iota(jnp.int32, (B, B), 1)
     return jnp.where(col <= row, jnp.concatenate(tiles, axis=0), 0.0)
@@ -58,7 +79,31 @@
     return (j * n - j * (j - 1) // 2) * B
 
 
-def whiten_kernel(total, n, bit_ref, mine_ref, other_ref, x_ref, out_ref, a_ref, x_blocks):
+def block(i, j, n, base=0):
+    at = first(j, n) - first(base, n) + (i - j) * B
+    return slice(at, at + B)
+
+
+def steps(which, n, inv, load, store, x_blocks, panel_ref, inv_ref):
+    base = which[0]
+    for now in which:
+        rest = range(now + 1, n)
+        panel = {i: mul_t(load(now, i, now), inv) for i in rest}
+        if rest:
+            following = inverse_factor(load(now, now + 1, now + 1) - mul_t(panel[now + 1], panel[now + 1]))
+        x_blocks[now] = solved = mul_t(x_blocks[now], inv)
+        for j in rest:
+            at = (j - now - 1) * B + sum(n - 1 - t for t in range(base, now)) * B
+            panel_ref[at : at + B] = panel[j]
+            for i in range(j, n):
+                if i > now + 1:
+                    store(now, i, j, load(now, i, j) - mul_t(panel[i], panel[j]))
+            x_blocks[j] -= mul_t(solved, panel[j])
+        if rest:
+            inv_ref[now + 1 - base] = inv = following
+
+
+def early_kernel(total, n, cut_at, bit_ref, mine_ref, other_ref, x_ref, panel_ref, inv_ref, left_ref, x_blocks, a_ref):
     row = lax.broadcasted_iota(jnp.int32, (B, B), 0)
     col = lax.broadcasted_iota(jnp.int32, (B, B), 1)
     half = mine_ref.shape[0]
@@ -66,45 +111,117 @@
     a_ref[pl.ds(pl.multiple_of(bit * half, 8), half)] = mine_ref[...] * (1.0 / total)
     a_ref[pl.ds(pl.multiple_of((1 - bit) * half, 8), half)] = other_ref[...] * (1.0 / total)
     for j in range(n):
-        at = first(j, n)
-        a_ref[at : at + B] += jnp.where(row == col, 1e-05, 0.0)
+        a_ref[block(j, j, n)] += jnp.where(row == col, 1e-05, 0.0)
         x_blocks[j] = x_ref[:, j * B : j * B + B]
 
-    inv = inverse_factor(a_ref[:B])
+    def load(now, i, j):
+        return a_ref[block(i, j, n)]
+
+    def store(now, i, j, value):
+        if now + 1 < cut_at:
+            a_ref[block(i, j, n)] = value
+        else:
+            left_ref[block(i, j, n, cut_at)] = value
+
+    inv_ref[0] = inv = inverse_factor(load(0, 0, 0))
+    steps(range(cut_at), n, inv, load, store, x_blocks, panel_ref, inv_ref)
+
+
+def late_kernel(n, cut_at, inv_in, left_ref, x_in, out_ref, panel_ref, inv_ref, a_ref, x_blocks):
+    x_blocks[...] = x_in[...]
+
+    def load(now, i, j):
+        return (left_ref if now == cut_at else a_ref)[block(i, j, n, cut_at)]
+
+    def store(now, i, j, value):
+        a_ref[block(i, j, n, cut_at)] = value
+
+    inv_ref[0] = inv = inv_in[cut_at]
+    steps(range(cut_at, n), n, inv, load, store, x_blocks, panel_ref, inv_ref)
+    for j in range(n):
+        out_ref[:, j * B : j * B + B] = x_blocks[j]
+
+
+def means_kernel(n, cut_at, got_ref, early_panel, early_inv, late_panel, late_inv, out_ref):
+    peers = got_ref.shape[0]
+    keep = out_ref.shape[0]
+
+    def gathered(j):
+        return functools.reduce(lambda a, b: a + b, [got_ref[q, j * keep : j * keep + keep] for q in range(peers)])
+
+    counts = jnp.maximum(gathered(n), 1.0)
+    x = [gathered(j) / counts for j in range(n)]
+    at = [0, 0]
     for now in range(n):
-        at = first(now, n) + B
-        rest = range(now + 1, n)
-        panel = {i: mul_t(a_ref[at + (i - now - 1) * B : at + (i - now) * B], inv) for i in rest}
-        if now + 1 < n:
-            to = first(now + 1, n)
-            following = inverse_factor(a_ref[to : to + B] - mul_t(panel[now + 1], panel[now + 1]))
-        solved = mul_t(x_blocks[now], inv)
-        out_ref[:, now * B : now * B + B] = solved
-        for j in rest:
-            for i in range(j, n):
-                if i > now + 1:
-                    to = first(j, n) + (i - j) * B
-                    a_ref[to : to + B] -= mul_t(panel[i], panel[j])
-            x_blocks[j] -= mul_t(solved, panel[j])
-        if now + 1 < n:
-            inv = following
-
-
-def whiten(bit, mine, other, x, total):
+        late = int(now >= cut_at)
+        inv = late_inv[now - cut_at] if late else early_inv[now]
+        x[now] = mul_t(x[now], inv)
+        out_ref[:, now * B : now * B + B] = x[now]
+        for j in range(now + 1, n):
+            panel = (early_panel, late_panel)[late][at[late] : at[late] + B]
+            at[late] += B
+            x[j] = x[j] - mul_t(x[now], panel)
+
+
+def f32(*shape):
+    return jax.ShapeDtypeStruct(shape, jnp.float32)
+
+
+def local_call(kernel, outs, ins, name, scratch=(), limit=12, flops=10_000_000_000, scalars=0):
+    return pl.pallas_call(
+        kernel,
+        out_shape=outs,
+        in_specs=[SCALAR] * scalars + [VMEM] * (len(ins) - scalars),
+        out_specs=[VMEM] * len(outs),
+        scratch_shapes=[pltpu.VMEM(shape, jnp.float32) for shape in scratch],
+        compiler_params=pltpu.CompilerParams(vmem_limit_bytes=limit << 20),
+        cost_estimate=pl.CostEstimate(flops=flops, bytes_accessed=4_000_000, transcendentals=0),
+        name=name,
+    )(*ins)
+
+
+def early(bit, mine, other, x, total, cut_at):
     n = x.shape[1] // B
-    return pl.pallas_call(
-        functools.partial(whiten_kernel, total, n),
-        out_shape=jax.ShapeDtypeStruct(x.shape, jnp.float32),
-        in_specs=[SCALAR, VMEM, VMEM, VMEM],
-        out_specs=VMEM,
-        scratch_shapes=[
-            pltpu.VMEM((2 * mine.shape[0], B), jnp.float32),
-            pltpu.VMEM((n, x.shape[0], B), jnp.float32),
-        ],
-        compiler_params=pltpu.CompilerParams(vmem_limit_bytes=12 << 20),
-        cost_estimate=pl.CostEstimate(flops=20_000_000_000, bytes_accessed=4_000_000, transcendentals=0),
-        name="whiten",
-    )(bit, mine, other, x)
+    rows = first(n, n)
+    panels = sum(n - 1 - t for t in range(cut_at)) * B
+    outs = [f32(panels, B), f32(cut_at + 1, B, B), f32(rows - first(cut_at, n), B), f32(n, x.shape[0], B)]
+    kernel = functools.partial(early_kernel, total, n, cut_at)
+    return local_call(kernel, outs, [bit, mine, other, x], "early", [(rows, B)], scalars=1)
+
+
+def late(inv, left, x_blocks, cut_at):
+    n, rows, _ = x_blocks.shape
+    panels = sum(n - 1 - t for t in range(cut_at, n)) * B
+    outs = [f32(rows, n * B), f32(panels, B), f32(n - cut_at, B, B)]
+    kernel = functools.partial(late_kernel, n, cut_at)
+    return local_call(kernel, outs, [inv, left, x_blocks], "late", [left.shape, x_blocks.shape])
+
+
+def sums_kernel(cap, n, groups, packed_ref, out_ref):
+    rows = packed_ref.shape[0]
+    per_owner = B
+    keep = per_owner // groups
+    width = n * B
+    ids = lax.broadcasted_iota(jnp.int32, (rows, per_owner), 1).astype(jnp.float32)
+    tn = (((0,), (0,)), ((), ()))
+    members = []
+    for c in range(cap):
+        tag = packed_ref[:, cap * width + c : cap * width + c + 1]
+        members.append(jnp.where(tag == ids, 1.0, 0.0))
+
+    def summed(values):
+        return functools.reduce(
+            lambda a, b: a + b,
+            [lax.dot_general(m, v, tn, precision=HI, preferred_element_type=jnp.float32) for m, v in zip(members, values)],
+        )
+
+    for j in range(n + 1):
+        if j < n:
+            part = summed([packed_ref[:, c * width + j * B : c * width + j * B + B] for c in range(cap)])
+        else:
+            part = summed([jnp.ones((rows, B), jnp.float32)] * cap)
+        for q in range(groups):
+            out_ref[q, j * keep : j * keep + keep] = part[q * keep : q * keep + keep]
 
 
 def gram_kernel(n, bit_ref, x_ref, keep_ref, send_ref, all_ref):
@@ -206,13 +323,16 @@
     return functools.reduce(lambda a, b: a + b, [pieces[0]] + [shifted(pieces[s], "x", s) for s in (1, 2, 3)])
 
 
-def gram_sum(mine):
+def gram_sum(mine, packed):
     rows = mine.shape[0]
     mine = reduced(mine.reshape(8, rows // 8, B), "y")
     mine = jnp.sum(spread(mine, "z"), axis=0)
     mine = spread(mine, "y").reshape(rows, B)
-    mine = place(index("x"), [mine] + [shifted(mine, "x", s) for s in (1, 2, 3)], "place_x")
-    return mine, swapped(mine, "core", 1)
+    parts = [mine] + [shifted(mine, "x", s) for s in (1, 2, 3)]
+    *parts[:2], packed = lax.optimization_barrier((*parts[:2], packed))
+    packed = lax.all_to_all(packed, ("z", "y", "core"), 0, 0, tiled=True)
+    mine = place(index("x"), parts, "place_x")
+    return mine, swapped(mine, "core", 1), packed
 
 
 def body(embeddings, assignments):
@@ -239,26 +359,23 @@
     outgoing = outgoing.reshape(owners, CAP * width)
     labels = jnp.pad(labels.reshape(owners, CAP).astype(jnp.float32), ((0, 0), (0, B - CAP)))
     packed = jnp.concatenate([outgoing, labels], axis=1).reshape(owners, 1, CAP * width + B)
-    packed = lax.all_to_all(packed, rows_axes, 0, 0, tiled=True)
     summed, packed = lax.optimization_barrier((x_sum(pieces), packed))
-    packed = packed.reshape(owners, CAP * width + B)
-    incoming = packed[:, : CAP * width].reshape(owners * CAP, width)
-    tags = packed[:, CAP * width : CAP * width + CAP].reshape(-1).astype(jnp.int32)
-    member = (tags[None, :] == jnp.arange(per_owner, dtype=jnp.int32)[:, None]).astype(jnp.float32)
-    sums = jnp.dot(member, incoming, precision=lax.Precision.HIGHEST, preferred_element_type=jnp.float32)
-    counts = jnp.sum(member, axis=1)
+    mine, other, packed = gram_sum(summed, packed)
+    cut_at = 2
+    early_panel, early_inv, left, x_blocks = early(bit, mine, other, embeddings, total, cut_at)
+    packed, early_inv = lax.optimization_barrier((packed, early_inv))
     groups = lax.axis_size("x")
     keep = per_owner // groups
-    sums = sums.reshape(groups, keep * n, B)
-    counts = jnp.pad(counts.reshape(groups, 1, keep), ((0, 0), (0, 7), (0, B - keep)))
-    mine = reduced(jnp.concatenate([sums, counts], axis=1), "x")
-    sums = mine[: keep * n].reshape(keep, width)
-    counts = mine[keep * n, :keep]
-
-    mine, other = gram_sum(summed)
-    means = sums / jnp.maximum(counts, 1.0)[:, None]
-    solved = whiten(bit, mine, other, jnp.concatenate([embeddings, means], axis=0), total)
-    return solved[:rows_here], solved[rows_here:]
+    packed = packed.reshape(owners, CAP * width + B)
+    kernel = functools.partial(sums_kernel, CAP, n, groups)
+    [sums] = local_call(kernel, [f32(groups, (n + 1) * keep, B)], [packed], "sums", flops=400_000_000)
+    sums = lax.all_to_all(sums, "x", 0, 0, tiled=True)
+    whitened, late_panel, late_inv = late(early_inv, left, x_blocks, cut_at)
+    sums, late_inv = lax.optimization_barrier((sums, late_inv))
+    kernel = functools.partial(means_kernel, n, cut_at)
+    panels = [sums, early_panel, early_inv, late_panel, late_inv]
+    [means] = local_call(kernel, [f32(keep, width)], panels, "means", flops=400_000_000)
+    return whitened, means
 
 
 def solution(mesh):

time: 145 us -> 141 us (0.972)
  blocking collectives: 11.7 us -> 39.2 us
  starting transfers between devices: 63 us -> 46.7 us
  waiting for transfers between devices: 32.1 us -> 16.6 us
  Pallas kernels: 27.2 us -> 31.4 us
  other arithmetic: 2.16 us -> 0.45 us
    all_to_all x0 -> x2, blocking collectives: none -> 28.2 us  [spread(): return lax.all_to_all(copies, axis, 0, 0, tiled=True)]
    all_to_all x4 -> x2, starting transfers between devices: 30.4 us -> 15.1 us  [the longest x1 11.4 us: gram_sum(): packed = lax.all_to_all(packed, ('z', 'y', 'core'), 0, 0, tiled=True)]
    all_to_all x4 -> x2, waiting for transfers between devices: 21.8 us -> 10.1 us  [the longest x1 10.1 us: gram_sum(): packed = lax.all_to_all(packed, ('z', 'y', 'core'), 0, 0, tiled=True)]
    pallas_call x1 -> x4, Pallas kernels: 25.7 us -> 29.8 us  [local_call(): pl.pallas_call(kernel, out_shape=outs, in_specs=[SCALAR] * scalars + [VME...]
    ppermute x6, waiting for transfers between devices: 7.27 us -> 4.93 us  [shifted(): lax.ppermute(value, axis, [(i, (i + by) % size) for i in range(size)])]
    unnamed x3 -> x9, local copies, waits for them, and re-layouts: 0.06 us -> 2.21 us
    ppermute x6, starting transfers between devices: 21.3 us -> 19.7 us  [shifted(): lax.ppermute(value, axis, [(i, (i + by) % size) for i in range(size)])]
    ppermute x2, waiting for transfers between devices: 3.09 us -> 1.57 us  [swapped(): lax.ppermute(value, axis, [(i, i ^ by) for i in range(lax.axis_size(axis))])]
  transfers between devices with their start and end apart: 12 -> 10, of which waited for: 9 -> 4; matrix products, arithmetic and copies ran while one was open for 1% -> 3% of each run, Pallas kernels for 1% -> 17%
where the time goes in v5:
time: 141 us
  starting transfers between devices  46.7 us (33%)
  blocking collectives  39.2 us (28%)
  Pallas kernels  31.4 us (22%)
  waiting for transfers between devices  16.6 us (12%)
  local copies, waits for them, and re-layouts  5.03 us (4%)
    pallas_call x4, Pallas kernels, local_call(): pl.pallas_call(kernel, out_shape=outs, in_specs=[SCALAR] * scalars + [VME...  29.8 us
    all_to_all x2, blocking collectives, spread(): return lax.all_to_all(copies, axis, 0, 0, tiled=True)  28.2 us
    ppermute x6, starting transfers between devices, shifted(): lax.ppermute(value, axis, [(i, (i + by) % size) for i in range(size)])  19.7 us
    ppermute x2, starting transfers between devices, swapped(): lax.ppermute(value, axis, [(i, i ^ by) for i in range(lax.axis_size(axis))])  11.9 us
    all_to_all x1, starting transfers between devices, gram_sum(): packed = lax.all_to_all(packed, ('z', 'y', 'core'), 0, 0, tiled=True)  11.4 us
    all_to_all x1, blocking collectives, reduced(): return jnp.sum(lax.all_to_all(pieces, axis, 0, 0, tiled=True), axis=0)  11 us
    all_to_all x1, waiting for transfers between devices, gram_sum(): packed = lax.all_to_all(packed, ('z', 'y', 'core'), 0, 0, tiled=True)  10.1 us
    ppermute x6, waiting for transfers between devices, shifted(): lax.ppermute(value, axis, [(i, (i + by) % size) for i in range(size)])  4.93 us
  transfers between devices with their start and end apart: 10, of which 4 were waited for; matrix products, arithmetic and copies ran while one was open for 3% of the time, Pallas kernels for 17%

profile of v5, /device:TPU:1, one launch (start us, length us, event | category | flops | bytes accessed | tf_op | source)
XLA Modules:
  0.0 140.8 jit_solution(3185787941304242116)
XLA Ops:
  1.6 1.4 gram.1
  3.0 8.8 %collective-permute-start = (f32[1344,128]{1,0:T(8,128)S(1)}, f32[1344,128]{1,0:T(8,128)S(1)}, u32[]{:S(2)}, u32[]{:S(2)}) collective-permute-start(f32[1344,128]{1,0:T(8,128)S(1)} %get-tuple-element.25), channel_id=1, source_target_pairs={{0,4},{4,0},{1,5},{5,1},{2,6},{6,2},{3,7},{7,3},{8,12},{12,8},{9,1... | collective-permute-start | bytes 2064392 | tf_op jit(solution)/shard_map/ppermute | solution.py:302
  14.1 2.1 %collective-permute-start.1 = (f32[336,128]{1,0:T(8,128)S(1)}, f32[336,128]{1,0:T(8,128)S(1)}, u32[]{:S(2)}, u32[]{:S(2)}) collective-permute-start(f32[336,128]{1,0:T(8,128)S(1)} %get-tuple-element.27), channel_id=1, source_target_pairs={{0,1},{1,2},{2,3},{3,0},{4,5},{5,6},{6,7},{7,4},{8,9},{9,10},{10,1... | collective-permute-start | bytes 516104 | tf_op jit(solution)/shard_map/ppermute | solution.py:298
  16.1 1.9 %collective-permute-start.2 = (f32[336,128]{1,0:T(8,128)S(1)}, f32[336,128]{1,0:T(8,128)S(1)}, u32[]{:S(2)}, u32[]{:S(2)}) collective-permute-start(f32[336,128]{1,0:T(8,128)S(1)} %get-tuple-element.28), channel_id=1, source_target_pairs={{0,2},{1,3},{2,0},{3,1},{4,6},{5,7},{6,4},{7,5},{8,10},{9,11},{10,... | collective-permute-start | bytes 516104 | tf_op jit(solution)/shard_map/ppermute | solution.py:298
  18.1 4.6 %collective-permute-start.3 = (f32[336,128]{1,0:T(8,128)S(1)}, f32[336,128]{1,0:T(8,128)S(1)}, u32[]{:S(2)}, u32[]{:S(2)}) collective-permute-start(f32[336,128]{1,0:T(8,128)S(1)} %get-tuple-element.29), channel_id=1, source_target_pairs={{0,3},{1,0},{2,1},{3,2},{4,7},{5,4},{6,5},{7,6},{8,11},{9,8},{10,9... | collective-permute-start | bytes 516104 | tf_op jit(solution)/shard_map/ppermute | solution.py:298
  22.7 1.5 %reshape.40 = f32[128,1,1664]{2,1,0:T(1,128)} reshape(f32[128,1664]{1,0:T(8,128)S(1)} %select_maximum_fusion) | data formatting | bytes 1703936 | tf_op jit(solution)/shard_map/reshape | solution.py:361
  24.2 2.7 %collective-permute-done.1 = f32[336,128]{1,0:T(8,128)S(1)} collective-permute-done((f32[336,128]{1,0:T(8,128)S(1)}, f32[336,128]{1,0:T(8,128)S(1)}, u32[]{:S(2)}, u32[]{:S(2)}) %collective-permute-start.1) | collective-permute-done | bytes 172064 | tf_op jit(solution)/shard_map/ppermute | solution.py:298
  27.0 2.2 %collective-permute-done.3 = f32[336,128]{1,0:T(8,128)S(1)} collective-permute-done((f32[336,128]{1,0:T(8,128)S(1)}, f32[336,128]{1,0:T(8,128)S(1)}, u32[]{:S(2)}, u32[]{:S(2)}) %collective-permute-start.3) | collective-permute-done | bytes 172064 | tf_op jit(solution)/shard_map/ppermute | solution.py:298
  29.2 11.0 %all_to_all.25 = f32[8,42,128]{2,1,0:T(8,128)S(1)} all-to-all(f32[8,42,128]{2,1,0:T(8,128)S(1)} %reshape.41), channel_id=1, replica_groups=mesh['z'=8,'y'=8,'core'=2,'x'=4] {'y'}, dimensions={0} | all-to-all | bytes 344064 | tf_op jit(solution)/shard_map/all_to_all | solution.py:310
  40.3 17.2 %all_to_all.26 = f32[8,42,128]{2,1,0:T(8,128)S(1)} all-to-all(f32[8,42,128]{2,1,0:T(8,128)S(1)} %broadcast_in_dim.18), channel_id=1, replica_groups=mesh['z'=8,'y'=8,'core'=2,'x'=4] {'z'}, dimensions={0} | all-to-all | bytes 344064 | tf_op jit(solution)/shard_map/all_to_all | solution.py:315
  57.5 11.0 %all_to_all.27 = f32[8,42,128]{2,1,0:T(8,128)S(1)} all-to-all(f32[8,42,128]{2,1,0:T(8,128)S(1)} %broadcast_in_dim.19), channel_id=1, replica_groups=mesh['z'=8,'y'=8,'core'=2,'x'=4] {'y'}, dimensions={0} | all-to-all | bytes 344064 | tf_op jit(solution)/shard_map/all_to_all | solution.py:315
  68.6 5.5 %collective-permute-start.4 = (f32[336,128]{1,0:T(8,128)S(1)}, f32[336,128]{1,0:T(8,128)S(1)}, u32[]{:S(2)}, u32[]{:S(2)}) collective-permute-start(f32[336,128]{1,0:T(8,128)S(1)} %reshape.42.refs_0_), channel_id=1, source_target_pairs={{0,1},{1,2},{2,3},{3,0},{4,5},{5,6},{6,7},{7,4},{8,9},{9,10},{10,1... | collective-permute-start | bytes 516104 | tf_op jit(solution)/shard_map/ppermute | solution.py:298
  74.1 1.9 %collective-permute-start.6 = (f32[336,128]{1,0:T(8,128)S(1)}, f32[336,128]{1,0:T(8,128)S(1)}, u32[]{:S(2)}, u32[]{:S(2)}) collective-permute-start(f32[336,128]{1,0:T(8,128)S(1)} %reshape.42.refs_0_), channel_id=1, source_target_pairs={{0,3},{1,0},{2,1},{3,2},{4,7},{5,4},{6,5},{7,6},{8,11},{9,8},{10,9... | collective-permute-start | bytes 516104 | tf_op jit(solution)/shard_map/ppermute | solution.py:298
  76.0 3.7 %collective-permute-start.5 = (f32[336,128]{1,0:T(8,128)S(1)}, f32[336,128]{1,0:T(8,128)S(1)}, u32[]{:S(2)}, u32[]{:S(2)}) collective-permute-start(f32[336,128]{1,0:T(8,128)S(1)} %reshape.42.refs_0_), channel_id=1, source_target_pairs={{0,2},{1,3},{2,0},{3,1},{4,6},{5,7},{6,4},{7,5},{8,10},{9,11},{10,... | collective-permute-start | bytes 516104 | tf_op jit(solution)/shard_map/ppermute | solution.py:298
  79.7 11.4 %all-to-all-start.3 = ((f32[128,1,1664]{2,1,0:T(1,128)}), f32[128,1,1664]{2,1,0:T(1,128)}, u32[]{:S(2)}, u32[]{:S(2)}) async-start(f32[128,1,1664]{2,1,0:T(1,128)} %reshape.40), calls=%async_computation.3 | async-start | bytes 1703936 | tf_op jit(solution)/shard_map/all_to_all | solution.py:333
  91.2 3.2 %collective-permute-start.7 = (f32[1344,128]{1,0:T(8,128)S(1)}, f32[1344,128]{1,0:T(8,128)S(1)}, u32[]{:S(2)}, u32[]{:S(2)}) collective-permute-start(f32[1344,128]{1,0:T(8,128)S(1)} %place_x.1.mine_ref), channel_id=1, source_target_pairs={{0,4},{4,0},{1,5},{5,1},{2,6},{6,2},{3,7},{7,3},{8,12},{12,8},{9,1... | collective-permute-start | bytes 2064392 | tf_op jit(solution)/shard_map/ppermute | solution.py:302
  94.4 1.6 %collective-permute-done.7.other_ref = f32[1344,128]{1,0:T(8,128)S(1)} collective-permute-done((f32[1344,128]{1,0:T(8,128)S(1)}, f32[1344,128]{1,0:T(8,128)S(1)}, u32[]{:S(2)}, u32[]{:S(2)}) %collective-permute-start.7) | collective-permute-done | bytes 688160 | tf_op jit(solution)/shard_map/ppermute | solution.py:302
  96.0 11.9 %early.1 = (f32[1152,128]{1,0:T(8,128)S(1)}, f32[3,128,128]{2,1,0:T(8,128)S(1)}, f32[1280,128]{1,0:T(8,128)S(1)}, f32[6,128,128]{2,1,0:T(8,128)S(1)}) custom-call(s32[1]{0:T(128)} %bitcast.1.bit_ref, f32[1344,128]{1,0:T(8,128)S(1)} %place_x.1.mine_ref, f32[1344,128]{1,0:T(8,128)S(1)} %collective-permute-done.7.other_ref, f32[128,768]{1,0:T(8,128)S(1)} %copy-done.1), custom_call_target="tpu_custom_call" | custom-call | flops 10000000000 | bytes 4000000 | tf_op jit(solution)/shard_map/early/pallas_call | solution.py:171
  107.8 10.1 %all-to-all-done.3 = f32[128,1,1664]{2,1,0:T(1,128)} async-done(((f32[128,1,1664]{2,1,0:T(1,128)}), f32[128,1,1664]{2,1,0:T(1,128)}, u32[]{:S(2)}, u32[]{:S(2)}) %all-to-all-start.3) | async-done | bytes 852000 | tf_op jit(solution)/shard_map/all_to_all | solution.py:333
  118.0 1.2 copy.8
  119.2 1.8 %sums.1 = f32[4,224,128]{2,1,0:T(8,128)} custom-call(f32[128,1664]{1,0:T(8,128)S(1)} %bitcast.6), custom_call_target="tpu_custom_call" | custom-call | flops 400000000 | bytes 4000000 | tf_op jit(solution)/shard_map/sums/pallas_call | solution.py:171
  121.0 3.7 %all-to-all-start.4 = ((f32[4,224,128]{2,1,0:T(8,128)}), f32[4,224,128]{2,1,0:T(8,128)S(1)}, u32[]{:S(2)}, u32[]{:S(2)}) async-start(f32[4,224,128]{2,1,0:T(8,128)} %sums.1), calls=%async_computation.4 | async-start | bytes 917504 | tf_op jit(solution)/shard_map/all_to_all | solution.py:372
  124.6 12.2 %late.1 = (f32[128,768]{1,0:T(8,128)}, f32[768,128]{1,0:T(8,128)S(1)}, f32[4,128,128]{2,1,0:T(8,128)S(1)}) custom-call(f32[3,128,128]{2,1,0:T(8,128)S(1)} %get-tuple-element.36.inv_in.early_inv, f32[1280,128]{1,0:T(8,128)S(1)} %get-tuple-element.37.left_ref, f32[6,128,128]{2,1,0:T(8,128)S(1)} %get-tuple-element.38.x_in), custom_call_target="tpu_custom_call" | custom-call | flops 10000000000 | bytes 4000000 | tf_op jit(solution)/shard_map/late/pallas_call | solution.py:171
  136.9 4.0 %means.1 = f32[32,768]{1,0:T(8,128)} custom-call(f32[4,224,128]{2,1,0:T(8,128)S(1)} %all-to-all-done.4.got_ref, f32[1152,128]{1,0:T(8,128)S(1)} %get-tuple-element.43.early_panel, f32[3,128,128]{2,1,0:T(8,128)S(1)} %get-tuple-element.36.inv_in.early_inv, f32[768,128]{1,0:T(8,128)S(1)} %get-tuple-element.44.late_panel, ...), custom_call_target="tpu_custom_call" | custom-call | flops 400000000 | bytes 4000000 | tf_op jit(solution)/shard_map/means/pallas_call | solution.py:171
  (32 shorter events, 3.4 us)
Async XLA Ops:
  0.6 1.0 copy-start
  1.6 10.7 %copy-start.1 = (f32[128,768]{1,0:T(8,128)S(1)}, f32[128,768]{1,0:T(8,128)}, u32[]{:S(2)}) copy-start(f32[128,768]{1,0:T(8,128)} %x_ref.3) | copy-start | bytes 1179652
  3.0 8.8 %copy-start.3 = (s32[128]{0:T(128)S(1)}, s32[128]{0:T(128)}, u32[]{:S(2)}) copy-start(s32[128]{0:T(128)} %param.3) | copy-start | bytes 1540
  3.0 10.9 %collective-permute-start = (f32[1344,128]{1,0:T(8,128)S(1)}, f32[1344,128]{1,0:T(8,128)S(1)}, u32[]{:S(2)}, u32[]{:S(2)}) collective-permute-start(f32[1344,128]{1,0:T(8,128)S(1)} %get-tuple-element.25), channel_id=1, source_target_pairs={{0,4},{4,0},{1,5},{5,1},{2,6},{6,2},{3,7},{7,3},{8,12},{12,8},{9,1... | collective-permute-start | bytes 2064392 | tf_op jit(solution)/shard_map/ppermute | solution.py:302
  13.9 8.7 %copy-start.2 = (f32[128,1536]{1,0:T(8,128)S(1)}, f32[128,1536]{1,0:T(8,128)}, u32[]{:S(2)}) copy-start(f32[128,1536]{1,0:T(8,128)} %reshape.39) | copy-start | bytes 2359300
  14.1 12.9 %collective-permute-start.1 = (f32[336,128]{1,0:T(8,128)S(1)}, f32[336,128]{1,0:T(8,128)S(1)}, u32[]{:S(2)}, u32[]{:S(2)}) collective-permute-start(f32[336,128]{1,0:T(8,128)S(1)} %get-tuple-element.27), channel_id=1, source_target_pairs={{0,1},{1,2},{2,3},{3,0},{4,5},{5,6},{6,7},{7,4},{8,9},{9,10},{10,1... | collective-permute-start | bytes 516104 | tf_op jit(solution)/shard_map/ppermute | solution.py:298
  16.1 10.9 %collective-permute-start.2 = (f32[336,128]{1,0:T(8,128)S(1)}, f32[336,128]{1,0:T(8,128)S(1)}, u32[]{:S(2)}, u32[]{:S(2)}) collective-permute-start(f32[336,128]{1,0:T(8,128)S(1)} %get-tuple-element.28), channel_id=1, source_target_pairs={{0,2},{1,3},{2,0},{3,1},{4,6},{5,7},{6,4},{7,5},{8,10},{9,11},{10,... | collective-permute-start | bytes 516104 | tf_op jit(solution)/shard_map/ppermute | solution.py:298
  18.1 11.1 %collective-permute-start.3 = (f32[336,128]{1,0:T(8,128)S(1)}, f32[336,128]{1,0:T(8,128)S(1)}, u32[]{:S(2)}, u32[]{:S(2)}) collective-permute-start(f32[336,128]{1,0:T(8,128)S(1)} %get-tuple-element.29), channel_id=1, source_target_pairs={{0,3},{1,0},{2,1},{3,2},{4,7},{5,4},{6,5},{7,6},{8,11},{9,8},{10,9... | collective-permute-start | bytes 516104 | tf_op jit(solution)/shard_map/ppermute | solution.py:298
  68.6 11.2 %collective-permute-start.4 = (f32[336,128]{1,0:T(8,128)S(1)}, f32[336,128]{1,0:T(8,128)S(1)}, u32[]{:S(2)}, u32[]{:S(2)}) collective-permute-start(f32[336,128]{1,0:T(8,128)S(1)} %reshape.42.refs_0_), channel_id=1, source_target_pairs={{0,1},{1,2},{2,3},{3,0},{4,5},{5,6},{6,7},{7,4},{8,9},{9,10},{10,1... | collective-permute-start | bytes 516104 | tf_op jit(solution)/shard_map/ppermute | solution.py:298
  74.1 17.1 %collective-permute-start.6 = (f32[336,128]{1,0:T(8,128)S(1)}, f32[336,128]{1,0:T(8,128)S(1)}, u32[]{:S(2)}, u32[]{:S(2)}) collective-permute-start(f32[336,128]{1,0:T(8,128)S(1)} %reshape.42.refs_0_), channel_id=1, source_target_pairs={{0,3},{1,0},{2,1},{3,2},{4,7},{5,4},{6,5},{7,6},{8,11},{9,8},{10,9... | collective-permute-start | bytes 516104 | tf_op jit(solution)/shard_map/ppermute | solution.py:298
  76.0 15.1 %collective-permute-start.5 = (f32[336,128]{1,0:T(8,128)S(1)}, f32[336,128]{1,0:T(8,128)S(1)}, u32[]{:S(2)}, u32[]{:S(2)}) collective-permute-start(f32[336,128]{1,0:T(8,128)S(1)} %reshape.42.refs_0_), channel_id=1, source_target_pairs={{0,2},{1,3},{2,0},{3,1},{4,6},{5,7},{6,4},{7,5},{8,10},{9,11},{10,... | collective-permute-start | bytes 516104 | tf_op jit(solution)/shard_map/ppermute | solution.py:298
  79.7 38.2 %all-to-all-start.3 = ((f32[128,1,1664]{2,1,0:T(1,128)}), f32[128,1,1664]{2,1,0:T(1,128)}, u32[]{:S(2)}, u32[]{:S(2)}) async-start(f32[128,1,1664]{2,1,0:T(1,128)} %reshape.40), calls=%async_computation.3 | async-start | bytes 1703936 | tf_op jit(solution)/shard_map/all_to_all | solution.py:333
  91.2 4.7 %collective-permute-start.7 = (f32[1344,128]{1,0:T(8,128)S(1)}, f32[1344,128]{1,0:T(8,128)S(1)}, u32[]{:S(2)}, u32[]{:S(2)}) collective-permute-start(f32[1344,128]{1,0:T(8,128)S(1)} %place_x.1.mine_ref), channel_id=1, source_target_pairs={{0,4},{4,0},{1,5},{5,1},{2,6},{6,2},{3,7},{7,3},{8,12},{12,8},{9,1... | collective-permute-start | bytes 2064392 | tf_op jit(solution)/shard_map/ppermute | solution.py:302
  121.0 15.9 %all-to-all-start.4 = ((f32[4,224,128]{2,1,0:T(8,128)}), f32[4,224,128]{2,1,0:T(8,128)S(1)}, u32[]{:S(2)}, u32[]{:S(2)}) async-start(f32[4,224,128]{2,1,0:T(8,128)} %sums.1), calls=%async_computation.4 | async-start | bytes 917504 | tf_op jit(solution)/shard_map/all_to_all | solution.py:372

commit v6 on v5

--- a/solution.py
+++ b/solution.py
@@ -84,7 +84,7 @@
     return slice(at, at + B)
 
 
-def steps(which, n, inv, load, store, x_blocks, panel_ref, inv_ref):
+def steps(which, n, inv, load, store, x_blocks, panel_ref, inv_ref, link_ref):
     base = which[0]
     for now in which:
         rest = range(now + 1, n)
@@ -100,10 +100,11 @@
                     store(now, i, j, load(now, i, j) - mul_t(panel[i], panel[j]))
             x_blocks[j] -= mul_t(solved, panel[j])
         if rest:
+            link_ref[now - base] = jnp.dot(panel[now + 1], inv, precision=HI, preferred_element_type=jnp.float32)
             inv_ref[now + 1 - base] = inv = following
 
 
-def early_kernel(total, n, cut_at, bit_ref, mine_ref, other_ref, x_ref, panel_ref, inv_ref, left_ref, x_blocks, a_ref):
+def early_kernel(total, n, cut_at, bit_ref, mine_ref, other_ref, x_ref, panel_ref, inv_ref, link_ref, left_ref, x_blocks, a_ref):
     row = lax.broadcasted_iota(jnp.int32, (B, B), 0)
     col = lax.broadcasted_iota(jnp.int32, (B, B), 1)
     half = mine_ref.shape[0]
@@ -124,10 +125,10 @@
             left_ref[block(i, j, n, cut_at)] = value
 
     inv_ref[0] = inv = inverse_factor(load(0, 0, 0))
-    steps(range(cut_at), n, inv, load, store, x_blocks, panel_ref, inv_ref)
-
-
-def late_kernel(n, cut_at, inv_in, left_ref, x_in, out_ref, panel_ref, inv_ref, a_ref, x_blocks):
+    steps(range(cut_at), n, inv, load, store, x_blocks, panel_ref, inv_ref, link_ref)
+
+
+def late_kernel(n, cut_at, inv_in, left_ref, x_in, out_ref, panel_ref, inv_ref, link_ref, a_ref, x_blocks):
     x_blocks[...] = x_in[...]
 
     def load(now, i, j):
@@ -137,12 +138,12 @@
         a_ref[block(i, j, n, cut_at)] = value
 
     inv_ref[0] = inv = inv_in[cut_at]
-    steps(range(cut_at, n), n, inv, load, store, x_blocks, panel_ref, inv_ref)
+    steps(range(cut_at, n), n, inv, load, store, x_blocks, panel_ref, inv_ref, link_ref)
     for j in range(n):
         out_ref[:, j * B : j * B + B] = x_blocks[j]
 
 
-def means_kernel(n, cut_at, got_ref, early_panel, early_inv, late_panel, late_inv, out_ref):
+def means_kernel(n, cut_at, got_ref, panel0, inv0, link0, panel1, inv1, link1, out_ref):
     peers = got_ref.shape[0]
     keep = out_ref.shape[0]
 
@@ -151,16 +152,18 @@
 
     counts = jnp.maximum(gathered(n), 1.0)
     x = [gathered(j) / counts for j in range(n)]
-    at = [0, 0]
+    panels = [panel0[k * B : k * B + B] for k in range(panel0.shape[0] // B)]
+    panels += [panel1[k * B : k * B + B] for k in range(panel1.shape[0] // B)]
+    panels = iter(panels)
     for now in range(n):
-        late = int(now >= cut_at)
-        inv = late_inv[now - cut_at] if late else early_inv[now]
-        x[now] = mul_t(x[now], inv)
-        out_ref[:, now * B : now * B + B] = x[now]
+        solved = mul_t(x[now], inv1[now - cut_at] if now >= cut_at else inv0[now])
+        out_ref[:, now * B : now * B + B] = solved
         for j in range(now + 1, n):
-            panel = (early_panel, late_panel)[late][at[late] : at[late] + B]
-            at[late] += B
-            x[j] = x[j] - mul_t(x[now], panel)
+            panel = next(panels)
+            if j == now + 1:
+                x[j] = x[j] - mul_t(x[now], link1[now - cut_at] if now >= cut_at else link0[now])
+            else:
+                x[j] = x[j] - mul_t(solved, panel)
 
 
 def f32(*shape):
@@ -184,7 +187,7 @@
     n = x.shape[1] // B
     rows = first(n, n)
     panels = sum(n - 1 - t for t in range(cut_at)) * B
-    outs = [f32(panels, B), f32(cut_at + 1, B, B), f32(rows - first(cut_at, n), B), f32(n, x.shape[0], B)]
+    outs = [f32(panels, B), f32(cut_at + 1, B, B), f32(cut_at, B, B), f32(rows - first(cut_at, n), B), f32(n, x.shape[0], B)]
     kernel = functools.partial(early_kernel, total, n, cut_at)
     return local_call(kernel, outs, [bit, mine, other, x], "early", [(rows, B)], scalars=1)
 
@@ -192,7 +195,7 @@
 def late(inv, left, x_blocks, cut_at):
     n, rows, _ = x_blocks.shape
     panels = sum(n - 1 - t for t in range(cut_at, n)) * B
-    outs = [f32(rows, n * B), f32(panels, B), f32(n - cut_at, B, B)]
+    outs = [f32(rows, n * B), f32(panels, B), f32(n - cut_at, B, B), f32(n - 1 - cut_at, B, B)]
     kernel = functools.partial(late_kernel, n, cut_at)
     return local_call(kernel, outs, [inv, left, x_blocks], "late", [left.shape, x_blocks.shape])
 
@@ -361,8 +364,8 @@
     packed = jnp.concatenate([outgoing, labels], axis=1).reshape(owners, 1, CAP * width + B)
     summed, packed = lax.optimization_barrier((x_sum(pieces), packed))
     mine, other, packed = gram_sum(summed, packed)
-    cut_at = 2
-    early_panel, early_inv, left, x_blocks = early(bit, mine, other, embeddings, total, cut_at)
+    cut_at = 3
+    early_panel, early_inv, early_link, left, x_blocks = early(bit, mine, other, embeddings, total, cut_at)
     packed, early_inv = lax.optimization_barrier((packed, early_inv))
     groups = lax.axis_size("x")
     keep = per_owner // groups
@@ -370,10 +373,10 @@
     kernel = functools.partial(sums_kernel, CAP, n, groups)
     [sums] = local_call(kernel, [f32(groups, (n + 1) * keep, B)], [packed], "sums", flops=400_000_000)
     sums = lax.all_to_all(sums, "x", 0, 0, tiled=True)
-    whitened, late_panel, late_inv = late(early_inv, left, x_blocks, cut_at)
+    whitened, late_panel, late_inv, late_link = late(early_inv, left, x_blocks, cut_at)
     sums, late_inv = lax.optimization_barrier((sums, late_inv))
     kernel = functools.partial(means_kernel, n, cut_at)
-    panels = [sums, early_panel, early_inv, late_panel, late_inv]
+    panels = [sums, early_panel, early_inv, early_link, late_panel, late_inv, late_link]
     [means] = local_call(kernel, [f32(keep, width)], panels, "means", flops=400_000_000)
     return whitened, means
 

time: 141 us -> 137 us (0.972)
  waiting for transfers between devices: 16.6 us -> 13.2 us
    all_to_all x1, waiting for transfers between devices: 10.1 us -> 6.42 us  [gram_sum(): packed = lax.all_to_all(packed, ('z', 'y', 'core'), 0, 0, tiled=True)]
  transfers between devices with their start and end apart: 10 -> 10, of which waited for: 4 -> 5; matrix products, arithmetic and copies ran while one was open for 3% -> 3% of each run, Pallas kernels for 17% -> 18%
where the time goes in v6:
time: 137 us; the launch traced here: 136 us
  starting transfers between devices  46.6 us (34%)
  blocking collectives  39.2 us (29%)
  Pallas kernels  30.6 us (22%)
  waiting for transfers between devices  13.2 us (10%)
  local copies, waits for them, and re-layouts  5.03 us (4%)
    pallas_call x4, Pallas kernels, local_call(): pl.pallas_call(kernel, out_shape=outs, in_specs=[SCALAR] * scalars + [VME...  29 us
    all_to_all x2, blocking collectives, spread(): return lax.all_to_all(copies, axis, 0, 0, tiled=True)  28.2 us
    ppermute x6, starting transfers between devices, shifted(): lax.ppermute(value, axis, [(i, (i + by) % size) for i in range(size)])  19.7 us
    ppermute x2, starting transfers between devices, swapped(): lax.ppermute(value, axis, [(i, i ^ by) for i in range(lax.axis_size(axis))])  11.9 us
    all_to_all x1, starting transfers between devices, gram_sum(): packed = lax.all_to_all(packed, ('z', 'y', 'core'), 0, 0, tiled=True)  11.4 us
    all_to_all x1, blocking collectives, reduced(): return jnp.sum(lax.all_to_all(pieces, axis, 0, 0, tiled=True), axis=0)  11 us
    all_to_all x1, waiting for transfers between devices, gram_sum(): packed = lax.all_to_all(packed, ('z', 'y', 'core'), 0, 0, tiled=True)  6.42 us
    ppermute x6, waiting for transfers between devices, shifted(): lax.ppermute(value, axis, [(i, (i + by) % size) for i in range(size)])  4.93 us
  transfers between devices with their start and end apart: 10, of which 5 were waited for; matrix products, arithmetic and copies ran while one was open for 3% of the time, Pallas kernels for 18%

profile of v6, /device:TPU:1, one launch (start us, length us, event | category | flops | bytes accessed | tf_op | source)
XLA Modules:
  0.0 136.5 jit_solution(15576213479140276782)
XLA Ops:
  1.6 1.4 %gram.1 = (f32[1344,128]{1,0:T(8,128)S(1)}, f32[1344,128]{1,0:T(8,128)S(1)}) custom-call(s32[1]{0:T(128)} %bitcast.1.bit_ref, f32[128,768]{1,0:T(8,128)S(1)} %copy-done), custom_call_target="tpu_custom_call" | custom-call | flops 700000000 | bytes 2000000 | tf_op jit(solution)/shard_map/gram/pallas_call | solution.py:245
  3.0 8.8 %collective-permute-start = (f32[1344,128]{1,0:T(8,128)S(1)}, f32[1344,128]{1,0:T(8,128)S(1)}, u32[]{:S(2)}, u32[]{:S(2)}) collective-permute-start(f32[1344,128]{1,0:T(8,128)S(1)} %get-tuple-element.27), channel_id=1, source_target_pairs={{0,4},{4,0},{1,5},{5,1},{2,6},{6,2},{3,7},{7,3},{8,12},{12,8},{9,1... | collective-permute-start | bytes 2064392 | tf_op jit(solution)/shard_map/ppermute | solution.py:305
  14.1 2.1 %collective-permute-start.1 = (f32[336,128]{1,0:T(8,128)S(1)}, f32[336,128]{1,0:T(8,128)S(1)}, u32[]{:S(2)}, u32[]{:S(2)}) collective-permute-start(f32[336,128]{1,0:T(8,128)S(1)} %get-tuple-element.29), channel_id=1, source_target_pairs={{0,1},{1,2},{2,3},{3,0},{4,5},{5,6},{6,7},{7,4},{8,9},{9,10},{10,1... | collective-permute-start | bytes 516104 | tf_op jit(solution)/shard_map/ppermute | solution.py:301
  16.1 1.9 %collective-permute-start.2 = (f32[336,128]{1,0:T(8,128)S(1)}, f32[336,128]{1,0:T(8,128)S(1)}, u32[]{:S(2)}, u32[]{:S(2)}) collective-permute-start(f32[336,128]{1,0:T(8,128)S(1)} %get-tuple-element.30), channel_id=1, source_target_pairs={{0,2},{1,3},{2,0},{3,1},{4,6},{5,7},{6,4},{7,5},{8,10},{9,11},{10,... | collective-permute-start | bytes 516104 | tf_op jit(solution)/shard_map/ppermute | solution.py:301
  18.1 4.6 %collective-permute-start.3 = (f32[336,128]{1,0:T(8,128)S(1)}, f32[336,128]{1,0:T(8,128)S(1)}, u32[]{:S(2)}, u32[]{:S(2)}) collective-permute-start(f32[336,128]{1,0:T(8,128)S(1)} %get-tuple-element.31), channel_id=1, source_target_pairs={{0,3},{1,0},{2,1},{3,2},{4,7},{5,4},{6,5},{7,6},{8,11},{9,8},{10,9... | collective-permute-start | bytes 516104 | tf_op jit(solution)/shard_map/ppermute | solution.py:301
  22.7 1.5 %reshape.40 = f32[128,1,1664]{2,1,0:T(1,128)} reshape(f32[128,1664]{1,0:T(8,128)S(1)} %select_maximum_fusion) | data formatting | bytes 1703936 | tf_op jit(solution)/shard_map/reshape | solution.py:364
  24.2 2.7 %collective-permute-done.1 = f32[336,128]{1,0:T(8,128)S(1)} collective-permute-done((f32[336,128]{1,0:T(8,128)S(1)}, f32[336,128]{1,0:T(8,128)S(1)}, u32[]{:S(2)}, u32[]{:S(2)}) %collective-permute-start.1) | collective-permute-done | bytes 172064 | tf_op jit(solution)/shard_map/ppermute | solution.py:301
  27.0 2.2 %collective-permute-done.3 = f32[336,128]{1,0:T(8,128)S(1)} collective-permute-done((f32[336,128]{1,0:T(8,128)S(1)}, f32[336,128]{1,0:T(8,128)S(1)}, u32[]{:S(2)}, u32[]{:S(2)}) %collective-permute-start.3) | collective-permute-done | bytes 172064 | tf_op jit(solution)/shard_map/ppermute | solution.py:301
  29.2 11.0 %all_to_all.25 = f32[8,42,128]{2,1,0:T(8,128)S(1)} all-to-all(f32[8,42,128]{2,1,0:T(8,128)S(1)} %reshape.41), channel_id=1, replica_groups=mesh['z'=8,'y'=8,'core'=2,'x'=4] {'y'}, dimensions={0} | all-to-all | bytes 344064 | tf_op jit(solution)/shard_map/all_to_all | solution.py:313
  40.3 17.2 %all_to_all.26 = f32[8,42,128]{2,1,0:T(8,128)S(1)} all-to-all(f32[8,42,128]{2,1,0:T(8,128)S(1)} %broadcast_in_dim.18), channel_id=1, replica_groups=mesh['z'=8,'y'=8,'core'=2,'x'=4] {'z'}, dimensions={0} | all-to-all | bytes 344064 | tf_op jit(solution)/shard_map/all_to_all | solution.py:318
  57.5 11.0 %all_to_all.27 = f32[8,42,128]{2,1,0:T(8,128)S(1)} all-to-all(f32[8,42,128]{2,1,0:T(8,128)S(1)} %broadcast_in_dim.19), channel_id=1, replica_groups=mesh['z'=8,'y'=8,'core'=2,'x'=4] {'y'}, dimensions={0} | all-to-all | bytes 344064 | tf_op jit(solution)/shard_map/all_to_all | solution.py:318
  68.6 5.5 %collective-permute-start.4 = (f32[336,128]{1,0:T(8,128)S(1)}, f32[336,128]{1,0:T(8,128)S(1)}, u32[]{:S(2)}, u32[]{:S(2)}) collective-permute-start(f32[336,128]{1,0:T(8,128)S(1)} %reshape.42.refs_0_), channel_id=1, source_target_pairs={{0,1},{1,2},{2,3},{3,0},{4,5},{5,6},{6,7},{7,4},{8,9},{9,10},{10,1... | collective-permute-start | bytes 516104 | tf_op jit(solution)/shard_map/ppermute | solution.py:301
  74.1 1.9 %collective-permute-start.6 = (f32[336,128]{1,0:T(8,128)S(1)}, f32[336,128]{1,0:T(8,128)S(1)}, u32[]{:S(2)}, u32[]{:S(2)}) collective-permute-start(f32[336,128]{1,0:T(8,128)S(1)} %reshape.42.refs_0_), channel_id=1, source_target_pairs={{0,3},{1,0},{2,1},{3,2},{4,7},{5,4},{6,5},{7,6},{8,11},{9,8},{10,9... | collective-permute-start | bytes 516104 | tf_op jit(solution)/shard_map/ppermute | solution.py:301
  76.0 3.7 %collective-permute-start.5 = (f32[336,128]{1,0:T(8,128)S(1)}, f32[336,128]{1,0:T(8,128)S(1)}, u32[]{:S(2)}, u32[]{:S(2)}) collective-permute-start(f32[336,128]{1,0:T(8,128)S(1)} %reshape.42.refs_0_), channel_id=1, source_target_pairs={{0,2},{1,3},{2,0},{3,1},{4,6},{5,7},{6,4},{7,5},{8,10},{9,11},{10,... | collective-permute-start | bytes 516104 | tf_op jit(solution)/shard_map/ppermute | solution.py:301
  79.7 11.4 %all-to-all-start.3 = ((f32[128,1,1664]{2,1,0:T(1,128)}), f32[128,1,1664]{2,1,0:T(1,128)}, u32[]{:S(2)}, u32[]{:S(2)}) async-start(f32[128,1,1664]{2,1,0:T(1,128)} %reshape.40), calls=%async_computation.3 | async-start | bytes 1703936 | tf_op jit(solution)/shard_map/all_to_all | solution.py:336
  91.2 3.2 %collective-permute-start.7 = (f32[1344,128]{1,0:T(8,128)S(1)}, f32[1344,128]{1,0:T(8,128)S(1)}, u32[]{:S(2)}, u32[]{:S(2)}) collective-permute-start(f32[1344,128]{1,0:T(8,128)S(1)} %place_x.1.mine_ref), channel_id=1, source_target_pairs={{0,4},{4,0},{1,5},{5,1},{2,6},{6,2},{3,7},{7,3},{8,12},{12,8},{9,1... | collective-permute-start | bytes 2064392 | tf_op jit(solution)/shard_map/ppermute | solution.py:305
  94.4 1.6 %collective-permute-done.7.other_ref = f32[1344,128]{1,0:T(8,128)S(1)} collective-permute-done((f32[1344,128]{1,0:T(8,128)S(1)}, f32[1344,128]{1,0:T(8,128)S(1)}, u32[]{:S(2)}, u32[]{:S(2)}) %collective-permute-start.7) | collective-permute-done | bytes 688160 | tf_op jit(solution)/shard_map/ppermute | solution.py:305
  96.0 15.6 %early.1 = (f32[1536,128]{1,0:T(8,128)S(1)}, f32[4,128,128]{2,1,0:T(8,128)S(1)}, f32[3,128,128]{2,1,0:T(8,128)S(1)}, f32[768,128]{1,0:T(8,128)S(1)}, f32[6,128,128]{2,1,0:T(8,128)S(1)}) custom-call(s32[1]{0:T(128)} %bitcast.1.bit_ref, f32[1344,128]{1,0:T(8,128)S(1)} %place_x.1.mine_ref, f32[1344,128]{1,0:T(8,128)S(1)} %collective-permute-done.7.other_ref, ...), custom_call_target="tpu_custom_call" | custom-call | flops 10000000000 | bytes 4000000 | tf_op jit(solution)/shard_map/early/pallas_call | solution.py:174
  111.6 6.4 %all-to-all-done.3 = f32[128,1,1664]{2,1,0:T(1,128)} async-done(((f32[128,1,1664]{2,1,0:T(1,128)}), f32[128,1,1664]{2,1,0:T(1,128)}, u32[]{:S(2)}, u32[]{:S(2)}) %all-to-all-start.3) | async-done | bytes 852000 | tf_op jit(solution)/shard_map/all_to_all | solution.py:336
  118.0 1.2 copy.8
  119.2 1.8 %sums.1 = f32[4,224,128]{2,1,0:T(8,128)} custom-call(f32[128,1664]{1,0:T(8,128)S(1)} %bitcast.6), custom_call_target="tpu_custom_call" | custom-call | flops 400000000 | bytes 4000000 | tf_op jit(solution)/shard_map/sums/pallas_call | solution.py:174
  121.0 3.6 %all-to-all-start.4 = ((f32[4,224,128]{2,1,0:T(8,128)}), f32[4,224,128]{2,1,0:T(8,128)S(1)}, u32[]{:S(2)}, u32[]{:S(2)}) async-start(f32[4,224,128]{2,1,0:T(8,128)} %sums.1), calls=%async_computation.4 | async-start | bytes 917504 | tf_op jit(solution)/shard_map/all_to_all | solution.py:375
  124.6 8.3 %late.1 = (f32[128,768]{1,0:T(8,128)}, f32[384,128]{1,0:T(8,128)S(1)}, f32[3,128,128]{2,1,0:T(8,128)S(1)}, f32[2,128,128]{2,1,0:T(8,128)S(1)}) custom-call(f32[4,128,128]{2,1,0:T(8,128)S(1)} %get-tuple-element.38.inv_in.inv0, f32[768,128]{1,0:T(8,128)S(1)} %get-tuple-element.39.left_ref, f32[6,128,128]{2,1,0:T(8,128)S(1)} %get-tuple-element.40.x_in), custom_call_target="tpu_custom_call" | custom-call | flops 10000000000 | bytes 4000000 | tf_op jit(solution)/shard_map/late/pallas_call | solution.py:174
  133.1 3.3 %means.1 = f32[32,768]{1,0:T(8,128)} custom-call(f32[4,224,128]{2,1,0:T(8,128)S(1)} %all-to-all-done.4.got_ref, f32[1536,128]{1,0:T(8,128)S(1)} %get-tuple-element.45.panel0, f32[4,128,128]{2,1,0:T(8,128)S(1)} %get-tuple-element.38.inv_in.inv0, f32[3,128,128]{2,1,0:T(8,128)S(1)} %get-tuple-element.46.link0, f32[384,128]{1,0:T(8,128)S(1)} %get-tuple-element.47.panel1, ...), custom_call_target="tpu_custom_call" | custom-call | flops 400000000 | bytes 4000000 | tf_op jit(solution)/shard_map/means/pallas_call | solution.py:174
  (32 shorter events, 3.7 us)
Async XLA Ops:
  0.6 1.0 copy-start
  1.6 10.7 %copy-start.1 = (f32[128,768]{1,0:T(8,128)S(1)}, f32[128,768]{1,0:T(8,128)}, u32[]{:S(2)}) copy-start(f32[128,768]{1,0:T(8,128)} %x_ref.3) | copy-start | bytes 1179652
  3.0 8.8 %copy-start.3 = (s32[128]{0:T(128)S(1)}, s32[128]{0:T(128)}, u32[]{:S(2)}) copy-start(s32[128]{0:T(128)} %param.3) | copy-start | bytes 1540
  3.0 10.9 %collective-permute-start = (f32[1344,128]{1,0:T(8,128)S(1)}, f32[1344,128]{1,0:T(8,128)S(1)}, u32[]{:S(2)}, u32[]{:S(2)}) collective-permute-start(f32[1344,128]{1,0:T(8,128)S(1)} %get-tuple-element.27), channel_id=1, source_target_pairs={{0,4},{4,0},{1,5},{5,1},{2,6},{6,2},{3,7},{7,3},{8,12},{12,8},{9,1... | collective-permute-start | bytes 2064392 | tf_op jit(solution)/shard_map/ppermute | solution.py:305
  13.9 8.7 %copy-start.2 = (f32[128,1536]{1,0:T(8,128)S(1)}, f32[128,1536]{1,0:T(8,128)}, u32[]{:S(2)}) copy-start(f32[128,1536]{1,0:T(8,128)} %reshape.39) | copy-start | bytes 2359300
  14.1 12.9 %collective-permute-start.1 = (f32[336,128]{1,0:T(8,128)S(1)}, f32[336,128]{1,0:T(8,128)S(1)}, u32[]{:S(2)}, u32[]{:S(2)}) collective-permute-start(f32[336,128]{1,0:T(8,128)S(1)} %get-tuple-element.29), channel_id=1, source_target_pairs={{0,1},{1,2},{2,3},{3,0},{4,5},{5,6},{6,7},{7,4},{8,9},{9,10},{10,1... | collective-permute-start | bytes 516104 | tf_op jit(solution)/shard_map/ppermute | solution.py:301
  16.1 10.9 %collective-permute-start.2 = (f32[336,128]{1,0:T(8,128)S(1)}, f32[336,128]{1,0:T(8,128)S(1)}, u32[]{:S(2)}, u32[]{:S(2)}) collective-permute-start(f32[336,128]{1,0:T(8,128)S(1)} %get-tuple-element.30), channel_id=1, source_target_pairs={{0,2},{1,3},{2,0},{3,1},{4,6},{5,7},{6,4},{7,5},{8,10},{9,11},{10,... | collective-permute-start | bytes 516104 | tf_op jit(solution)/shard_map/ppermute | solution.py:301
  18.1 11.1 %collective-permute-start.3 = (f32[336,128]{1,0:T(8,128)S(1)}, f32[336,128]{1,0:T(8,128)S(1)}, u32[]{:S(2)}, u32[]{:S(2)}) collective-permute-start(f32[336,128]{1,0:T(8,128)S(1)} %get-tuple-element.31), channel_id=1, source_target_pairs={{0,3},{1,0},{2,1},{3,2},{4,7},{5,4},{6,5},{7,6},{8,11},{9,8},{10,9... | collective-permute-start | bytes 516104 | tf_op jit(solution)/shard_map/ppermute | solution.py:301
  68.6 11.2 %collective-permute-start.4 = (f32[336,128]{1,0:T(8,128)S(1)}, f32[336,128]{1,0:T(8,128)S(1)}, u32[]{:S(2)}, u32[]{:S(2)}) collective-permute-start(f32[336,128]{1,0:T(8,128)S(1)} %reshape.42.refs_0_), channel_id=1, source_target_pairs={{0,1},{1,2},{2,3},{3,0},{4,5},{5,6},{6,7},{7,4},{8,9},{9,10},{10,1... | collective-permute-start | bytes 516104 | tf_op jit(solution)/shard_map/ppermute | solution.py:301
  74.1 17.1 %collective-permute-start.6 = (f32[336,128]{1,0:T(8,128)S(1)}, f32[336,128]{1,0:T(8,128)S(1)}, u32[]{:S(2)}, u32[]{:S(2)}) collective-permute-start(f32[336,128]{1,0:T(8,128)S(1)} %reshape.42.refs_0_), channel_id=1, source_target_pairs={{0,3},{1,0},{2,1},{3,2},{4,7},{5,4},{6,5},{7,6},{8,11},{9,8},{10,9... | collective-permute-start | bytes 516104 | tf_op jit(solution)/shard_map/ppermute | solution.py:301
  76.0 15.1 %collective-permute-start.5 = (f32[336,128]{1,0:T(8,128)S(1)}, f32[336,128]{1,0:T(8,128)S(1)}, u32[]{:S(2)}, u32[]{:S(2)}) collective-permute-start(f32[336,128]{1,0:T(8,128)S(1)} %reshape.42.refs_0_), channel_id=1, source_target_pairs={{0,2},{1,3},{2,0},{3,1},{4,6},{5,7},{6,4},{7,5},{8,10},{9,11},{10,... | collective-permute-start | bytes 516104 | tf_op jit(solution)/shard_map/ppermute | solution.py:301
  79.7 38.2 %all-to-all-start.3 = ((f32[128,1,1664]{2,1,0:T(1,128)}), f32[128,1,1664]{2,1,0:T(1,128)}, u32[]{:S(2)}, u32[]{:S(2)}) async-start(f32[128,1,1664]{2,1,0:T(1,128)} %reshape.40), calls=%async_computation.3 | async-start | bytes 1703936 | tf_op jit(solution)/shard_map/all_to_all | solution.py:336
  91.2 4.7 %collective-permute-start.7 = (f32[1344,128]{1,0:T(8,128)S(1)}, f32[1344,128]{1,0:T(8,128)S(1)}, u32[]{:S(2)}, u32[]{:S(2)}) collective-permute-start(f32[1344,128]{1,0:T(8,128)S(1)} %place_x.1.mine_ref), channel_id=1, source_target_pairs={{0,4},{4,0},{1,5},{5,1},{2,6},{6,2},{3,7},{7,3},{8,12},{12,8},{9,1... | collective-permute-start | bytes 2064392 | tf_op jit(solution)/shard_map/ppermute | solution.py:305
  121.0 12.2 %all-to-all-start.4 = ((f32[4,224,128]{2,1,0:T(8,128)}), f32[4,224,128]{2,1,0:T(8,128)S(1)}, u32[]{:S(2)}, u32[]{:S(2)}) async-start(f32[4,224,128]{2,1,0:T(8,128)} %sums.1), calls=%async_computation.4 | async-start | bytes 917504 | tf_op jit(solution)/shard_map/all_to_all | solution.py:375

commit v7 on v6

--- a/solution.py
+++ b/solution.py
@@ -143,12 +143,12 @@
         out_ref[:, j * B : j * B + B] = x_blocks[j]
 
 
-def means_kernel(n, cut_at, got_ref, panel0, inv0, link0, panel1, inv1, link1, out_ref):
-    peers = got_ref.shape[0]
+def means_kernel(n, cut_at, panel0, inv0, link0, panel1, inv1, link1, *refs):
+    *got, out_ref = refs
     keep = out_ref.shape[0]
 
     def gathered(j):
-        return functools.reduce(lambda a, b: a + b, [got_ref[q, j * keep : j * keep + keep] for q in range(peers)])
+        return functools.reduce(lambda a, b: a + b, [g[j * keep : j * keep + keep] for g in got])
 
     counts = jnp.maximum(gathered(n), 1.0)
     x = [gathered(j) / counts for j in range(n)]
@@ -200,17 +200,16 @@
     return local_call(kernel, outs, [inv, left, x_blocks], "late", [left.shape, x_blocks.shape])
 
 
-def sums_kernel(cap, n, groups, packed_ref, out_ref):
+def sums_kernel(cap, n, at_ref, packed_ref, *refs):
+    outs, all_ref = refs[:-1], refs[-1]
     rows = packed_ref.shape[0]
-    per_owner = B
-    keep = per_owner // groups
+    groups = len(outs)
+    keep = B // groups
     width = n * B
-    ids = lax.broadcasted_iota(jnp.int32, (rows, per_owner), 1).astype(jnp.float32)
+    ids = lax.broadcasted_iota(jnp.int32, (rows, B), 1).astype(jnp.float32)
     tn = (((0,), (0,)), ((), ()))
-    members = []
-    for c in range(cap):
-        tag = packed_ref[:, cap * width + c : cap * width + c + 1]
-        members.append(jnp.where(tag == ids, 1.0, 0.0))
+    tags = packed_ref[:, 0, cap * width : cap * width + B]
+    members = [jnp.where(tags[:, c : c + 1] == ids, 1.0, 0.0) for c in range(cap)]
 
     def summed(values):
         return functools.reduce(
@@ -220,11 +219,13 @@
 
     for j in range(n + 1):
         if j < n:
-            part = summed([packed_ref[:, c * width + j * B : c * width + j * B + B] for c in range(cap)])
+            part = summed([packed_ref[:, 0, c * width + j * B : c * width + j * B + B] for c in range(cap)])
         else:
             part = summed([jnp.ones((rows, B), jnp.float32)] * cap)
         for q in range(groups):
-            out_ref[q, j * keep : j * keep + keep] = part[q * keep : q * keep + keep]
+            all_ref[q, j * keep : j * keep + keep] = part[q * keep : q * keep + keep]
+    for s, out in enumerate(outs):
+        out[...] = all_ref[(at_ref[0] + s) & (groups - 1)]
 
 
 def gram_kernel(n, bit_ref, x_ref, keep_ref, send_ref, all_ref):
@@ -364,20 +365,22 @@
     packed = jnp.concatenate([outgoing, labels], axis=1).reshape(owners, 1, CAP * width + B)
     summed, packed = lax.optimization_barrier((x_sum(pieces), packed))
     mine, other, packed = gram_sum(summed, packed)
-    cut_at = 3
+    cut_at = 4
     early_panel, early_inv, early_link, left, x_blocks = early(bit, mine, other, embeddings, total, cut_at)
     packed, early_inv = lax.optimization_barrier((packed, early_inv))
     groups = lax.axis_size("x")
     keep = per_owner // groups
-    packed = packed.reshape(owners, CAP * width + B)
-    kernel = functools.partial(sums_kernel, CAP, n, groups)
-    [sums] = local_call(kernel, [f32(groups, (n + 1) * keep, B)], [packed], "sums", flops=400_000_000)
-    sums = lax.all_to_all(sums, "x", 0, 0, tiled=True)
-    whitened, late_panel, late_inv, late_link = late(early_inv, left, x_blocks, cut_at)
-    sums, late_inv = lax.optimization_barrier((sums, late_inv))
+    kernel = functools.partial(sums_kernel, CAP, n)
+    piece = ((n + 1) * keep, B)
+    sums = local_call(
+        kernel, [f32(*piece)] * groups, [index("x"), packed], "sums", [(groups, *piece)], flops=400_000_000, scalars=1
+    )
+    sums = [sums[0]] + [shifted(sums[s], "x", s) for s in range(1, groups)]
+    whitened, *late_parts = late(early_inv, left, x_blocks, cut_at)
+    *sums, late_parts[1] = lax.optimization_barrier((*sums, late_parts[1]))
     kernel = functools.partial(means_kernel, n, cut_at)
-    panels = [sums, early_panel, early_inv, early_link, late_panel, late_inv, late_link]
-    [means] = local_call(kernel, [f32(keep, width)], panels, "means", flops=400_000_000)
+    parts = [early_panel, early_inv, early_link, *late_parts, *sums]
+    [means] = local_call(kernel, [f32(keep, width)], parts, "means", flops=400_000_000)
     return whitened, means
 
 

time: 137 us -> 137 us (level)
  starting transfers between devices: 46.6 us -> 51.2 us
  waiting for transfers between devices: 13.2 us -> 9.63 us
    ppermute x6 -> x9, starting transfers between devices: 19.7 us -> 28.9 us  [shifted(): lax.ppermute(value, axis, [(i, (i + by) % size) for i in range(size)])]
    all_to_all x1 -> x0, starting transfers between devices: 3.61 us -> none  [body(): sums = lax.all_to_all(sums, 'x', 0, 0, tiled=True)]
    all_to_all x1, waiting for transfers between devices: 6.42 us -> 3.11 us  [gram_sum(): packed = lax.all_to_all(packed, ('z', 'y', 'core'), 0, 0, tiled=True)]
    ppermute x6 -> x9, waiting for transfers between devices: 4.93 us -> 4.95 us  [shifted(): lax.ppermute(value, axis, [(i, (i + by) % size) for i in range(size)])]
  transfers between devices with their start and end apart: 10 -> 12, of which waited for: 5 -> 4; matrix products, arithmetic and copies ran while one was open for 3% -> 3% of each run, Pallas kernels for 18% -> 18%
where the time goes in v7:
time: 137 us; the launch traced here: 136 us
  starting transfers between devices  51.2 us (37%)
  blocking collectives  39.2 us (29%)
  Pallas kernels  30.3 us (22%)
  waiting for transfers between devices  9.63 us (7%)
  local copies, waits for them, and re-layouts  3.82 us (3%)
    ppermute x9, starting transfers between devices, shifted(): lax.ppermute(value, axis, [(i, (i + by) % size) for i in range(size)])  28.9 us
    pallas_call x4, Pallas kernels, local_call(): pl.pallas_call(kernel, out_shape=outs, in_specs=[SCALAR] * scalars + [VME...  28.7 us
    all_to_all x2, blocking collectives, spread(): return lax.all_to_all(copies, axis, 0, 0, tiled=True)  28.2 us
    ppermute x2, starting transfers between devices, swapped(): lax.ppermute(value, axis, [(i, i ^ by) for i in range(lax.axis_size(axis))])  11.9 us
    all_to_all x1, blocking collectives, reduced(): return jnp.sum(lax.all_to_all(pieces, axis, 0, 0, tiled=True), axis=0)  11 us
    all_to_all x1, starting transfers between devices, gram_sum(): packed = lax.all_to_all(packed, ('z', 'y', 'core'), 0, 0, tiled=True)  10.4 us
    ppermute x9, waiting for transfers between devices, shifted(): lax.ppermute(value, axis, [(i, (i + by) % size) for i in range(size)])  4.95 us
    all_to_all x1, waiting for transfers between devices, gram_sum(): packed = lax.all_to_all(packed, ('z', 'y', 'core'), 0, 0, tiled=True)  3.11 us
  transfers between devices with their start and end apart: 12, of which 4 were waited for; matrix products, arithmetic and copies ran while one was open for 3% of the time, Pallas kernels for 18%

profile of v7, /device:TPU:1, one launch (start us, length us, event | category | flops | bytes accessed | tf_op | source)
XLA Modules:
  0.0 136.0 jit_solution(6233913836807818731)
XLA Ops:
  1.6 1.4 %gram.1 = (f32[1344,128]{1,0:T(8,128)S(1)}, f32[1344,128]{1,0:T(8,128)S(1)}) custom-call(s32[1]{0:T(128)} %bitcast.1.bit_ref, f32[128,768]{1,0:T(8,128)S(1)} %copy-done), custom_call_target="tpu_custom_call" | custom-call | flops 700000000 | bytes 2000000 | tf_op jit(solution)/shard_map/gram/pallas_call | solution.py:246
  3.0 8.8 %collective-permute-start = (f32[1344,128]{1,0:T(8,128)S(1)}, f32[1344,128]{1,0:T(8,128)S(1)}, u32[]{:S(2)}, u32[]{:S(2)}) collective-permute-start(f32[1344,128]{1,0:T(8,128)S(1)} %get-tuple-element.34), channel_id=1, source_target_pairs={{0,4},{4,0},{1,5},{5,1},{2,6},{6,2},{3,7},{7,3},{8,12},{12,8},{9,1... | collective-permute-start | bytes 2064392 | tf_op jit(solution)/shard_map/ppermute | solution.py:306
  14.1 2.1 %collective-permute-start.1 = (f32[336,128]{1,0:T(8,128)S(1)}, f32[336,128]{1,0:T(8,128)S(1)}, u32[]{:S(2)}, u32[]{:S(2)}) collective-permute-start(f32[336,128]{1,0:T(8,128)S(1)} %get-tuple-element.36), channel_id=1, source_target_pairs={{0,1},{1,2},{2,3},{3,0},{4,5},{5,6},{6,7},{7,4},{8,9},{9,10},{10,1... | collective-permute-start | bytes 516104 | tf_op jit(solution)/shard_map/ppermute | solution.py:302
  16.1 1.9 %collective-permute-start.2 = (f32[336,128]{1,0:T(8,128)S(1)}, f32[336,128]{1,0:T(8,128)S(1)}, u32[]{:S(2)}, u32[]{:S(2)}) collective-permute-start(f32[336,128]{1,0:T(8,128)S(1)} %get-tuple-element.37), channel_id=1, source_target_pairs={{0,2},{1,3},{2,0},{3,1},{4,6},{5,7},{6,4},{7,5},{8,10},{9,11},{10,... | collective-permute-start | bytes 516104 | tf_op jit(solution)/shard_map/ppermute | solution.py:302
  18.1 4.6 %collective-permute-start.3 = (f32[336,128]{1,0:T(8,128)S(1)}, f32[336,128]{1,0:T(8,128)S(1)}, u32[]{:S(2)}, u32[]{:S(2)}) collective-permute-start(f32[336,128]{1,0:T(8,128)S(1)} %get-tuple-element.38), channel_id=1, source_target_pairs={{0,3},{1,0},{2,1},{3,2},{4,7},{5,4},{6,5},{7,6},{8,11},{9,8},{10,9... | collective-permute-start | bytes 516104 | tf_op jit(solution)/shard_map/ppermute | solution.py:302
  22.7 1.5 %reshape.38 = f32[128,1,1664]{2,1,0:T(1,128)} reshape(f32[128,1664]{1,0:T(8,128)S(1)} %select_maximum_fusion) | data formatting | bytes 1703936 | tf_op jit(solution)/shard_map/reshape | solution.py:365
  24.2 2.8 %collective-permute-done.1 = f32[336,128]{1,0:T(8,128)S(1)} collective-permute-done((f32[336,128]{1,0:T(8,128)S(1)}, f32[336,128]{1,0:T(8,128)S(1)}, u32[]{:S(2)}, u32[]{:S(2)}) %collective-permute-start.1) | collective-permute-done | bytes 172064 | tf_op jit(solution)/shard_map/ppermute | solution.py:302
  27.0 2.2 %collective-permute-done.3 = f32[336,128]{1,0:T(8,128)S(1)} collective-permute-done((f32[336,128]{1,0:T(8,128)S(1)}, f32[336,128]{1,0:T(8,128)S(1)}, u32[]{:S(2)}, u32[]{:S(2)}) %collective-permute-start.3) | collective-permute-done | bytes 172064 | tf_op jit(solution)/shard_map/ppermute | solution.py:302
  29.2 11.0 %all_to_all.20 = f32[8,42,128]{2,1,0:T(8,128)S(1)} all-to-all(f32[8,42,128]{2,1,0:T(8,128)S(1)} %reshape.39), channel_id=1, replica_groups=mesh['z'=8,'y'=8,'core'=2,'x'=4] {'y'}, dimensions={0} | all-to-all | bytes 344064 | tf_op jit(solution)/shard_map/all_to_all | solution.py:314
  40.3 17.2 %all_to_all.21 = f32[8,42,128]{2,1,0:T(8,128)S(1)} all-to-all(f32[8,42,128]{2,1,0:T(8,128)S(1)} %broadcast_in_dim.18), channel_id=1, replica_groups=mesh['z'=8,'y'=8,'core'=2,'x'=4] {'z'}, dimensions={0} | all-to-all | bytes 344064 | tf_op jit(solution)/shard_map/all_to_all | solution.py:319
  57.5 11.0 %all_to_all.22 = f32[8,42,128]{2,1,0:T(8,128)S(1)} all-to-all(f32[8,42,128]{2,1,0:T(8,128)S(1)} %broadcast_in_dim.19), channel_id=1, replica_groups=mesh['z'=8,'y'=8,'core'=2,'x'=4] {'y'}, dimensions={0} | all-to-all | bytes 344064 | tf_op jit(solution)/shard_map/all_to_all | solution.py:319
  68.6 5.5 %collective-permute-start.4 = (f32[336,128]{1,0:T(8,128)S(1)}, f32[336,128]{1,0:T(8,128)S(1)}, u32[]{:S(2)}, u32[]{:S(2)}) collective-permute-start(f32[336,128]{1,0:T(8,128)S(1)} %reshape.40.refs_0_), channel_id=1, source_target_pairs={{0,1},{1,2},{2,3},{3,0},{4,5},{5,6},{6,7},{7,4},{8,9},{9,10},{10,1... | collective-permute-start | bytes 516104 | tf_op jit(solution)/shard_map/ppermute | solution.py:302
  74.1 1.9 %collective-permute-start.6 = (f32[336,128]{1,0:T(8,128)S(1)}, f32[336,128]{1,0:T(8,128)S(1)}, u32[]{:S(2)}, u32[]{:S(2)}) collective-permute-start(f32[336,128]{1,0:T(8,128)S(1)} %reshape.40.refs_0_), channel_id=1, source_target_pairs={{0,3},{1,0},{2,1},{3,2},{4,7},{5,4},{6,5},{7,6},{8,11},{9,8},{10,9... | collective-permute-start | bytes 516104 | tf_op jit(solution)/shard_map/ppermute | solution.py:302
  76.0 3.7 %collective-permute-start.5 = (f32[336,128]{1,0:T(8,128)S(1)}, f32[336,128]{1,0:T(8,128)S(1)}, u32[]{:S(2)}, u32[]{:S(2)}) collective-permute-start(f32[336,128]{1,0:T(8,128)S(1)} %reshape.40.refs_0_), channel_id=1, source_target_pairs={{0,2},{1,3},{2,0},{3,1},{4,6},{5,7},{6,4},{7,5},{8,10},{9,11},{10,... | collective-permute-start | bytes 516104 | tf_op jit(solution)/shard_map/ppermute | solution.py:302
  79.7 10.4 %all-to-all-start.3 = ((f32[128,1,1664]{2,1,0:T(1,128)}), f32[128,1,1664]{2,1,0:T(1,128)S(1)}, u32[]{:S(2)}, u32[]{:S(2)}) async-start(f32[128,1,1664]{2,1,0:T(1,128)} %reshape.38), calls=%async_computation.3 | async-start | bytes 1703936 | tf_op jit(solution)/shard_map/all_to_all | solution.py:337
  90.2 3.1 %collective-permute-start.7 = (f32[1344,128]{1,0:T(8,128)S(1)}, f32[1344,128]{1,0:T(8,128)S(1)}, u32[]{:S(2)}, u32[]{:S(2)}) collective-permute-start(f32[1344,128]{1,0:T(8,128)S(1)} %place_x.1.mine_ref), channel_id=1, source_target_pairs={{0,4},{4,0},{1,5},{5,1},{2,6},{6,2},{3,7},{7,3},{8,12},{12,8},{9,1... | collective-permute-start | bytes 2064392 | tf_op jit(solution)/shard_map/ppermute | solution.py:306
  93.3 1.6 %collective-permute-done.7.other_ref = f32[1344,128]{1,0:T(8,128)S(1)} collective-permute-done((f32[1344,128]{1,0:T(8,128)S(1)}, f32[1344,128]{1,0:T(8,128)S(1)}, u32[]{:S(2)}, u32[]{:S(2)}) %collective-permute-start.7) | collective-permute-done | bytes 688160 | tf_op jit(solution)/shard_map/ppermute | solution.py:306
  94.9 19.3 %early.1 = (f32[1792,128]{1,0:T(8,128)S(1)}, f32[5,128,128]{2,1,0:T(8,128)S(1)}, f32[4,128,128]{2,1,0:T(8,128)S(1)}, f32[384,128]{1,0:T(8,128)S(1)}, f32[6,128,128]{2,1,0:T(8,128)S(1)}) custom-call(s32[1]{0:T(128)} %bitcast.1.bit_ref, f32[1344,128]{1,0:T(8,128)S(1)} %place_x.1.mine_ref, f32[1344,128]{1,0:T(8,128)S(1)} %collective-permute-done.7.other_ref, ...), custom_call_target="tpu_custom_call" | custom-call | flops 10000000000 | bytes 4000000 | tf_op jit(solution)/shard_map/early/pallas_call | solution.py:174
  114.2 3.1 %all-to-all-done.3.packed_ref = f32[128,1,1664]{2,1,0:T(1,128)S(1)} async-done(((f32[128,1,1664]{2,1,0:T(1,128)}), f32[128,1,1664]{2,1,0:T(1,128)S(1)}, u32[]{:S(2)}, u32[]{:S(2)}) %all-to-all-start.3) | async-done | bytes 852000 | tf_op jit(solution)/shard_map/all_to_all | solution.py:337
  118.7 2.5 %collective-permute-start.8 = (f32[224,128]{1,0:T(8,128)S(1)}, f32[224,128]{1,0:T(8,128)S(1)}, u32[]{:S(2)}, u32[]{:S(2)}) collective-permute-start(f32[224,128]{1,0:T(8,128)S(1)} %get-tuple-element.54), channel_id=1, source_target_pairs={{0,1},{1,2},{2,3},{3,0},{4,5},{5,6},{6,7},{7,4},{8,9},{9,10},{10,1... | collective-permute-start | bytes 344072 | tf_op jit(solution)/shard_map/ppermute | solution.py:302
  121.1 4.9 %collective-permute-start.9 = (f32[224,128]{1,0:T(8,128)S(1)}, f32[224,128]{1,0:T(8,128)S(1)}, u32[]{:S(2)}, u32[]{:S(2)}) collective-permute-start(f32[224,128]{1,0:T(8,128)S(1)} %get-tuple-element.55), channel_id=1, source_target_pairs={{0,2},{1,3},{2,0},{3,1},{4,6},{5,7},{6,4},{7,5},{8,10},{9,11},{10,... | collective-permute-start | bytes 344072 | tf_op jit(solution)/shard_map/ppermute | solution.py:302
  126.0 1.9 %collective-permute-start.10 = (f32[224,128]{1,0:T(8,128)S(1)}, f32[224,128]{1,0:T(8,128)S(1)}, u32[]{:S(2)}, u32[]{:S(2)}) collective-permute-start(f32[224,128]{1,0:T(8,128)S(1)} %get-tuple-element.56), channel_id=1, source_target_pairs={{0,3},{1,0},{2,1},{3,2},{4,7},{5,4},{6,5},{7,6},{8,11},{9,8},{10,9... | collective-permute-start | bytes 344072 | tf_op jit(solution)/shard_map/ppermute | solution.py:302
  127.9 4.7 %late.1 = (f32[128,768]{1,0:T(8,128)}, f32[128,128]{1,0:T(8,128)S(1)}, f32[2,128,128]{2,1,0:T(8,128)S(1)}, f32[1,128,128]{2,1,0:T(8,128)S(1)}) custom-call(f32[5,128,128]{2,1,0:T(8,128)S(1)} %get-tuple-element.45.inv_in.inv0, f32[384,128]{1,0:T(8,128)S(1)} %get-tuple-element.46.left_ref, f32[6,128,128]{2,1,0:T(8,128)S(1)} %get-tuple-element.47.x_in), custom_call_target="tpu_custom_call" | custom-call | flops 10000000000 | bytes 4000000 | tf_op jit(solution)/shard_map/late/pallas_call | solution.py:174
  132.7 3.4 %means.1 = f32[32,768]{1,0:T(8,128)} custom-call(f32[1792,128]{1,0:T(8,128)S(1)} %get-tuple-element.49.panel0, f32[5,128,128]{2,1,0:T(8,128)S(1)} %get-tuple-element.45.inv_in.inv0, f32[4,128,128]{2,1,0:T(8,128)S(1)} %get-tuple-element.50.link0, f32[128,128]{1,0:T(8,128)S(1)} %get-tuple-element.51.panel1, f32[2,128,128]{2,1,0:T(8,128)S(1)} %get-tuple-element.58.inv1, ...), custom_call_target="tpu_custom_call" | custom-call | flops 400000000 | bytes 4000000 | tf_op jit(solution)/shard_map/means/pallas_call | solution.py:174
  (35 shorter events, 4.8 us)
Async XLA Ops:
  0.6 1.0 copy-start
  1.6 10.7 %copy-start.1 = (f32[128,768]{1,0:T(8,128)S(1)}, f32[128,768]{1,0:T(8,128)}, u32[]{:S(2)}) copy-start(f32[128,768]{1,0:T(8,128)} %x_ref.3) | copy-start | bytes 1179652
  3.0 8.8 %copy-start.3 = (s32[128]{0:T(128)S(1)}, s32[128]{0:T(128)}, u32[]{:S(2)}) copy-start(s32[128]{0:T(128)} %param.3) | copy-start | bytes 1540
  3.0 10.9 %collective-permute-start = (f32[1344,128]{1,0:T(8,128)S(1)}, f32[1344,128]{1,0:T(8,128)S(1)}, u32[]{:S(2)}, u32[]{:S(2)}) collective-permute-start(f32[1344,128]{1,0:T(8,128)S(1)} %get-tuple-element.34), channel_id=1, source_target_pairs={{0,4},{4,0},{1,5},{5,1},{2,6},{6,2},{3,7},{7,3},{8,12},{12,8},{9,1... | collective-permute-start | bytes 2064392 | tf_op jit(solution)/shard_map/ppermute | solution.py:306
  13.9 8.7 %copy-start.2 = (f32[128,1536]{1,0:T(8,128)S(1)}, f32[128,1536]{1,0:T(8,128)}, u32[]{:S(2)}) copy-start(f32[128,1536]{1,0:T(8,128)} %reshape.37) | copy-start | bytes 2359300
  14.1 12.9 %collective-permute-start.1 = (f32[336,128]{1,0:T(8,128)S(1)}, f32[336,128]{1,0:T(8,128)S(1)}, u32[]{:S(2)}, u32[]{:S(2)}) collective-permute-start(f32[336,128]{1,0:T(8,128)S(1)} %get-tuple-element.36), channel_id=1, source_target_pairs={{0,1},{1,2},{2,3},{3,0},{4,5},{5,6},{6,7},{7,4},{8,9},{9,10},{10,1... | collective-permute-start | bytes 516104 | tf_op jit(solution)/shard_map/ppermute | solution.py:302
  16.1 10.9 %collective-permute-start.2 = (f32[336,128]{1,0:T(8,128)S(1)}, f32[336,128]{1,0:T(8,128)S(1)}, u32[]{:S(2)}, u32[]{:S(2)}) collective-permute-start(f32[336,128]{1,0:T(8,128)S(1)} %get-tuple-element.37), channel_id=1, source_target_pairs={{0,2},{1,3},{2,0},{3,1},{4,6},{5,7},{6,4},{7,5},{8,10},{9,11},{10,... | collective-permute-start | bytes 516104 | tf_op jit(solution)/shard_map/ppermute | solution.py:302
  18.1 11.1 %collective-permute-start.3 = (f32[336,128]{1,0:T(8,128)S(1)}, f32[336,128]{1,0:T(8,128)S(1)}, u32[]{:S(2)}, u32[]{:S(2)}) collective-permute-start(f32[336,128]{1,0:T(8,128)S(1)} %get-tuple-element.38), channel_id=1, source_target_pairs={{0,3},{1,0},{2,1},{3,2},{4,7},{5,4},{6,5},{7,6},{8,11},{9,8},{10,9... | collective-permute-start | bytes 516104 | tf_op jit(solution)/shard_map/ppermute | solution.py:302
  68.6 11.2 %collective-permute-start.4 = (f32[336,128]{1,0:T(8,128)S(1)}, f32[336,128]{1,0:T(8,128)S(1)}, u32[]{:S(2)}, u32[]{:S(2)}) collective-permute-start(f32[336,128]{1,0:T(8,128)S(1)} %reshape.40.refs_0_), channel_id=1, source_target_pairs={{0,1},{1,2},{2,3},{3,0},{4,5},{5,6},{6,7},{7,4},{8,9},{9,10},{10,1... | collective-permute-start | bytes 516104 | tf_op jit(solution)/shard_map/ppermute | solution.py:302
  74.1 16.1 %collective-permute-start.6 = (f32[336,128]{1,0:T(8,128)S(1)}, f32[336,128]{1,0:T(8,128)S(1)}, u32[]{:S(2)}, u32[]{:S(2)}) collective-permute-start(f32[336,128]{1,0:T(8,128)S(1)} %reshape.40.refs_0_), channel_id=1, source_target_pairs={{0,3},{1,0},{2,1},{3,2},{4,7},{5,4},{6,5},{7,6},{8,11},{9,8},{10,9... | collective-permute-start | bytes 516104 | tf_op jit(solution)/shard_map/ppermute | solution.py:302
  76.0 14.1 %collective-permute-start.5 = (f32[336,128]{1,0:T(8,128)S(1)}, f32[336,128]{1,0:T(8,128)S(1)}, u32[]{:S(2)}, u32[]{:S(2)}) collective-permute-start(f32[336,128]{1,0:T(8,128)S(1)} %reshape.40.refs_0_), channel_id=1, source_target_pairs={{0,2},{1,3},{2,0},{3,1},{4,6},{5,7},{6,4},{7,5},{8,10},{9,11},{10,... | collective-permute-start | bytes 516104 | tf_op jit(solution)/shard_map/ppermute | solution.py:302
  79.7 37.6 %all-to-all-start.3 = ((f32[128,1,1664]{2,1,0:T(1,128)}), f32[128,1,1664]{2,1,0:T(1,128)S(1)}, u32[]{:S(2)}, u32[]{:S(2)}) async-start(f32[128,1,1664]{2,1,0:T(1,128)} %reshape.38), calls=%async_computation.3 | async-start | bytes 1703936 | tf_op jit(solution)/shard_map/all_to_all | solution.py:337
  90.2 4.7 %collective-permute-start.7 = (f32[1344,128]{1,0:T(8,128)S(1)}, f32[1344,128]{1,0:T(8,128)S(1)}, u32[]{:S(2)}, u32[]{:S(2)}) collective-permute-start(f32[1344,128]{1,0:T(8,128)S(1)} %place_x.1.mine_ref), channel_id=1, source_target_pairs={{0,4},{4,0},{1,5},{5,1},{2,6},{6,2},{3,7},{7,3},{8,12},{12,8},{9,1... | collective-permute-start | bytes 2064392 | tf_op jit(solution)/shard_map/ppermute | solution.py:306
  118.7 14.0 %collective-permute-start.8 = (f32[224,128]{1,0:T(8,128)S(1)}, f32[224,128]{1,0:T(8,128)S(1)}, u32[]{:S(2)}, u32[]{:S(2)}) collective-permute-start(f32[224,128]{1,0:T(8,128)S(1)} %get-tuple-element.54), channel_id=1, source_target_pairs={{0,1},{1,2},{2,3},{3,0},{4,5},{5,6},{6,7},{7,4},{8,9},{9,10},{10,1... | collective-permute-start | bytes 344072 | tf_op jit(solution)/shard_map/ppermute | solution.py:302
  121.1 11.5 %collective-permute-start.9 = (f32[224,128]{1,0:T(8,128)S(1)}, f32[224,128]{1,0:T(8,128)S(1)}, u32[]{:S(2)}, u32[]{:S(2)}) collective-permute-start(f32[224,128]{1,0:T(8,128)S(1)} %get-tuple-element.55), channel_id=1, source_target_pairs={{0,2},{1,3},{2,0},{3,1},{4,6},{5,7},{6,4},{7,5},{8,10},{9,11},{10,... | collective-permute-start | bytes 344072 | tf_op jit(solution)/shard_map/ppermute | solution.py:302
  126.0 6.7 %collective-permute-start.10 = (f32[224,128]{1,0:T(8,128)S(1)}, f32[224,128]{1,0:T(8,128)S(1)}, u32[]{:S(2)}, u32[]{:S(2)}) collective-permute-start(f32[224,128]{1,0:T(8,128)S(1)} %get-tuple-element.56), channel_id=1, source_target_pairs={{0,3},{1,0},{2,1},{3,2},{4,7},{5,4},{6,5},{7,6},{8,11},{9,8},{10,9... | collective-permute-start | bytes 344072 | tf_op jit(solution)/shard_map/ppermute | solution.py:302

commit v8 on v7

--- a/solution.py
+++ b/solution.py
@@ -197,7 +197,7 @@
     panels = sum(n - 1 - t for t in range(cut_at, n)) * B
     outs = [f32(rows, n * B), f32(panels, B), f32(n - cut_at, B, B), f32(n - 1 - cut_at, B, B)]
     kernel = functools.partial(late_kernel, n, cut_at)
-    return local_call(kernel, outs, [inv, left, x_blocks], "late", [left.shape, x_blocks.shape])
+    return local_call(kernel, outs, [inv, left, x_blocks], "late", [left.shape, x_blocks.shape], flops=100_000_000)
 
 
 def sums_kernel(cap, n, at_ref, packed_ref, *refs):
@@ -367,7 +367,8 @@
     mine, other, packed = gram_sum(summed, packed)
     cut_at = 4
     early_panel, early_inv, early_link, left, x_blocks = early(bit, mine, other, embeddings, total, cut_at)
-    packed, early_inv = lax.optimization_barrier((packed, early_inv))
+    whitened, *late_parts = late(early_inv, left, x_blocks, cut_at)
+    packed, late_parts[1] = lax.optimization_barrier((packed, late_parts[1]))
     groups = lax.axis_size("x")
     keep = per_owner // groups
     kernel = functools.partial(sums_kernel, CAP, n)
@@ -376,8 +377,6 @@
         kernel, [f32(*piece)] * groups, [index("x"), packed], "sums", [(groups, *piece)], flops=400_000_000, scalars=1
     )
     sums = [sums[0]] + [shifted(sums[s], "x", s) for s in range(1, groups)]
-    whitened, *late_parts = late(early_inv, left, x_blocks, cut_at)
-    *sums, late_parts[1] = lax.optimization_barrier((*sums, late_parts[1]))
     kernel = functools.partial(means_kernel, n, cut_at)
     parts = [early_panel, early_inv, early_link, *late_parts, *sums]
     [means] = local_call(kernel, [f32(keep, width)], parts, "means", flops=400_000_000)

time: 137 us -> 137 us (level)
    ppermute x9, waiting for transfers between devices: 4.95 us -> 8.54 us  [shifted(): lax.ppermute(value, axis, [(i, (i + by) % size) for i in range(size)])]
    all_to_all x1, waiting for transfers between devices: 3.11 us -> 0.01 us  [gram_sum(): packed = lax.all_to_all(packed, ('z', 'y', 'core'), 0, 0, tiled=True)]
  transfers between devices with their start and end apart: 12 -> 12, of which waited for: 4 -> 5; matrix products, arithmetic and copies ran while one was open for 3% -> 3% of each run, Pallas kernels for 18% -> 18%
where the time goes in v8:
time: 137 us
  starting transfers between devices  51.2 us (37%)
  blocking collectives  39.2 us (29%)
  Pallas kernels  30.3 us (22%)
  waiting for transfers between devices  10.1 us (7%)
  local copies, waits for them, and re-layouts  3.82 us (3%)
    ppermute x9, starting transfers between devices, shifted(): lax.ppermute(value, axis, [(i, (i + by) % size) for i in range(size)])  28.9 us
    pallas_call x4, Pallas kernels, local_call(): pl.pallas_call(kernel, out_shape=outs, in_specs=[SCALAR] * scalars + [VME...  28.7 us
    all_to_all x2, blocking collectives, spread(): return lax.all_to_all(copies, axis, 0, 0, tiled=True)  28.2 us
    ppermute x2, starting transfers between devices, swapped(): lax.ppermute(value, axis, [(i, i ^ by) for i in range(lax.axis_size(axis))])  11.9 us
    all_to_all x1, blocking collectives, reduced(): return jnp.sum(lax.all_to_all(pieces, axis, 0, 0, tiled=True), axis=0)  11 us
    all_to_all x1, starting transfers between devices, gram_sum(): packed = lax.all_to_all(packed, ('z', 'y', 'core'), 0, 0, tiled=True)  10.4 us
    ppermute x9, waiting for transfers between devices, shifted(): lax.ppermute(value, axis, [(i, (i + by) % size) for i in range(size)])  8.54 us
  transfers between devices with their start and end apart: 12, of which 5 were waited for; matrix products, arithmetic and copies ran while one was open for 3% of the time, Pallas kernels for 18%

profile of v8, /device:TPU:1, one launch (start us, length us, event | category | flops | bytes accessed | tf_op | source)
XLA Modules:
  0.0 136.5 jit_solution(12266586305934192054)
XLA Ops:
  3.0 8.8 %collective-permute-start = (f32[1344,128]{1,0:T(8,128)S(1)}, f32[1344,128]{1,0:T(8,128)S(1)}, u32[]{:S(2)}, u32[]{:S(2)}) collective-permute-start(f32[1344,128]{1,0:T(8,128)S(1)} %get-tuple-element.29), channel_id=1, source_target_pairs={{0,4},{4,0},{1,5},{5,1},{2,6},{6,2},{3,7},{7,3},{8,12},{12,8},{9,1... | collective-permute-start | bytes 2064392 | tf_op jit(solution)/shard_map/ppermute | solution.py:306
  14.1 2.1 %collective-permute-start.1 = (f32[336,128]{1,0:T(8,128)S(1)}, f32[336,128]{1,0:T(8,128)S(1)}, u32[]{:S(2)}, u32[]{:S(2)}) collective-permute-start(f32[336,128]{1,0:T(8,128)S(1)} %get-tuple-element.31), channel_id=1, source_target_pairs={{0,1},{1,2},{2,3},{3,0},{4,5},{5,6},{6,7},{7,4},{8,9},{9,10},{10,1... | collective-permute-start | bytes 516104 | tf_op jit(solution)/shard_map/ppermute | solution.py:302
  16.1 1.9 %collective-permute-start.2 = (f32[336,128]{1,0:T(8,128)S(1)}, f32[336,128]{1,0:T(8,128)S(1)}, u32[]{:S(2)}, u32[]{:S(2)}) collective-permute-start(f32[336,128]{1,0:T(8,128)S(1)} %get-tuple-element.32), channel_id=1, source_target_pairs={{0,2},{1,3},{2,0},{3,1},{4,6},{5,7},{6,4},{7,5},{8,10},{9,11},{10,... | collective-permute-start | bytes 516104 | tf_op jit(solution)/shard_map/ppermute | solution.py:302
  18.1 4.6 %collective-permute-start.3 = (f32[336,128]{1,0:T(8,128)S(1)}, f32[336,128]{1,0:T(8,128)S(1)}, u32[]{:S(2)}, u32[]{:S(2)}) collective-permute-start(f32[336,128]{1,0:T(8,128)S(1)} %get-tuple-element.33), channel_id=1, source_target_pairs={{0,3},{1,0},{2,1},{3,2},{4,7},{5,4},{6,5},{7,6},{8,11},{9,8},{10,9... | collective-permute-start | bytes 516104 | tf_op jit(solution)/shard_map/ppermute | solution.py:302
  22.7 1.5 %reshape.38 = f32[128,1,1664]{2,1,0:T(1,128)} reshape(f32[128,1664]{1,0:T(8,128)S(1)} %select_maximum_fusion) | data formatting | bytes 1703936 | tf_op jit(solution)/shard_map/reshape | solution.py:365
  24.2 2.8 %collective-permute-done.1 = f32[336,128]{1,0:T(8,128)S(1)} collective-permute-done((f32[336,128]{1,0:T(8,128)S(1)}, f32[336,128]{1,0:T(8,128)S(1)}, u32[]{:S(2)}, u32[]{:S(2)}) %collective-permute-start.1) | collective-permute-done | bytes 172064 | tf_op jit(solution)/shard_map/ppermute | solution.py:302
  27.0 2.2 %collective-permute-done.3 = f32[336,128]{1,0:T(8,128)S(1)} collective-permute-done((f32[336,128]{1,0:T(8,128)S(1)}, f32[336,128]{1,0:T(8,128)S(1)}, u32[]{:S(2)}, u32[]{:S(2)}) %collective-permute-start.3) | collective-permute-done | bytes 172064 | tf_op jit(solution)/shard_map/ppermute | solution.py:302
  29.2 11.0 %all_to_all.20 = f32[8,42,128]{2,1,0:T(8,128)S(1)} all-to-all(f32[8,42,128]{2,1,0:T(8,128)S(1)} %reshape.39), channel_id=1, replica_groups=mesh['z'=8,'y'=8,'core'=2,'x'=4] {'y'}, dimensions={0} | all-to-all | bytes 344064 | tf_op jit(solution)/shard_map/all_to_all | solution.py:314
  40.3 17.2 %all_to_all.21 = f32[8,42,128]{2,1,0:T(8,128)S(1)} all-to-all(f32[8,42,128]{2,1,0:T(8,128)S(1)} %broadcast_in_dim.18), channel_id=1, replica_groups=mesh['z'=8,'y'=8,'core'=2,'x'=4] {'z'}, dimensions={0} | all-to-all | bytes 344064 | tf_op jit(solution)/shard_map/all_to_all | solution.py:319
  57.5 11.0 %all_to_all.22 = f32[8,42,128]{2,1,0:T(8,128)S(1)} all-to-all(f32[8,42,128]{2,1,0:T(8,128)S(1)} %broadcast_in_dim.19), channel_id=1, replica_groups=mesh['z'=8,'y'=8,'core'=2,'x'=4] {'y'}, dimensions={0} | all-to-all | bytes 344064 | tf_op jit(solution)/shard_map/all_to_all | solution.py:319
  68.6 5.5 %collective-permute-start.4 = (f32[336,128]{1,0:T(8,128)S(1)}, f32[336,128]{1,0:T(8,128)S(1)}, u32[]{:S(2)}, u32[]{:S(2)}) collective-permute-start(f32[336,128]{1,0:T(8,128)S(1)} %reshape.40.refs_0_), channel_id=1, source_target_pairs={{0,1},{1,2},{2,3},{3,0},{4,5},{5,6},{6,7},{7,4},{8,9},{9,10},{10,1... | collective-permute-start | bytes 516104 | tf_op jit(solution)/shard_map/ppermute | solution.py:302
  74.1 1.9 %collective-permute-start.6 = (f32[336,128]{1,0:T(8,128)S(1)}, f32[336,128]{1,0:T(8,128)S(1)}, u32[]{:S(2)}, u32[]{:S(2)}) collective-permute-start(f32[336,128]{1,0:T(8,128)S(1)} %reshape.40.refs_0_), channel_id=1, source_target_pairs={{0,3},{1,0},{2,1},{3,2},{4,7},{5,4},{6,5},{7,6},{8,11},{9,8},{10,9... | collective-permute-start | bytes 516104 | tf_op jit(solution)/shard_map/ppermute | solution.py:302
  76.0 3.7 %collective-permute-start.5 = (f32[336,128]{1,0:T(8,128)S(1)}, f32[336,128]{1,0:T(8,128)S(1)}, u32[]{:S(2)}, u32[]{:S(2)}) collective-permute-start(f32[336,128]{1,0:T(8,128)S(1)} %reshape.40.refs_0_), channel_id=1, source_target_pairs={{0,2},{1,3},{2,0},{3,1},{4,6},{5,7},{6,4},{7,5},{8,10},{9,11},{10,... | collective-permute-start | bytes 516104 | tf_op jit(solution)/shard_map/ppermute | solution.py:302
  79.7 10.4 %all-to-all-start.3 = ((f32[128,1,1664]{2,1,0:T(1,128)}), f32[128,1,1664]{2,1,0:T(1,128)S(1)}, u32[]{:S(2)}, u32[]{:S(2)}) async-start(f32[128,1,1664]{2,1,0:T(1,128)} %reshape.38), calls=%async_computation.3 | async-start | bytes 1703936 | tf_op jit(solution)/shard_map/all_to_all | solution.py:337
  90.2 3.1 %collective-permute-start.7 = (f32[1344,128]{1,0:T(8,128)S(1)}, f32[1344,128]{1,0:T(8,128)S(1)}, u32[]{:S(2)}, u32[]{:S(2)}) collective-permute-start(f32[1344,128]{1,0:T(8,128)S(1)} %place_x.1.mine_ref), channel_id=1, source_target_pairs={{0,4},{4,0},{1,5},{5,1},{2,6},{6,2},{3,7},{7,3},{8,12},{12,8},{9,1... | collective-permute-start | bytes 2064392 | tf_op jit(solution)/shard_map/ppermute | solution.py:306
  93.3 1.6 %collective-permute-done.7.other_ref = f32[1344,128]{1,0:T(8,128)S(1)} collective-permute-done((f32[1344,128]{1,0:T(8,128)S(1)}, f32[1344,128]{1,0:T(8,128)S(1)}, u32[]{:S(2)}, u32[]{:S(2)}) %collective-permute-start.7) | collective-permute-done | bytes 688160 | tf_op jit(solution)/shard_map/ppermute | solution.py:306
  94.9 19.3 %early.1 = (f32[1792,128]{1,0:T(8,128)S(1)}, f32[5,128,128]{2,1,0:T(8,128)S(1)}, f32[4,128,128]{2,1,0:T(8,128)S(1)}, f32[384,128]{1,0:T(8,128)S(1)}, f32[6,128,128]{2,1,0:T(8,128)S(1)}) custom-call(s32[1]{0:T(128)} %bitcast.bit_ref, f32[1344,128]{1,0:T(8,128)S(1)} %place_x.1.mine_ref, f32[1344,128]{1,0:T(8,128)S(1)} %collective-permute-done.7.other_ref, ...), custom_call_target="tpu_custom_call" | custom-call | flops 10000000000 | bytes 4000000 | tf_op jit(solution)/shard_map/early/pallas_call | solution.py:174
  114.2 4.7 %late.1 = (f32[128,768]{1,0:T(8,128)}, f32[128,128]{1,0:T(8,128)S(1)}, f32[2,128,128]{2,1,0:T(8,128)S(1)}, f32[1,128,128]{2,1,0:T(8,128)S(1)}) custom-call(f32[5,128,128]{2,1,0:T(8,128)S(1)} %get-tuple-element.38.inv_in.inv0, f32[384,128]{1,0:T(8,128)S(1)} %get-tuple-element.39.left_ref, f32[6,128,128]{2,1,0:T(8,128)S(1)} %get-tuple-element.40.x_in), custom_call_target="tpu_custom_call" | custom-call | flops 100000000 | bytes 4000000 | tf_op jit(solution)/shard_map/late/pallas_call | solution.py:174
  120.3 2.5 %collective-permute-start.8 = (f32[224,128]{1,0:T(8,128)S(1)}, f32[224,128]{1,0:T(8,128)S(1)}, u32[]{:S(2)}, u32[]{:S(2)}) collective-permute-start(f32[224,128]{1,0:T(8,128)S(1)} %get-tuple-element.51), channel_id=1, source_target_pairs={{0,1},{1,2},{2,3},{3,0},{4,5},{5,6},{6,7},{7,4},{8,9},{9,10},{10,1... | collective-permute-start | bytes 344072 | tf_op jit(solution)/shard_map/ppermute | solution.py:302
  122.8 4.9 %collective-permute-start.9 = (f32[224,128]{1,0:T(8,128)S(1)}, f32[224,128]{1,0:T(8,128)S(1)}, u32[]{:S(2)}, u32[]{:S(2)}) collective-permute-start(f32[224,128]{1,0:T(8,128)S(1)} %get-tuple-element.52), channel_id=1, source_target_pairs={{0,2},{1,3},{2,0},{3,1},{4,6},{5,7},{6,4},{7,5},{8,10},{9,11},{10,... | collective-permute-start | bytes 344072 | tf_op jit(solution)/shard_map/ppermute | solution.py:302
  127.6 1.9 %collective-permute-start.10 = (f32[224,128]{1,0:T(8,128)S(1)}, f32[224,128]{1,0:T(8,128)S(1)}, u32[]{:S(2)}, u32[]{:S(2)}) collective-permute-start(f32[224,128]{1,0:T(8,128)S(1)} %get-tuple-element.53), channel_id=1, source_target_pairs={{0,3},{1,0},{2,1},{3,2},{4,7},{5,4},{6,5},{7,6},{8,11},{9,8},{10,9... | collective-permute-start | bytes 344072 | tf_op jit(solution)/shard_map/ppermute | solution.py:302
  129.6 1.7 %collective-permute-done.9.refs_2_ = f32[224,128]{1,0:T(8,128)S(1)} collective-permute-done((f32[224,128]{1,0:T(8,128)S(1)}, f32[224,128]{1,0:T(8,128)S(1)}, u32[]{:S(2)}, u32[]{:S(2)}) %collective-permute-start.9) | collective-permute-done | bytes 114720 | tf_op jit(solution)/shard_map/ppermute | solution.py:302
  131.3 1.9 %collective-permute-done.10.refs_3_ = f32[224,128]{1,0:T(8,128)S(1)} collective-permute-done((f32[224,128]{1,0:T(8,128)S(1)}, f32[224,128]{1,0:T(8,128)S(1)}, u32[]{:S(2)}, u32[]{:S(2)}) %collective-permute-start.10) | collective-permute-done | bytes 114720 | tf_op jit(solution)/shard_map/ppermute | solution.py:302
  133.2 3.3 %means.1 = f32[32,768]{1,0:T(8,128)} custom-call(f32[1792,128]{1,0:T(8,128)S(1)} %get-tuple-element.42.panel0, f32[5,128,128]{2,1,0:T(8,128)S(1)} %get-tuple-element.38.inv_in.inv0, f32[4,128,128]{2,1,0:T(8,128)S(1)} %get-tuple-element.43.link0, f32[128,128]{1,0:T(8,128)S(1)} %get-tuple-element.44.panel1, f32[2,128,128]{2,1,0:T(8,128)S(1)} %get-tuple-element.47.inv1, ...), custom_call_target="tpu_custom_call" | custom-call | flops 400000000 | bytes 4000000 | tf_op jit(solution)/shard_map/means/pallas_call | solution.py:174
  (35 shorter events, 6.2 us)
Async XLA Ops:
  0.6 1.0 copy-start
  1.6 10.7 %copy-start.1 = (f32[128,768]{1,0:T(8,128)S(1)}, f32[128,768]{1,0:T(8,128)}, u32[]{:S(2)}) copy-start(f32[128,768]{1,0:T(8,128)} %x_ref.3) | copy-start | bytes 1179652
  3.0 8.8 %copy-start.3 = (s32[128]{0:T(128)S(1)}, s32[128]{0:T(128)}, u32[]{:S(2)}) copy-start(s32[128]{0:T(128)} %param.3) | copy-start | bytes 1540
  3.0 10.9 %collective-permute-start = (f32[1344,128]{1,0:T(8,128)S(1)}, f32[1344,128]{1,0:T(8,128)S(1)}, u32[]{:S(2)}, u32[]{:S(2)}) collective-permute-start(f32[1344,128]{1,0:T(8,128)S(1)} %get-tuple-element.29), channel_id=1, source_target_pairs={{0,4},{4,0},{1,5},{5,1},{2,6},{6,2},{3,7},{7,3},{8,12},{12,8},{9,1... | collective-permute-start | bytes 2064392 | tf_op jit(solution)/shard_map/ppermute | solution.py:306
  13.9 8.7 %copy-start.2 = (f32[128,1536]{1,0:T(8,128)S(1)}, f32[128,1536]{1,0:T(8,128)}, u32[]{:S(2)}) copy-start(f32[128,1536]{1,0:T(8,128)} %reshape.37) | copy-start | bytes 2359300
  14.1 12.9 %collective-permute-start.1 = (f32[336,128]{1,0:T(8,128)S(1)}, f32[336,128]{1,0:T(8,128)S(1)}, u32[]{:S(2)}, u32[]{:S(2)}) collective-permute-start(f32[336,128]{1,0:T(8,128)S(1)} %get-tuple-element.31), channel_id=1, source_target_pairs={{0,1},{1,2},{2,3},{3,0},{4,5},{5,6},{6,7},{7,4},{8,9},{9,10},{10,1... | collective-permute-start | bytes 516104 | tf_op jit(solution)/shard_map/ppermute | solution.py:302
  16.1 10.9 %collective-permute-start.2 = (f32[336,128]{1,0:T(8,128)S(1)}, f32[336,128]{1,0:T(8,128)S(1)}, u32[]{:S(2)}, u32[]{:S(2)}) collective-permute-start(f32[336,128]{1,0:T(8,128)S(1)} %get-tuple-element.32), channel_id=1, source_target_pairs={{0,2},{1,3},{2,0},{3,1},{4,6},{5,7},{6,4},{7,5},{8,10},{9,11},{10,... | collective-permute-start | bytes 516104 | tf_op jit(solution)/shard_map/ppermute | solution.py:302
  18.1 11.1 %collective-permute-start.3 = (f32[336,128]{1,0:T(8,128)S(1)}, f32[336,128]{1,0:T(8,128)S(1)}, u32[]{:S(2)}, u32[]{:S(2)}) collective-permute-start(f32[336,128]{1,0:T(8,128)S(1)} %get-tuple-element.33), channel_id=1, source_target_pairs={{0,3},{1,0},{2,1},{3,2},{4,7},{5,4},{6,5},{7,6},{8,11},{9,8},{10,9... | collective-permute-start | bytes 516104 | tf_op jit(solution)/shard_map/ppermute | solution.py:302
  68.6 11.2 %collective-permute-start.4 = (f32[336,128]{1,0:T(8,128)S(1)}, f32[336,128]{1,0:T(8,128)S(1)}, u32[]{:S(2)}, u32[]{:S(2)}) collective-permute-start(f32[336,128]{1,0:T(8,128)S(1)} %reshape.40.refs_0_), channel_id=1, source_target_pairs={{0,1},{1,2},{2,3},{3,0},{4,5},{5,6},{6,7},{7,4},{8,9},{9,10},{10,1... | collective-permute-start | bytes 516104 | tf_op jit(solution)/shard_map/ppermute | solution.py:302
  74.1 16.1 %collective-permute-start.6 = (f32[336,128]{1,0:T(8,128)S(1)}, f32[336,128]{1,0:T(8,128)S(1)}, u32[]{:S(2)}, u32[]{:S(2)}) collective-permute-start(f32[336,128]{1,0:T(8,128)S(1)} %reshape.40.refs_0_), channel_id=1, source_target_pairs={{0,3},{1,0},{2,1},{3,2},{4,7},{5,4},{6,5},{7,6},{8,11},{9,8},{10,9... | collective-permute-start | bytes 516104 | tf_op jit(solution)/shard_map/ppermute | solution.py:302
  76.0 14.1 %collective-permute-start.5 = (f32[336,128]{1,0:T(8,128)S(1)}, f32[336,128]{1,0:T(8,128)S(1)}, u32[]{:S(2)}, u32[]{:S(2)}) collective-permute-start(f32[336,128]{1,0:T(8,128)S(1)} %reshape.40.refs_0_), channel_id=1, source_target_pairs={{0,2},{1,3},{2,0},{3,1},{4,6},{5,7},{6,4},{7,5},{8,10},{9,11},{10,... | collective-permute-start | bytes 516104 | tf_op jit(solution)/shard_map/ppermute | solution.py:302
  79.7 39.2 %all-to-all-start.3 = ((f32[128,1,1664]{2,1,0:T(1,128)}), f32[128,1,1664]{2,1,0:T(1,128)S(1)}, u32[]{:S(2)}, u32[]{:S(2)}) async-start(f32[128,1,1664]{2,1,0:T(1,128)} %reshape.38), calls=%async_computation.3 | async-start | bytes 1703936 | tf_op jit(solution)/shard_map/all_to_all | solution.py:337
  90.2 4.7 %collective-permute-start.7 = (f32[1344,128]{1,0:T(8,128)S(1)}, f32[1344,128]{1,0:T(8,128)S(1)}, u32[]{:S(2)}, u32[]{:S(2)}) collective-permute-start(f32[1344,128]{1,0:T(8,128)S(1)} %place_x.1.mine_ref), channel_id=1, source_target_pairs={{0,4},{4,0},{1,5},{5,1},{2,6},{6,2},{3,7},{7,3},{8,12},{12,8},{9,1... | collective-permute-start | bytes 2064392 | tf_op jit(solution)/shard_map/ppermute | solution.py:306
  120.3 9.3 %collective-permute-start.8 = (f32[224,128]{1,0:T(8,128)S(1)}, f32[224,128]{1,0:T(8,128)S(1)}, u32[]{:S(2)}, u32[]{:S(2)}) collective-permute-start(f32[224,128]{1,0:T(8,128)S(1)} %get-tuple-element.51), channel_id=1, source_target_pairs={{0,1},{1,2},{2,3},{3,0},{4,5},{5,6},{6,7},{7,4},{8,9},{9,10},{10,1... | collective-permute-start | bytes 344072 | tf_op jit(solution)/shard_map/ppermute | solution.py:302
  122.8 8.5 %collective-permute-start.9 = (f32[224,128]{1,0:T(8,128)S(1)}, f32[224,128]{1,0:T(8,128)S(1)}, u32[]{:S(2)}, u32[]{:S(2)}) collective-permute-start(f32[224,128]{1,0:T(8,128)S(1)} %get-tuple-element.52), channel_id=1, source_target_pairs={{0,2},{1,3},{2,0},{3,1},{4,6},{5,7},{6,4},{7,5},{8,10},{9,11},{10,... | collective-permute-start | bytes 344072 | tf_op jit(solution)/shard_map/ppermute | solution.py:302
  127.6 5.5 %collective-permute-start.10 = (f32[224,128]{1,0:T(8,128)S(1)}, f32[224,128]{1,0:T(8,128)S(1)}, u32[]{:S(2)}, u32[]{:S(2)}) collective-permute-start(f32[224,128]{1,0:T(8,128)S(1)} %get-tuple-element.53), channel_id=1, source_target_pairs={{0,3},{1,0},{2,1},{3,2},{4,7},{5,4},{6,5},{7,6},{8,11},{9,8},{10,9... | collective-permute-start | bytes 344072 | tf_op jit(solution)/shard_map/ppermute | solution.py:302
